TPU v7x, 128 devices: a whole 4x4x4 slice. The times are simulated.
128 devices in a mesh: dp: 32 (over y, z, core), mp: 4 (over x).
Axes of the slice: x: 4, y: 4, z: 4, core: 2. Of those that a mesh axis runs over, the one named last changes fastest.
Arguments:
- queries: bfloat16 [7168, 2560], P('dp', 'mp'), may hold values from -7 to 7
- keys: bfloat16 [7168, 512], P('dp', 'mp'), may hold values from -7 to 7
- values: bfloat16 [7168, 512], P('dp', 'mp'), may hold values from -6 to 6
- seg_ids: int32 [7168], P('dp'), may hold values from 0 to 7, never falling along the last dimension, each value on 1 to 3584 neighbouring positions
- out_weight: bfloat16 [2560, 5120], P('mp'), may hold values from -0.125 to 0.125
- grad_out: bfloat16 [7168, 5120], P('dp', 'mp'), may hold values from -6 to 6
Outputs:
- projected: bfloat16 [7168, 5120], P('dp', 'mp')
- grad_query: bfloat16 [7168, 2560], P('dp', 'mp')
- grad_key: bfloat16 [7168, 512], P('dp', 'mp')
- grad_value: bfloat16 [7168, 512], P('dp', 'mp')
Inputs may be any that keep to these rules, and one draw needn't show every extreme that they name: `seg_ids`: never falling along the tokens; 8 sequences of 1 to 3584 tokens, the longest exactly 3584.
All inputs are finite; a program needn't handle non-finite values.
Results may differ from a plain program's by a relative error of at most 0.011.
Values may be sent and summed in bfloat16 or wider, within the bound.
No kernel may reach another device: no remote copies, remote signals or barrier semaphores. Data moves between devices by JAX's collectives and lax.ppermute only.
A program may use at most 128 MiB of HBM per device.

v0:
```python
import math

import jax
import jax.numpy as jnp
from jax import lax
from jax.sharding import PartitionSpec as P

HD = 128


NEGATIVE = -1e30


def from_behind(value, axis, steps):
    count = lax.axis_size(axis)
    leading, last = (max(0, -steps), min(count, count - steps))
    return lax.ppermute(value, axis, [(source, source + steps) for source in range(leading, last)])


def attend_scores(query_part, key_part, scale):
    return (
        jnp.einsum("rkgh,skh->kgrs", query_part, key_part, preferred_element_type=jnp.float32)
        * scale
    )


def visible_pairs(query_rows, query_segs, key_rows, key_segs):
    return (query_segs[:, None] == key_segs[None, :]) & (key_rows[None, :] <= query_rows[:, None])


def may_touch(query_rows, query_segs, key_rows, key_segs):
    return (
        (key_rows[0] <= query_rows[-1])
        & (key_segs[0] <= query_segs[-1])
        & (key_segs[-1] >= query_segs[0])
    )


def grad_block(query_part, grad_part, lse, delta, key_part, value_part, visible, scale):
    scores = jnp.where(visible, attend_scores(query_part, key_part, scale), NEGATIVE)
    weights = jnp.where(visible, jnp.exp(scores - lse[..., None]), 0.0)
    dprob = jnp.einsum("rkgh,skh->kgrs", grad_part, value_part, preferred_element_type=jnp.float32)
    score_grad = (weights * (dprob - delta[..., None])).astype(jnp.bfloat16)
    return (weights, score_grad)


def key_terms(query_part, grad_part, weights, score_grad, scale):
    rows = score_grad.shape[3]
    key_grad = (
        jnp.einsum("kgrs,rkgh->skh", score_grad, query_part, preferred_element_type=jnp.float32)
        * scale
    )
    value_grad = jnp.einsum(
        "kgrs,rkgh->skh",
        weights.astype(jnp.bfloat16),
        grad_part,
        preferred_element_type=jnp.float32,
    )
    return jnp.concatenate([key_grad.reshape(rows, -1), value_grad.reshape(rows, -1)], axis=1)


def keep_carry(carry):
    return carry


def per_device(queries, keys, values, seg_ids, out_weight, grad_out):
    tok_rows = queries.shape[0]
    kv_local = keys.shape[1] // HD
    group = queries.shape[1] // (kv_local * HD)
    scale = 1.0 / math.sqrt(HD)
    my_index = lax.axis_index("dp")
    query_rows = my_index * tok_rows + jnp.arange(tok_rows, dtype=jnp.int32)
    query_mat = queries.reshape(tok_rows, kv_local, group, HD)
    all_keys, all_values, all_segs = (
        lax.all_gather(keys, "dp", axis=0, tiled=True),
        lax.all_gather(values, "dp", axis=0, tiled=True),
        lax.all_gather(seg_ids, "dp", axis=0, tiled=True),
    )
    total_rows = all_keys.shape[0]
    shards = total_rows // tok_rows
    repeats = 1
    while repeats * 2 * tok_rows <= 1024 and shards % (repeats * 2) == 0:
        repeats = repeats * 2
    key_block = repeats * tok_rows
    key_blocks = total_rows // key_block
    key_mat = all_keys.reshape(total_rows, kv_local, HD)
    value_mat = all_values.reshape(total_rows, kv_local, HD)

    def block_at(index):
        start = index * key_block
        return (
            lax.dynamic_slice_in_dim(key_mat, start, key_block, 0),
            lax.dynamic_slice_in_dim(value_mat, start, key_block, 0),
            start + jnp.arange(key_block, dtype=jnp.int32),
            lax.dynamic_slice_in_dim(all_segs, start, key_block, 0),
        )

    def lse_step(index, carry):
        key_part, value_part, key_rows, key_segs = block_at(index)

        def lse_accumulate(state):
            peak, total = state
            visible = visible_pairs(query_rows, seg_ids, key_rows, key_segs)
            scores = jnp.where(visible, attend_scores(query_mat, key_part, scale), NEGATIVE)
            new_peak = jnp.maximum(peak, jnp.max(scores, axis=3))
            added = jnp.sum(jnp.where(visible, jnp.exp(scores - new_peak[..., None]), 0.0), axis=3)
            return (new_peak, total * jnp.exp(peak - new_peak) + added)

        return lax.cond(
            may_touch(query_rows, seg_ids, key_rows, key_segs), lse_accumulate, keep_carry, carry
        )

    stat_shape = (kv_local, group, tok_rows)
    peak, total = lax.fori_loop(
        0,
        key_blocks,
        lse_step,
        (jnp.full(stat_shape, NEGATIVE, jnp.float32), jnp.zeros(stat_shape, jnp.float32)),
    )
    lse = peak + jnp.log(total)

    def out_step(index, carry):
        key_part, value_part, key_rows, key_segs = block_at(index)

        def out_accumulate(state):
            visible = visible_pairs(query_rows, seg_ids, key_rows, key_segs)
            scores = jnp.where(visible, attend_scores(query_mat, key_part, scale), NEGATIVE)
            weights = jnp.where(visible, jnp.exp(scores - lse[..., None]), 0.0).astype(jnp.bfloat16)
            return state + jnp.einsum(
                "kgrs,skh->rkgh", weights, value_part, preferred_element_type=jnp.float32
            )

        return lax.cond(
            may_touch(query_rows, seg_ids, key_rows, key_segs), out_accumulate, keep_carry, carry
        )

    attn_mat = lax.fori_loop(
        0, key_blocks, out_step, jnp.zeros((tok_rows, kv_local, group, HD), jnp.float32)
    ).astype(jnp.bfloat16)
    attn = attn_mat.reshape(tok_rows, kv_local * group * HD)
    term = jnp.dot(attn, out_weight, preferred_element_type=jnp.float32)
    projected = lax.psum_scatter(term, "mp", scatter_dimension=1, tiled=True).astype(jnp.bfloat16)
    d_attn = lax.dot_general(
        lax.all_gather(grad_out, "mp", axis=1, tiled=True),
        out_weight,
        (((1,), (1,)), ((), ())),
        preferred_element_type=jnp.float32,
    ).astype(jnp.bfloat16)
    grad_mat = d_attn.reshape(tok_rows, kv_local, group, HD)
    delta = jnp.transpose(
        jnp.sum(grad_mat.astype(jnp.float32) * attn_mat.astype(jnp.float32), axis=3), (1, 2, 0)
    )

    def query_step(index, carry):
        key_part, value_part, key_rows, key_segs = block_at(index)

        def query_accumulate(state):
            visible = visible_pairs(query_rows, seg_ids, key_rows, key_segs)
            weights, score_grad = grad_block(
                query_mat, grad_mat, lse, delta, key_part, value_part, visible, scale
            )
            return state + jnp.einsum(
                "kgrs,skh->rkgh", score_grad, key_part, preferred_element_type=jnp.float32
            )

        return lax.cond(
            may_touch(query_rows, seg_ids, key_rows, key_segs), query_accumulate, keep_carry, carry
        )

    query_acc = lax.fori_loop(
        0, key_blocks, query_step, jnp.zeros((tok_rows, kv_local, group, HD), jnp.float32)
    )
    grad_query = (query_acc * scale).astype(jnp.bfloat16).reshape(tok_rows, attn.shape[1])
    width = 2 * kv_local * HD
    lse_rows = jnp.transpose(lse, (2, 0, 1))
    delta_rows = jnp.transpose(delta, (2, 0, 1))
    own_keys = keys.reshape(tok_rows, kv_local, HD)
    own_values = values.reshape(tok_rows, kv_local, HD)
    n_dev = lax.axis_size("dp")

    def add_queries(carry, pieces, start, usable):
        query_piece, grad_piece, lse_piece, delta_piece, seg_piece = pieces
        query_part = query_piece.reshape(tok_rows, kv_local, group, HD)
        grad_part = grad_piece.reshape(tok_rows, kv_local, group, HD)
        lse_part = jnp.transpose(lse_piece, (1, 2, 0))
        delta_part = jnp.transpose(delta_piece, (1, 2, 0))
        rows_part = start + jnp.arange(tok_rows, dtype=jnp.int32)

        def add_accumulate(inner):
            visible = visible_pairs(rows_part, seg_piece, query_rows, seg_ids)
            weights, score_grad = grad_block(
                query_part, grad_part, lse_part, delta_part, own_keys, own_values, visible, scale
            )
            return inner + key_terms(query_part, grad_part, weights, score_grad, scale)

        touch = usable & may_touch(rows_part, seg_piece, query_rows, seg_ids)
        return lax.cond(touch, add_accumulate, keep_carry, carry)

    own_side = (queries, d_attn, lse_rows, delta_rows, seg_ids)
    combined = add_queries(
        jnp.zeros((tok_rows, width), jnp.float32), own_side, my_index * tok_rows, my_index >= 0
    )

    def one_turn(turn, state):
        acc, pieces = state
        pieces = from_behind(pieces, "dp", -1)
        source = my_index + turn + 1
        acc = add_queries(acc, pieces, source * tok_rows, source < n_dev)
        return (acc, pieces)

    combined, unused_side = lax.fori_loop(0, n_dev - 1, one_turn, (combined, own_side))
    grad_key = combined[:, : kv_local * HD].astype(jnp.bfloat16)
    grad_value = combined[:, kv_local * HD :].astype(jnp.bfloat16)
    return (projected, grad_query, grad_key, grad_value)


def solution(mesh):
    return jax.shard_map(
        per_device,
        mesh=mesh,
        in_specs=(
            P("dp", "mp"),
            P("dp", "mp"),
            P("dp", "mp"),
            P("dp"),
            P("mp", None),
            P("dp", "mp"),
        ),
        out_specs=(P("dp", "mp"), P("dp", "mp"), P("dp", "mp"), P("dp", "mp")),
        check_vma=False,
    )
```

profile of v0, /device:TPU:92, one launch (start us, length us, event | category | flops | bytes accessed | tf_op | source)
XLA Modules:
  0.0 981.1 jit_solution(9471297449096288724)
XLA Ops:
  19.4 116.4 %all-reduce = s32[7168]{0:T(1024)S(1)} all-reduce(s32[7168]{0:T(1024)S(1)} %dynamic-update-slice), channel_id=1, replica_groups=mesh['dp'=32,'mp'=4] {'dp'}, use_global_device_ids=true, to_apply=%add | all-reduce | flops 7168 | bytes 57344
  135.8 5.8 convolution_convert_fusion
  142.1 59.5 %while.73 = (s32[]{:T(128)}, f32[1,5,224]{2,1,0:T(8,128)S(1)}, f32[1,5,224]{2,1,0:T(8,128)S(1)}, s32[224]{0:T(256)S(1)}, s32[7168]{0:T(1024)S(1)}, /*index=5*/s3...) while((s32[]{:T(128)}, f32[1,5,224]{2,1,0:T(8,128)S(1)}, ...), condition=%wide.region_5.6_spmd, body=%wide.region_0.5_spmd.sunk | while | flops 265534544 | bytes 9225201 | solution.py:114
  201.7 57.1 %while.74 = (s32[]{:T(128)}, f32[224,1,5,128]{3,0,2,1:T(8,128)S(1)}, s32[224]{0:T(256)S(1)}, s32[7168]{0:T(1024)S(1)}, s32[224]{0:T(256)S(1)}, /*index=5*/bf16[7...) while((s32[]{:T(128)}, ...), condition=%wide.region_9.10_spmd, body=%wide.region_6.9_spmd.sunk | while | flops 519566208 | bytes 2319329 | solution.py:137
  259.1 6.9 fusion.110
  268.6 624.1 %while.76 = (s32[]{:T(128)}, f32[224,256]{1,0:T(8,128)S(1)}, bf16[224,640]{0,1:T(8,128)(2,1)S(1)}, bf16[224,640]{0,1:T(8,128)(2,1)S(1)}, f32[224,1,5]{0,2,1:T(8,...) while((s32[]{:T(128)}, f32[224,256]{1,0:T(8,128)S(1)}, ...), condition=%wide.region_21.22_spmd, body=%wide.region_18.21_spmd.sunk | while | flops 259202288 | bytes 8803775 | solution.py:211
  305.9 4.1 collective-permute-start
  343.4 5.2 collective-permute-start
  375.0 5.6 collective-permute-start.1
  391.1 5.1 collective-permute-start.2
  398.1 5.1 collective-permute-start.1
  419.0 5.6 collective-permute-start.1
  440.5 5.6 collective-permute-start.1
  501.6 5.6 collective-permute-start.1
  523.1 5.6 collective-permute-start.1
  892.8 77.9 %while.75 = (s32[]{:T(128)}, f32[224,1,5,128]{3,0,2,1:T(8,128)S(1)}, s32[224]{0:T(256)S(1)}, s32[7168]{0:T(1024)S(1)}, s32[224]{0:T(256)S(1)}, /*index=5*/bf16[7...) while((s32[]{:T(128)}, ...), condition=%wide.region_15.16_spmd, body=%wide.region_12.15_spmd.sunk | while | flops 778474368 | bytes 10868609 | solution.py:170
  921.2 8.1 conditional.12
  925.1 4.2 fusion.41
  935.0 8.1 conditional.12
  938.9 4.2 fusion.41
  948.8 8.1 conditional.12
  952.7 4.2 fusion.41
  962.6 8.1 conditional.12
  966.5 4.2 fusion.41
  (887 shorter events, 582.6 us)
Async XLA Ops:
  7.2 128.6 %all-gather.8.cloned.1.call-start = ((), (), s32[]{:S(2)}) async-start(), calls=%async_computation.4 | async-start | bytes 2867200 | tf_op jit(solution)/shard_map/all_gather | solution.py:144
  7.9 134.1 %all-gather.6.cloned.1.call-start = ((), (), s32[]{:S(2)}) async-start(), calls=%async_computation.2 | async-start | bytes 1892352 | tf_op jit(solution)/shard_map/all_gather | solution.py:75
  8.7 193.0 %all-gather.4.cloned.1.call-start = ((), (), s32[]{:S(2)}) async-start(), calls=%async_computation.1 | async-start | bytes 1892352 | tf_op jit(solution)/shard_map/all_gather | solution.py:76
  9.4 963.1 %reduce-scatter.2.cloned.1.call-start = ((), (), s32[]{:S(2)}) async-start(), calls=%async_computation.3 | async-start | bytes 5734400 | tf_op jit(solution)/shard_map/reduce_scatter | solution.py:142
  362.7 21.0 %collective-permute-start = (s32[224]{0:T(256)S(1)}, s32[224]{0:T(256)S(1)}, u32[]{:S(2)}, u32[]{:S(2)}) collective-permute-start(s32[224]{0:T(256)S(1)} %get-tuple-element.1608), channel_id=1, source_target_pairs={{4,0},{8,4},{12,8},{16,12},{20,16},{24,20},{28,24},{32,28},{36,32}... | collective-permute-start | bytes 2696 | tf_op jit(solution)/shard_map/while/body/eval_jaxpr/ppermute | solution.py:17
  366.4 20.5 %collective-permute-start.4 = (f32[224,1,5]{0,2,1:T(8,128)S(1)}, f32[224,1,5]{0,2,1:T(8,128)S(1)}, u32[]{:S(2)}, u32[]{:S(2)}) collective-permute-start(f32[224,1,5]{0,2,1:T(8,128)S(1)} %get-tuple-element.1607), channel_id=1, source_target_pairs={{4,0},{8,4},{12,8},{16,12},{20,16},{24,20},{28,24},{32,28},{36,32}... | collective-permute-start | bytes 13448 | tf_op jit(solution)/shard_map/while/body/eval_jaxpr/ppermute | solution.py:17
  369.2 17.6 %collective-permute-start.2 = (f32[224,1,5]{0,2,1:T(8,128)S(1)}, f32[224,1,5]{0,2,1:T(8,128)S(1)}, u32[]{:S(2)}, u32[]{:S(2)}) collective-permute-start(f32[224,1,5]{0,2,1:T(8,128)S(1)} %get-tuple-element.1606), channel_id=1, source_target_pairs={{4,0},{8,4},{12,8},{16,12},{20,16},{24,20},{28,24},{32,28},{36,32}... | collective-permute-start | bytes 13448 | tf_op jit(solution)/shard_map/while/body/eval_jaxpr/ppermute | solution.py:17
  387.0 19.2 %collective-permute-start = (s32[224]{0:T(256)S(1)}, s32[224]{0:T(256)S(1)}, u32[]{:S(2)}, u32[]{:S(2)}) collective-permute-start(s32[224]{0:T(256)S(1)} %get-tuple-element.1608), channel_id=1, source_target_pairs={{4,0},{8,4},{12,8},{16,12},{20,16},{24,20},{28,24},{32,28},{36,32}... | collective-permute-start | bytes 2696 | tf_op jit(solution)/shard_map/while/body/eval_jaxpr/ppermute | solution.py:17
  389.1 20.3 %collective-permute-start.4 = (f32[224,1,5]{0,2,1:T(8,128)S(1)}, f32[224,1,5]{0,2,1:T(8,128)S(1)}, u32[]{:S(2)}, u32[]{:S(2)}) collective-permute-start(f32[224,1,5]{0,2,1:T(8,128)S(1)} %get-tuple-element.1607), channel_id=1, source_target_pairs={{4,0},{8,4},{12,8},{16,12},{20,16},{24,20},{28,24},{32,28},{36,32}... | collective-permute-start | bytes 13448 | tf_op jit(solution)/shard_map/while/body/eval_jaxpr/ppermute | solution.py:17
  391.1 18.3 %collective-permute-start.2 = (f32[224,1,5]{0,2,1:T(8,128)S(1)}, f32[224,1,5]{0,2,1:T(8,128)S(1)}, u32[]{:S(2)}, u32[]{:S(2)}) collective-permute-start(f32[224,1,5]{0,2,1:T(8,128)S(1)} %get-tuple-element.1606), channel_id=1, source_target_pairs={{4,0},{8,4},{12,8},{16,12},{20,16},{24,20},{28,24},{32,28},{36,32}... | collective-permute-start | bytes 13448 | tf_op jit(solution)/shard_map/while/body/eval_jaxpr/ppermute | solution.py:17
  409.5 18.1 %collective-permute-start = (s32[224]{0:T(256)S(1)}, s32[224]{0:T(256)S(1)}, u32[]{:S(2)}, u32[]{:S(2)}) collective-permute-start(s32[224]{0:T(256)S(1)} %get-tuple-element.1608), channel_id=1, source_target_pairs={{4,0},{8,4},{12,8},{16,12},{20,16},{24,20},{28,24},{32,28},{36,32}... | collective-permute-start | bytes 2696 | tf_op jit(solution)/shard_map/while/body/eval_jaxpr/ppermute | solution.py:17
  411.7 19.1 %collective-permute-start.4 = (f32[224,1,5]{0,2,1:T(8,128)S(1)}, f32[224,1,5]{0,2,1:T(8,128)S(1)}, u32[]{:S(2)}, u32[]{:S(2)}) collective-permute-start(f32[224,1,5]{0,2,1:T(8,128)S(1)} %get-tuple-element.1607), channel_id=1, source_target_pairs={{4,0},{8,4},{12,8},{16,12},{20,16},{24,20},{28,24},{32,28},{36,32}... | collective-permute-start | bytes 13448 | tf_op jit(solution)/shard_map/while/body/eval_jaxpr/ppermute | solution.py:17
  431.0 18.1 %collective-permute-start = (s32[224]{0:T(256)S(1)}, s32[224]{0:T(256)S(1)}, u32[]{:S(2)}, u32[]{:S(2)}) collective-permute-start(s32[224]{0:T(256)S(1)} %get-tuple-element.1608), channel_id=1, source_target_pairs={{4,0},{8,4},{12,8},{16,12},{20,16},{24,20},{28,24},{32,28},{36,32}... | collective-permute-start | bytes 2696 | tf_op jit(solution)/shard_map/while/body/eval_jaxpr/ppermute | solution.py:17
  433.1 19.1 %collective-permute-start.4 = (f32[224,1,5]{0,2,1:T(8,128)S(1)}, f32[224,1,5]{0,2,1:T(8,128)S(1)}, u32[]{:S(2)}, u32[]{:S(2)}) collective-permute-start(f32[224,1,5]{0,2,1:T(8,128)S(1)} %get-tuple-element.1607), channel_id=1, source_target_pairs={{4,0},{8,4},{12,8},{16,12},{20,16},{24,20},{28,24},{32,28},{36,32}... | collective-permute-start | bytes 13448 | tf_op jit(solution)/shard_map/while/body/eval_jaxpr/ppermute | solution.py:17
  474.4 17.6 %collective-permute-start.4 = (f32[224,1,5]{0,2,1:T(8,128)S(1)}, f32[224,1,5]{0,2,1:T(8,128)S(1)}, u32[]{:S(2)}, u32[]{:S(2)}) collective-permute-start(f32[224,1,5]{0,2,1:T(8,128)S(1)} %get-tuple-element.1607), channel_id=1, source_target_pairs={{4,0},{8,4},{12,8},{16,12},{20,16},{24,20},{28,24},{32,28},{36,32}... | collective-permute-start | bytes 13448 | tf_op jit(solution)/shard_map/while/body/eval_jaxpr/ppermute | solution.py:17
  492.1 18.1 %collective-permute-start = (s32[224]{0:T(256)S(1)}, s32[224]{0:T(256)S(1)}, u32[]{:S(2)}, u32[]{:S(2)}) collective-permute-start(s32[224]{0:T(256)S(1)} %get-tuple-element.1608), channel_id=1, source_target_pairs={{4,0},{8,4},{12,8},{16,12},{20,16},{24,20},{28,24},{32,28},{36,32}... | collective-permute-start | bytes 2696 | tf_op jit(solution)/shard_map/while/body/eval_jaxpr/ppermute | solution.py:17
  494.3 19.2 %collective-permute-start.4 = (f32[224,1,5]{0,2,1:T(8,128)S(1)}, f32[224,1,5]{0,2,1:T(8,128)S(1)}, u32[]{:S(2)}, u32[]{:S(2)}) collective-permute-start(f32[224,1,5]{0,2,1:T(8,128)S(1)} %get-tuple-element.1607), channel_id=1, source_target_pairs={{4,0},{8,4},{12,8},{16,12},{20,16},{24,20},{28,24},{32,28},{36,32}... | collective-permute-start | bytes 13448 | tf_op jit(solution)/shard_map/while/body/eval_jaxpr/ppermute | solution.py:17
  513.6 18.1 %collective-permute-start = (s32[224]{0:T(256)S(1)}, s32[224]{0:T(256)S(1)}, u32[]{:S(2)}, u32[]{:S(2)}) collective-permute-start(s32[224]{0:T(256)S(1)} %get-tuple-element.1608), channel_id=1, source_target_pairs={{4,0},{8,4},{12,8},{16,12},{20,16},{24,20},{28,24},{32,28},{36,32}... | collective-permute-start | bytes 2696 | tf_op jit(solution)/shard_map/while/body/eval_jaxpr/ppermute | solution.py:17
  515.7 19.1 %collective-permute-start.4 = (f32[224,1,5]{0,2,1:T(8,128)S(1)}, f32[224,1,5]{0,2,1:T(8,128)S(1)}, u32[]{:S(2)}, u32[]{:S(2)}) collective-permute-start(f32[224,1,5]{0,2,1:T(8,128)S(1)} %get-tuple-element.1607), channel_id=1, source_target_pairs={{4,0},{8,4},{12,8},{16,12},{20,16},{24,20},{28,24},{32,28},{36,32}... | collective-permute-start | bytes 13448 | tf_op jit(solution)/shard_map/while/body/eval_jaxpr/ppermute | solution.py:17
  537.1 17.6 %collective-permute-start.4 = (f32[224,1,5]{0,2,1:T(8,128)S(1)}, f32[224,1,5]{0,2,1:T(8,128)S(1)}, u32[]{:S(2)}, u32[]{:S(2)}) collective-permute-start(f32[224,1,5]{0,2,1:T(8,128)S(1)} %get-tuple-element.1607), channel_id=1, source_target_pairs={{4,0},{8,4},{12,8},{16,12},{20,16},{24,20},{28,24},{32,28},{36,32}... | collective-permute-start | bytes 13448 | tf_op jit(solution)/shard_map/while/body/eval_jaxpr/ppermute | solution.py:17
  557.0 17.6 %collective-permute-start.4 = (f32[224,1,5]{0,2,1:T(8,128)S(1)}, f32[224,1,5]{0,2,1:T(8,128)S(1)}, u32[]{:S(2)}, u32[]{:S(2)}) collective-permute-start(f32[224,1,5]{0,2,1:T(8,128)S(1)} %get-tuple-element.1607), channel_id=1, source_target_pairs={{4,0},{8,4},{12,8},{16,12},{20,16},{24,20},{28,24},{32,28},{36,32}... | collective-permute-start | bytes 13448 | tf_op jit(solution)/shard_map/while/body/eval_jaxpr/ppermute | solution.py:17
  576.9 17.6 %collective-permute-start.4 = (f32[224,1,5]{0,2,1:T(8,128)S(1)}, f32[224,1,5]{0,2,1:T(8,128)S(1)}, u32[]{:S(2)}, u32[]{:S(2)}) collective-permute-start(f32[224,1,5]{0,2,1:T(8,128)S(1)} %get-tuple-element.1607), channel_id=1, source_target_pairs={{4,0},{8,4},{12,8},{16,12},{20,16},{24,20},{28,24},{32,28},{36,32}... | collective-permute-start | bytes 13448 | tf_op jit(solution)/shard_map/while/body/eval_jaxpr/ppermute | solution.py:17
  596.7 17.6 %collective-permute-start.4 = (f32[224,1,5]{0,2,1:T(8,128)S(1)}, f32[224,1,5]{0,2,1:T(8,128)S(1)}, u32[]{:S(2)}, u32[]{:S(2)}) collective-permute-start(f32[224,1,5]{0,2,1:T(8,128)S(1)} %get-tuple-element.1607), channel_id=1, source_target_pairs={{4,0},{8,4},{12,8},{16,12},{20,16},{24,20},{28,24},{32,28},{36,32}... | collective-permute-start | bytes 13448 | tf_op jit(solution)/shard_map/while/body/eval_jaxpr/ppermute | solution.py:17
  696.1 17.6 %collective-permute-start.4 = (f32[224,1,5]{0,2,1:T(8,128)S(1)}, f32[224,1,5]{0,2,1:T(8,128)S(1)}, u32[]{:S(2)}, u32[]{:S(2)}) collective-permute-start(f32[224,1,5]{0,2,1:T(8,128)S(1)} %get-tuple-element.1607), channel_id=1, source_target_pairs={{4,0},{8,4},{12,8},{16,12},{20,16},{24,20},{28,24},{32,28},{36,32}... | collective-permute-start | bytes 13448 | tf_op jit(solution)/shard_map/while/body/eval_jaxpr/ppermute | solution.py:17
  (138 other events, 1868.8 us)
Sparse Core Ops, SparseCore 0:
  9.7 32.6 all-gather.7
  44.6 42.8 all-gather.5
  89.8 42.8 all-gather.3
  266.2 56.2 reduce-scatter.1
where the time goes:
time: 989 us; the launch traced here: 981 us
  starting transfers between devices  422 us (43%)
  loops' own time  220 us (22%)
  local copies, waits for them, and re-layouts  123 us (12%)
  blocking collectives  116 us (12%)
  matrix products  68.2 us (7%)
  between operations  18.4 us (2%)
  other arithmetic  11.3 us (1%)
    ppermute x155, starting transfers between devices, from_behind(): lax.ppermute(value, axis, [(source, source + steps) for source in range(l...  421 us
    another operation x1, loops' own time, per_device(): lax.fori_loop(0, n_dev - 1, one_turn, (combined, own_side))  125 us
    unnamed x1, blocking collectives  116 us
    slice x56, local copies, waits for them, and re-layouts, may_touch(): query_rows[-1]  32.6 us
    slice x55, local copies, waits for them, and re-layouts, may_touch(): key_segs[-1] >= query_segs[0]  32.6 us
    another operation x1, loops' own time, per_device(): lax.fori_loop(0, key_blocks, query_step, jnp.zeros((tok_rows, kv_local, g...  31.3 us
    another operation x1, loops' own time, per_device(): lax.fori_loop(0, key_blocks, out_step, jnp.zeros((tok_rows, kv_local, gro...  31.1 us
    another operation x1, loops' own time, per_device(): lax.fori_loop(0, key_blocks, lse_step, (jnp.full(stat_shape, NEGATIVE, jn...  30.6 us
  transfers between devices with their start and end apart: 159, of which 0 were waited for; matrix products, arithmetic and copies ran while one was open for 17% of the time, Pallas kernels for 0%

commit v1 on v0

v1 whole, which is shorter than its diff:
```python
import math

import jax
import jax.numpy as jnp
from jax import lax
from jax.experimental import pallas as pl
from jax.experimental.pallas import tpu as pltpu
from jax.sharding import PartitionSpec as P

HD = 128
GROUP = 5
NZ = 4
NY = 4
REACH = 2
TILE = 16
LOW = -1e30
HIGH = 1e30
F32 = jnp.float32
BF16 = jnp.bfloat16
NT = (((1,), (1,)), ((), ()))
TN = (((0,), (0,)), ((), ()))
NN = (((1,), (0,)), ((), ()))


def place(y, z, core):
    return ((y % NY) * NZ + (z % NZ)) * 2 + core


def shift(dy, dz, flip):
    pairs = []
    for y in range(NY):
        for z in range(NZ):
            for core in range(2):
                if 0 <= y + dy < NY:
                    pairs.append((place(y, z, core), place(y + dy, z + dz, core ^ flip)))
    return pairs


def move(value, dy=0, dz=0, flip=0):
    return lax.ppermute(value, "dp", shift(dy, dz, flip))


def dot(a, b, dims):
    return lax.dot_general(a, b, dims, preferred_element_type=F32)


def where_am_i():
    index = lax.axis_index("dp")
    return index // (2 * NZ), (index // 2) % NZ, index % 2


def copies(near, near_other, far, far_other, kv, sem):
    y, z, core = where_am_i()
    started = []
    for back in range(NZ):
        source_z = lax.rem(z + NZ - back, NZ)
        for flip, near_ref, far_ref in ((0, near, far), (1, near_other, far_other)):
            col = source_z * 2 + (core if flip == 0 else 1 - core)
            started.append((near_ref.at[back], kv.at[REACH * 2 * NZ + col]))
            for dy in range(1, REACH + 1):
                started.append((far_ref.at[back, dy - 1], kv.at[(REACH - dy) * 2 * NZ + col]))
    return [pltpu.make_async_copy(s, d, sem.at[i]) for i, (s, d) in enumerate(started)]


def stack_heads(source, target, rows):
    for head in range(GROUP):
        target[head * rows : (head + 1) * rows, :] = source[:, head * HD : (head + 1) * HD]
    target[GROUP * rows :, :] = jnp.zeros((target.shape[0] - GROUP * rows, HD), BF16)


def forward_kernel(rows, factor, seg0, info, q, near, near_o, far, far_o, attn, attn_t, lse, prior_out, kv, q5, top, total, acc, sem):
    started = copies(near, near_o, far, far_o, kv, sem)
    for copy in started:
        copy.start()
    stack_heads(q, q5, rows)
    y, z, core = where_am_i()
    mine = REACH * 2 * NZ + z * 2 + core
    first = (REACH - y) * 2 * NZ
    for copy in started:
        copy.wait()
    seg = seg0[0].astype(F32)

    def count(slot, so_far):
        tile = kv[slot, rows:, :].astype(F32)
        return so_far + jnp.where(tile == seg, 1.0, 0.0)

    counted = lax.fori_loop(jnp.maximum(first, 0), mine, count, jnp.zeros((TILE, 2 * HD), F32))
    prior = jnp.sum(counted).astype(jnp.int32)
    prior_out[0] = prior
    row_pos = info[0:1, :]
    row_start = info[1:2, :]
    row_near = info[2:3, :] > 0.5
    width = info.shape[1]
    key_pos = lax.broadcasted_iota(jnp.int32, (rows, width), 0)

    key = kv[mine, :rows, :HD]
    value = kv[mine, :rows, HD:]
    scores = dot(key, q5[...], NT) * factor
    key_f = key_pos.astype(F32)
    scores = jnp.where((key_f <= row_pos) & (key_f >= row_start), scores, LOW)
    peak = jnp.max(scores, axis=0, keepdims=True)
    p = jnp.exp2(scores - peak)
    top[...] = peak
    total[...] = jnp.sum(p, axis=0, keepdims=True)
    acc[...] = dot(value, p.astype(BF16), TN)

    def step(slot, _):
        key = kv[slot, :rows, :HD]
        value = kv[slot, :rows, HD:]
        begin = (mine - slot) * rows - prior
        scores = dot(key, q5[...], NT) * factor
        scores = jnp.where(key_pos >= begin, scores, LOW)
        peak = jnp.max(scores, axis=0, keepdims=True)
        old = top[...]
        new = jnp.maximum(old, jnp.where(row_near, peak, LOW))
        top[...] = new
        alpha = jnp.exp2(old - new)
        p = jnp.exp2(scores - jnp.where(row_near, new, HIGH))
        total[...] = total[...] * alpha + jnp.sum(p, axis=0, keepdims=True)
        acc[...] = acc[...] * alpha + dot(value, p.astype(BF16), TN)
        return 0

    low = jnp.maximum(mine - (prior + rows - 1) // rows, 0)
    lax.fori_loop(low, mine, step, 0)
    out_t = (acc[...] / total[...]).astype(BF16)
    attn_t[...] = out_t
    lse[...] = top[...] + jnp.log2(total[...])
    out = out_t.T
    for head in range(GROUP):
        attn[:, head * HD : (head + 1) * HD] = out[head * rows : (head + 1) * rows, :]


def backward_kernel(rows, factor, scale, prior_in, info, q, grad, attn_t, lse, near, near_o, far, far_o, dq, stay, leave, kv, q5, g5, acc, sem):
    started = copies(near, near_o, far, far_o, kv, sem)
    for copy in started:
        copy.start()
    stack_heads(q, q5, rows)
    stack_heads(grad, g5, rows)
    stay[...] = jnp.zeros(stay.shape, BF16)
    leave[...] = jnp.zeros(leave.shape, BF16)
    y, z, core = where_am_i()
    mine = REACH * 2 * NZ + z * 2 + core
    prior = prior_in[0]
    row_pos = info[0:1, :]
    row_start = info[1:2, :]
    row_near = info[2:3, :] > 0.5
    width = info.shape[1]
    key_pos = lax.broadcasted_iota(jnp.int32, (rows, width), 0)
    delta = jnp.sum(attn_t[...].astype(F32) * g5[...].T.astype(F32), axis=0, keepdims=True)
    for copy in started:
        copy.wait()

    def block(slot, visible, norm):
        key = kv[slot, :rows, :HD]
        value = kv[slot, :rows, HD:]
        scores = dot(key, q5[...], NT) * factor
        p = jnp.where(visible, jnp.exp2(scores - norm), 0.0)
        slope = (p * (dot(value, g5[...], NT) - delta)).astype(BF16)
        d_value = dot(p.astype(BF16), g5[...], NN).astype(BF16)
        d_key = (dot(slope, q5[...], NN) * scale).astype(BF16)
        depth = REACH - slot // (2 * NZ)
        slot_z = (slot // 2) % NZ
        away = lax.rem(slot_z + NZ - z, NZ)
        same = slot % 2 == core

        @pl.when(same)
        def _():
            stay[away, depth, :, :HD] = d_key
            stay[away, depth, :, HD:] = d_value

        @pl.when(jnp.logical_not(same))
        def _():
            leave[away, depth, :, :HD] = d_key
            leave[away, depth, :, HD:] = d_value

        return dot(key, slope, TN)

    key_f = key_pos.astype(F32)
    acc[...] = block(mine, (key_f <= row_pos) & (key_f >= row_start), lse[...])
    norm = jnp.where(row_near, lse[...], HIGH)

    def step(slot, _):
        begin = (mine - slot) * rows - prior
        acc[...] += block(slot, key_pos >= begin, norm)
        return 0

    low = jnp.maximum(mine - (prior + rows - 1) // rows, 0)
    lax.fori_loop(low, mine, step, 0)
    out = (acc[...] * scale).astype(BF16).T
    for head in range(GROUP):
        dq[:, head * HD : (head + 1) * HD] = out[head * rows : (head + 1) * rows, :]


def gather_keys(keys, values, seg_ids):
    rows = keys.shape[0]
    segs = jnp.pad(seg_ids.astype(BF16)[None, :], ((0, TILE - 1), (0, 2 * HD - rows)), constant_values=-1)
    own = jnp.concatenate([jnp.concatenate([keys, values], axis=1), segs], axis=0)
    behind = jnp.stack([move(own, dy=dy) for dy in range(1, REACH + 1)])
    near = jnp.stack([own] + [move(own, dz=dz) for dz in range(1, NZ)])
    near_other = move(near, flip=1)
    far = jnp.stack([behind] + [move(behind, dz=dz) for dz in range(1, NZ)])
    far_other = move(far, flip=1)
    return near, near_other, far, far_other


def add_up(*terms):
    return sum(t.astype(F32) for t in terms)


def return_grads(stay, leave):
    mixed = add_up(stay, move(leave, flip=1)).astype(BF16)
    column = add_up(mixed[0], *[move(mixed[dz], dz=dz) for dz in range(1, NZ)])
    rounded = column.astype(BF16)
    return add_up(column[0], *[move(rounded[dy], dy=-dy) for dy in range(1, REACH + 1)]).astype(BF16)


def row_info(seg_ids, width):
    rows = seg_ids.shape[0]
    position = jnp.arange(rows, dtype=F32)
    start = jnp.sum(seg_ids[None, :] < seg_ids[:, None], axis=1).astype(F32)
    near = (seg_ids == seg_ids[0]).astype(F32)
    info = jnp.stack([position, start, near] + [jnp.zeros(rows, F32)] * 5)
    info = jnp.tile(info, (1, GROUP))
    return jnp.concatenate([info, jnp.tile(info[:, -1:], (1, width - GROUP * rows))], axis=1)


def per_device(queries, keys, values, seg_ids, out_weight, grad_out):
    rows = queries.shape[0]
    scale = 1.0 / math.sqrt(HD)
    factor = scale * math.log2(math.e)
    width = -(-GROUP * rows // 128) * 128
    slots = (REACH + 1) * 2 * NZ
    pieces = gather_keys(keys, values, seg_ids)
    info = row_info(seg_ids, width)
    any_spec = pl.BlockSpec(memory_space=pl.ANY)
    vmem = pl.BlockSpec(memory_space=pltpu.VMEM)
    smem = pl.BlockSpec(memory_space=pltpu.SMEM)
    params = pltpu.CompilerParams(vmem_limit_bytes=56 * 1024 * 1024)
    kv_scratch = pltpu.VMEM((slots, rows + TILE, 2 * HD), BF16)
    stacked = pltpu.VMEM((width, HD), BF16)
    attn, attn_t, lse, prior = pl.pallas_call(
        lambda *refs: forward_kernel(rows, factor, *refs),
        out_shape=(
            jax.ShapeDtypeStruct((rows, GROUP * HD), BF16),
            jax.ShapeDtypeStruct((HD, width), BF16),
            jax.ShapeDtypeStruct((1, width), F32),
            jax.ShapeDtypeStruct((1,), jnp.int32),
        ),
        in_specs=[smem, vmem, vmem] + [any_spec] * 4,
        out_specs=(vmem, vmem, vmem, smem),
        scratch_shapes=[
            kv_scratch,
            stacked,
            pltpu.VMEM((1, width), F32),
            pltpu.VMEM((1, width), F32),
            pltpu.VMEM((HD, width), F32),
            pltpu.SemaphoreType.DMA((slots,)),
        ],
        compiler_params=params,
    )(seg_ids[:1], info, queries, *pieces)
    term = jnp.dot(attn, out_weight, preferred_element_type=F32).astype(BF16)
    projected = lax.psum_scatter(term, "mp", scatter_dimension=1, tiled=True)
    d_attn = lax.dot_general(
        lax.all_gather(grad_out, "mp", axis=1, tiled=True),
        out_weight,
        NT,
        preferred_element_type=F32,
    ).astype(BF16)
    grads = jax.ShapeDtypeStruct((NZ, REACH + 1, rows, 2 * HD), BF16)
    grad_query, stay, leave = pl.pallas_call(
        lambda *refs: backward_kernel(rows, factor, scale, *refs),
        out_shape=(jax.ShapeDtypeStruct((rows, GROUP * HD), BF16), grads, grads),
        in_specs=[smem] + [vmem] * 5 + [any_spec] * 4,
        out_specs=(vmem, vmem, vmem),
        scratch_shapes=[
            kv_scratch,
            stacked,
            stacked,
            pltpu.VMEM((HD, width), F32),
            pltpu.SemaphoreType.DMA((slots,)),
        ],
        compiler_params=params,
    )(prior, info, queries, d_attn, attn_t, lse, *pieces)
    own = return_grads(stay, leave)
    return (projected, grad_query, own[:, :HD], own[:, HD:])


def solution(mesh):
    return jax.shard_map(
        per_device,
        mesh=mesh,
        in_specs=(
            P("dp", "mp"),
            P("dp", "mp"),
            P("dp", "mp"),
            P("dp"),
            P("mp", None),
            P("dp", "mp"),
        ),
        out_specs=(P("dp", "mp"), P("dp", "mp"), P("dp", "mp"), P("dp", "mp")),
        check_vma=False,
    )
```

time: 989 us -> 144 us (0.15)
  the two profiles are of different devices: /device:TPU:92 before, /device:TPU:14 now
where the time goes in v1:
time: 144 us; the launch traced here: 142 us
  waiting for transfers between devices  44.3 us (31%)
  starting transfers between devices  35.4 us (25%)
  Pallas kernels  26.5 us (18%)
  between operations  14.2 us (10%)
  matrix products  12.9 us (9%)
  other arithmetic  5.3 us (4%)
  local copies, waits for them, and re-layouts  3.43 us (2%)
    ppermute x16, waiting for transfers between devices, move(): return lax.ppermute(value, 'dp', shift(dy, dz, flip))  43.6 us
    ppermute x16, starting transfers between devices, move(): return lax.ppermute(value, 'dp', shift(dy, dz, flip))  35.3 us
    pallas_call x1, Pallas kernels, per_device(): pl.pallas_call(lambda *refs: backward_kernel(rows, factor, scale, *refs),...  15.6 us
    pallas_call x1, Pallas kernels, per_device(): pl.pallas_call(lambda *refs: forward_kernel(rows, factor, *refs), out_sha...  10.9 us
    dot_general x1, matrix products, per_device(): lax.dot_general(lax.all_gather(grad_out, 'mp', axis=1, tiled=True), out_w...  6.54 us
    dot_general x1, matrix products, per_device(): term = jnp.dot(attn, out_weight, preferred_element_type=F32).astype(BF16)  6.35 us
  transfers between devices with their start and end apart: 18, of which 15 were waited for; matrix products, arithmetic and copies ran while one was open for 14% of the time, Pallas kernels for 19%

profile of v1, /device:TPU:14, one launch (start us, length us, event | category | flops | bytes accessed | tf_op | source)
XLA Modules:
  0.0 142.0 jit_solution(4191151495253294736)
XLA Ops:
  9.5 3.5 %collective-permute-start.4 = (bf16[240,256]{1,0:T(8,128)(2,1)S(1)}, bf16[240,256]{1,0:T(8,128)(2,1)S(1)}, u32[]{:S(2)}, u32[]{:S(2)}) collective-permute-start(bf16[240,256]{1,0:T(8,128)(2,1)S(1)} %get-tuple-element.28), channel_id=1, source_target_pairs={{0,32},{4,36},{8,40},{12,44},{16,48},{20,52},{24,56},{28,60},{32,6... | collective-permute-start | bytes 368648 | tf_op jit(solution)/shard_map/ppermute | solution.py:40
  13.0 2.0 %collective-permute-start.5 = (bf16[240,256]{1,0:T(8,128)(2,1)S(1)}, bf16[240,256]{1,0:T(8,128)(2,1)S(1)}, u32[]{:S(2)}, u32[]{:S(2)}) collective-permute-start(bf16[240,256]{1,0:T(8,128)(2,1)S(1)} %get-tuple-element.28), channel_id=1, source_target_pairs={{0,64},{4,68},{8,72},{12,76},{16,80},{20,84},{24,88},{28,92},{32,9... | collective-permute-start | bytes 368648 | tf_op jit(solution)/shard_map/ppermute | solution.py:40
  17.6 4.0 %collective-permute-start.7 = (bf16[2,240,256]{2,1,0:T(8,128)(2,1)S(1)}, bf16[2,240,256]{2,1,0:T(8,128)(2,1)S(1)}, u32[]{:S(2)}, u32[]{:S(2)}) collective-permute-start(bf16[2,240,256]{2,1,0:T(8,128)(2,1)S(1)} %get-tuple-element.26), channel_id=1, source_target_pairs={{0,16},{4,20},{8,24},{12,28},{16,0},{20,4},{24,8},{28,12},{32,48},... | collective-permute-start | bytes 737288 | tf_op jit(solution)/shard_map/ppermute | solution.py:40
  22.6 2.2 %collective-permute-start.8 = (bf16[2,240,256]{2,1,0:T(8,128)(2,1)S(1)}, bf16[2,240,256]{2,1,0:T(8,128)(2,1)S(1)}, u32[]{:S(2)}, u32[]{:S(2)}) collective-permute-start(bf16[2,240,256]{2,1,0:T(8,128)(2,1)S(1)} %get-tuple-element.26), channel_id=1, source_target_pairs={{0,24},{4,28},{8,0},{12,4},{16,8},{20,12},{24,16},{28,20},{32,56},... | collective-permute-start | bytes 737288 | tf_op jit(solution)/shard_map/ppermute | solution.py:40
  24.8 3.6 %collective-permute-done.7 = bf16[2,240,256]{2,1,0:T(8,128)(2,1)S(1)} collective-permute-done((bf16[2,240,256]{2,1,0:T(8,128)(2,1)S(1)}, bf16[2,240,256]{2,1,0:T(8,128)(2,1)S(1)}, u32[]{:S(2)}, u32[]{:S(2)}) %collective-permute-start.7) | collective-permute-done | bytes 245792 | tf_op jit(solution)/shard_map/ppermute | solution.py:40
  28.5 3.4 %collective-permute-done.6 = bf16[2,240,256]{2,1,0:T(8,128)(2,1)S(1)} collective-permute-done((bf16[2,240,256]{2,1,0:T(8,128)(2,1)S(1)}, bf16[2,240,256]{2,1,0:T(8,128)(2,1)S(1)}, u32[]{:S(2)}, u32[]{:S(2)}) %collective-permute-start.6) | collective-permute-done | bytes 245792 | tf_op jit(solution)/shard_map/ppermute | solution.py:40
  32.8 2.7 %collective-permute-start.2 = (bf16[240,256]{1,0:T(8,128)(2,1)S(1)}, bf16[240,256]{1,0:T(8,128)(2,1)S(1)}, u32[]{:S(2)}, u32[]{:S(2)}) collective-permute-start(bf16[240,256]{1,0:T(8,128)(2,1)S(1)} %get-tuple-element.28), channel_id=1, source_target_pairs={{0,24},{4,28},{8,0},{12,4},{16,8},{20,12},{24,16},{28,20},{32,56},... | collective-permute-start | bytes 368648 | tf_op jit(solution)/shard_map/ppermute | solution.py:40
  37.2 4.2 %collective-permute-done.2 = bf16[240,256]{1,0:T(8,128)(2,1)S(1)} collective-permute-done((bf16[240,256]{1,0:T(8,128)(2,1)S(1)}, bf16[240,256]{1,0:T(8,128)(2,1)S(1)}, u32[]{:S(2)}, u32[]{:S(2)}) %collective-permute-start.2) | collective-permute-done | bytes 122912 | tf_op jit(solution)/shard_map/ppermute | solution.py:40
  41.4 1.9 %collective-permute-done.1 = bf16[240,256]{1,0:T(8,128)(2,1)S(1)} collective-permute-done((bf16[240,256]{1,0:T(8,128)(2,1)S(1)}, bf16[240,256]{1,0:T(8,128)(2,1)S(1)}, u32[]{:S(2)}, u32[]{:S(2)}) %collective-permute-start.1) | collective-permute-done | bytes 122912 | tf_op jit(solution)/shard_map/ppermute | solution.py:40
  48.7 10.9 %shard_map.93 = (bf16[224,640]{1,0:T(8,128)(2,1)}, bf16[128,1152]{1,0:T(8,128)(2,1)}, f32[1,1152]{1,0:T(1,128)}, s32[1]{0:T(128)}) custom-call(s32[1]{0:T(128)} %slice.34.refs_0_, f32[8,1152]{1,0:T(8,128)} %pad_maximum_fusion.3.refs_1_, bf16[224,640]{1,0:T(8,128)(2,1)} %refs_2_.3, bf16[4,240,256]{2,1,0:T(8,128)(2,1)} %copy-done.1, ...), custom_call_target="tpu_custom_call" | custom-call | tf_op jit(solution)/shard_map/pallas_call | solution.py:241
  59.6 6.3 %convolution_convert_fusion = bf16[224,5120]{1,0:T(8,128)(2,1)} fusion(bf16[224,640]{1,0:T(8,128)(2,1)} %get-tuple-element.11, bf16[640,5120]{1,0:T(8,128)(2,1)} %param.10), kind=kOutput, calls=%fused_computation | convolution fusion | flops 1469153280 | bytes 9134080 | tf_op jit(solution)/shard_map/dot_general | solution.py:261
  66.0 6.5 %convolution_convert_fusion.1.refs_3_ = bf16[224,640]{1,0:T(8,128)(2,1)} fusion(bf16[224,5120]{1,0:T(8,128)(2,1)} %all-gather.2.cloned.1.call-done, bf16[640,5120]{1,0:T(8,128)(2,1)} %param.10), kind=kOutput, calls=%fused_computation.2 | convolution fusion | flops 1468149760 | bytes 9134080 | tf_op jit(solution)/shard_map/dot_general | solution.py:263
  72.6 15.6 %shard_map.94 = (bf16[224,640]{1,0:T(8,128)(2,1)}, bf16[4,3,224,256]{3,2,1,0:T(8,128)(2,1)}, bf16[4,3,224,256]{3,2,1,0:T(8,128)(2,1)}) custom-call(s32[1]{0:T(128)} %get-tuple-element.12.refs_0_, f32[8,1152]{1,0:T(8,128)} %pad_maximum_fusion.3.refs_1_, bf16[224,640]{1,0:T(8,128)(2,1)} %refs_2_.3, bf16[224,640]{1,0:T(8,128)(2,1)} %convolution_convert_fusion.1.refs_3_, ...), custom_call_target="tpu_custom_call" | custom-call | tf_op jit(solution)/shard_map/pallas_call | solution.py:270
  88.2 2.5 %collective-permute-start.10 = (bf16[4,3,224,256]{3,2,1,0:T(8,128)(2,1)}, bf16[4,3,224,256]{3,2,1,0:T(8,128)(2,1)S(1)}, u32[]{:S(2)}, u32[]{:S(2)}) collective-permute-start(bf16[4,3,224,256]{3,2,1,0:T(8,128)(2,1)} %get-tuple-element.17), channel_id=1, source_target_pairs={{0,4},{4,0},{8,12},{12,8},{16,20},{20,16},{24,28},{28,24},{32,36},... | collective-permute-start | bytes 4128776 | tf_op jit(solution)/shard_map/ppermute | solution.py:40
  90.6 3.0 %collective-permute-done.10 = bf16[4,3,224,256]{3,2,1,0:T(8,128)(2,1)S(1)} collective-permute-done((bf16[4,3,224,256]{3,2,1,0:T(8,128)(2,1)}, bf16[4,3,224,256]{3,2,1,0:T(8,128)(2,1)S(1)}, u32[]{:S(2)}, u32[]{:S(2)}) %collective-permute-start.10) | collective-permute-done | bytes 1376288 | tf_op jit(solution)/shard_map/ppermute | solution.py:40
  93.6 1.7 %add_convert_fusion = bf16[4,3,224,256]{3,2,1,0:T(8,128)(2,1)S(1)} fusion(bf16[4,3,224,256]{3,2,1,0:T(8,128)(2,1)S(1)} %collective-permute-done.10, bf16[4,3,224,256]{3,2,1,0:T(8,128)(2,1)} %get-tuple-element.16), kind=kLoop, calls=%fused_computation.1 | loop fusion | flops 2752512 | bytes 4128768 | tf_op jit(solution)/shard_map/convert_element_type | solution.py:211
  95.4 2.6 %collective-permute-start.11 = (bf16[3,224,256]{2,1,0:T(8,128)(2,1)S(1)}, bf16[3,224,256]{2,1,0:T(8,128)(2,1)S(1)}, u32[]{:S(2)}, u32[]{:S(2)}) collective-permute-start(bf16[3,224,256]{2,1,0:T(8,128)(2,1)S(1)} %get-tuple-element.20), channel_id=1, source_target_pairs={{0,8},{4,12},{8,16},{12,20},{16,24},{20,28},{24,0},{28,4},{32,40},... | collective-permute-start | bytes 1032200 | tf_op jit(solution)/shard_map/ppermute | solution.py:40
  98.1 9.0 %collective-permute-start.13 = (bf16[3,224,256]{2,1,0:T(8,128)(2,1)S(1)}, bf16[3,224,256]{2,1,0:T(8,128)(2,1)S(1)}, u32[]{:S(2)}, u32[]{:S(2)}) collective-permute-start(bf16[3,224,256]{2,1,0:T(8,128)(2,1)S(1)} %get-tuple-element.21), channel_id=1, source_target_pairs={{0,24},{4,28},{8,0},{12,4},{16,8},{20,12},{24,16},{28,20},{32,56},... | collective-permute-start | bytes 1032200 | tf_op jit(solution)/shard_map/ppermute | solution.py:40
  108.5 7.1 %collective-permute-done.11 = bf16[3,224,256]{2,1,0:T(8,128)(2,1)S(1)} collective-permute-done((bf16[3,224,256]{2,1,0:T(8,128)(2,1)S(1)}, bf16[3,224,256]{2,1,0:T(8,128)(2,1)S(1)}, u32[]{:S(2)}, u32[]{:S(2)}) %collective-permute-start.11) | collective-permute-done | bytes 344096 | tf_op jit(solution)/shard_map/ppermute | solution.py:40
  115.6 6.7 %collective-permute-done.13 = bf16[3,224,256]{2,1,0:T(8,128)(2,1)S(1)} collective-permute-done((bf16[3,224,256]{2,1,0:T(8,128)(2,1)S(1)}, bf16[3,224,256]{2,1,0:T(8,128)(2,1)S(1)}, u32[]{:S(2)}, u32[]{:S(2)}) %collective-permute-start.13) | collective-permute-done | bytes 344096 | tf_op jit(solution)/shard_map/ppermute | solution.py:40
  122.3 1.8 %collective-permute-done.12 = bf16[3,224,256]{2,1,0:T(8,128)(2,1)S(1)} collective-permute-done((bf16[3,224,256]{2,1,0:T(8,128)(2,1)S(1)}, bf16[3,224,256]{2,1,0:T(8,128)(2,1)S(1)}, u32[]{:S(2)}, u32[]{:S(2)}) %collective-permute-start.12) | collective-permute-done | bytes 344096 | tf_op jit(solution)/shard_map/ppermute | solution.py:40
  124.4 1.9 %collective-permute-start.14 = (bf16[224,256]{1,0:T(8,128)(2,1)S(1)}, bf16[224,256]{1,0:T(8,128)(2,1)S(1)}, u32[]{:S(2)}, u32[]{:S(2)}) collective-permute-start(bf16[224,256]{1,0:T(8,128)(2,1)S(1)} %get-tuple-element.23), channel_id=1, source_target_pairs={{32,0},{36,4},{40,8},{44,12},{48,16},{52,20},{56,24},{60,28},{64,3... | collective-permute-start | bytes 344072 | tf_op jit(solution)/shard_map/ppermute | solution.py:40
  127.6 3.5 %collective-permute-done.14 = bf16[224,256]{1,0:T(8,128)(2,1)S(1)} collective-permute-done((bf16[224,256]{1,0:T(8,128)(2,1)S(1)}, bf16[224,256]{1,0:T(8,128)(2,1)S(1)}, u32[]{:S(2)}, u32[]{:S(2)}) %collective-permute-start.14) | collective-permute-done | bytes 114720 | tf_op jit(solution)/shard_map/ppermute | solution.py:40
  131.1 3.4 %collective-permute-done.15 = bf16[224,256]{1,0:T(8,128)(2,1)S(1)} collective-permute-done((bf16[224,256]{1,0:T(8,128)(2,1)S(1)}, bf16[224,256]{1,0:T(8,128)(2,1)S(1)}, u32[]{:S(2)}, u32[]{:S(2)}) %collective-permute-start.15) | collective-permute-done | bytes 114720 | tf_op jit(solution)/shard_map/ppermute | solution.py:40
  (53 shorter events, 17.6 us)
Async XLA Ops:
  7.2 29.3 %copy-start.4 = (s32[224]{0:T(256)S(1)}, s32[224]{0:T(256)}, u32[]{:S(2)}) copy-start(s32[224]{0:T(256)} %param.9) | copy-start | bytes 2692
  7.2 58.8 %all-gather.2.cloned.1.call-start = ((), (), s32[]{:S(2)}) async-start(), calls=%async_computation.2 | async-start | bytes 2867200 | tf_op jit(solution)/shard_map/all_gather | solution.py:264
  7.9 127.3 %reduce-scatter.2.cloned.1.call-start = ((), (), s32[]{:S(2)}) async-start(), calls=%async_computation.1 | async-start | bytes 2867200 | tf_op jit(solution)/shard_map/reduce_scatter | solution.py:262
  9.5 7.0 %collective-permute-start.4 = (bf16[240,256]{1,0:T(8,128)(2,1)S(1)}, bf16[240,256]{1,0:T(8,128)(2,1)S(1)}, u32[]{:S(2)}, u32[]{:S(2)}) collective-permute-start(bf16[240,256]{1,0:T(8,128)(2,1)S(1)} %get-tuple-element.28), channel_id=1, source_target_pairs={{0,32},{4,36},{8,40},{12,44},{16,48},{20,52},{24,56},{28,60},{32,6... | collective-permute-start | bytes 368648 | tf_op jit(solution)/shard_map/ppermute | solution.py:40
  13.0 4.6 %collective-permute-start.5 = (bf16[240,256]{1,0:T(8,128)(2,1)S(1)}, bf16[240,256]{1,0:T(8,128)(2,1)S(1)}, u32[]{:S(2)}, u32[]{:S(2)}) collective-permute-start(bf16[240,256]{1,0:T(8,128)(2,1)S(1)} %get-tuple-element.28), channel_id=1, source_target_pairs={{0,64},{4,68},{8,72},{12,76},{16,80},{20,84},{24,88},{28,92},{32,9... | collective-permute-start | bytes 368648 | tf_op jit(solution)/shard_map/ppermute | solution.py:40
  17.6 10.8 %collective-permute-start.7 = (bf16[2,240,256]{2,1,0:T(8,128)(2,1)S(1)}, bf16[2,240,256]{2,1,0:T(8,128)(2,1)S(1)}, u32[]{:S(2)}, u32[]{:S(2)}) collective-permute-start(bf16[2,240,256]{2,1,0:T(8,128)(2,1)S(1)} %get-tuple-element.26), channel_id=1, source_target_pairs={{0,16},{4,20},{8,24},{12,28},{16,0},{20,4},{24,8},{28,12},{32,48},... | collective-permute-start | bytes 737288 | tf_op jit(solution)/shard_map/ppermute | solution.py:40
  21.6 10.2 %collective-permute-start.6 = (bf16[2,240,256]{2,1,0:T(8,128)(2,1)S(1)}, bf16[2,240,256]{2,1,0:T(8,128)(2,1)S(1)}, u32[]{:S(2)}, u32[]{:S(2)}) collective-permute-start(bf16[2,240,256]{2,1,0:T(8,128)(2,1)S(1)} %get-tuple-element.26), channel_id=1, source_target_pairs={{0,8},{4,12},{8,16},{12,20},{16,24},{20,28},{24,0},{28,4},{32,40},... | collective-permute-start | bytes 737288 | tf_op jit(solution)/shard_map/ppermute | solution.py:40
  22.6 9.9 %collective-permute-start.8 = (bf16[2,240,256]{2,1,0:T(8,128)(2,1)S(1)}, bf16[2,240,256]{2,1,0:T(8,128)(2,1)S(1)}, u32[]{:S(2)}, u32[]{:S(2)}) collective-permute-start(bf16[2,240,256]{2,1,0:T(8,128)(2,1)S(1)} %get-tuple-element.26), channel_id=1, source_target_pairs={{0,24},{4,28},{8,0},{12,4},{16,8},{20,12},{24,16},{28,20},{32,56},... | collective-permute-start | bytes 737288 | tf_op jit(solution)/shard_map/ppermute | solution.py:40
  32.7 14.3 %copy-start = (bf16[4,2,240,256]{3,2,1,0:T(8,128)(2,1)}, bf16[4,2,240,256]{3,2,1,0:T(8,128)(2,1)S(1)}, u32[]{:S(2)}) copy-start(bf16[4,2,240,256]{3,2,1,0:T(8,128)(2,1)S(1)} %pad_maximum_fusion.refs_5_.refs_8_) | copy-start | bytes 2949124
  32.7 14.3 %collective-permute-start.9 = (bf16[4,2,240,256]{3,2,1,0:T(8,128)(2,1)S(1)}, bf16[4,2,240,256]{3,2,1,0:T(8,128)(2,1)S(1)}, u32[]{:S(2)}, u32[]{:S(2)}) collective-permute-start(bf16[4,2,240,256]{3,2,1,0:T(8,128)(2,1)S(1)} %pad_maximum_fusion.refs_5_.refs_8_), channel_id=1, source_target_pairs={{0,4},{4,0},{8,12},{12,8},{16,20},{20,16},{24,28},{28,24},{32,36},... | collective-permute-start | bytes 2949128 | tf_op jit(solution)/shard_map/ppermute | solution.py:40
  32.8 8.6 %collective-permute-start.2 = (bf16[240,256]{1,0:T(8,128)(2,1)S(1)}, bf16[240,256]{1,0:T(8,128)(2,1)S(1)}, u32[]{:S(2)}, u32[]{:S(2)}) collective-permute-start(bf16[240,256]{1,0:T(8,128)(2,1)S(1)} %get-tuple-element.28), channel_id=1, source_target_pairs={{0,24},{4,28},{8,0},{12,4},{16,8},{20,12},{24,16},{28,20},{32,56},... | collective-permute-start | bytes 368648 | tf_op jit(solution)/shard_map/ppermute | solution.py:40
  35.5 7.7 %collective-permute-start.1 = (bf16[240,256]{1,0:T(8,128)(2,1)S(1)}, bf16[240,256]{1,0:T(8,128)(2,1)S(1)}, u32[]{:S(2)}, u32[]{:S(2)}) collective-permute-start(bf16[240,256]{1,0:T(8,128)(2,1)S(1)} %get-tuple-element.28), channel_id=1, source_target_pairs={{0,16},{4,20},{8,24},{12,28},{16,0},{20,4},{24,8},{28,12},{32,48},... | collective-permute-start | bytes 368648 | tf_op jit(solution)/shard_map/ppermute | solution.py:40
  36.0 9.0 %collective-permute-start = (bf16[240,256]{1,0:T(8,128)(2,1)S(1)}, bf16[240,256]{1,0:T(8,128)(2,1)S(1)}, u32[]{:S(2)}, u32[]{:S(2)}) collective-permute-start(bf16[240,256]{1,0:T(8,128)(2,1)S(1)} %get-tuple-element.28), channel_id=1, source_target_pairs={{0,8},{4,12},{8,16},{12,20},{16,24},{20,28},{24,0},{28,4},{32,40},... | collective-permute-start | bytes 368648 | tf_op jit(solution)/shard_map/ppermute | solution.py:40
  45.0 2.0 %copy-start.1 = (bf16[4,240,256]{2,1,0:T(8,128)(2,1)}, bf16[4,240,256]{2,1,0:T(8,128)(2,1)S(1)}, u32[]{:S(2)}) copy-start(bf16[4,240,256]{2,1,0:T(8,128)(2,1)S(1)} %pad_maximum_fusion.1.refs_3_.refs_6_) | copy-start | bytes 1474564
  45.0 1.9 %collective-permute-start.3 = (bf16[4,240,256]{2,1,0:T(8,128)(2,1)S(1)}, bf16[4,240,256]{2,1,0:T(8,128)(2,1)S(1)}, u32[]{:S(2)}, u32[]{:S(2)}) collective-permute-start(bf16[4,240,256]{2,1,0:T(8,128)(2,1)S(1)} %pad_maximum_fusion.1.refs_3_.refs_6_), channel_id=1, source_target_pairs={{0,4},{4,0},{8,12},{12,8},{16,20},{20,16},{24,28},{28,24},{32,36},... | collective-permute-start | bytes 1474568 | tf_op jit(solution)/shard_map/ppermute | solution.py:40
  46.9 0.8 copy-start.3
  47.8 1.0 copy-start.2
  88.2 5.4 %collective-permute-start.10 = (bf16[4,3,224,256]{3,2,1,0:T(8,128)(2,1)}, bf16[4,3,224,256]{3,2,1,0:T(8,128)(2,1)S(1)}, u32[]{:S(2)}, u32[]{:S(2)}) collective-permute-start(bf16[4,3,224,256]{3,2,1,0:T(8,128)(2,1)} %get-tuple-element.17), channel_id=1, source_target_pairs={{0,4},{4,0},{8,12},{12,8},{16,20},{20,16},{24,28},{28,24},{32,36},... | collective-permute-start | bytes 4128776 | tf_op jit(solution)/shard_map/ppermute | solution.py:40
  95.4 20.2 %collective-permute-start.11 = (bf16[3,224,256]{2,1,0:T(8,128)(2,1)S(1)}, bf16[3,224,256]{2,1,0:T(8,128)(2,1)S(1)}, u32[]{:S(2)}, u32[]{:S(2)}) collective-permute-start(bf16[3,224,256]{2,1,0:T(8,128)(2,1)S(1)} %get-tuple-element.20), channel_id=1, source_target_pairs={{0,8},{4,12},{8,16},{12,20},{16,24},{20,28},{24,0},{28,4},{32,40},... | collective-permute-start | bytes 1032200 | tf_op jit(solution)/shard_map/ppermute | solution.py:40
  98.1 24.3 %collective-permute-start.13 = (bf16[3,224,256]{2,1,0:T(8,128)(2,1)S(1)}, bf16[3,224,256]{2,1,0:T(8,128)(2,1)S(1)}, u32[]{:S(2)}, u32[]{:S(2)}) collective-permute-start(bf16[3,224,256]{2,1,0:T(8,128)(2,1)S(1)} %get-tuple-element.21), channel_id=1, source_target_pairs={{0,24},{4,28},{8,0},{12,4},{16,8},{20,12},{24,16},{28,20},{32,56},... | collective-permute-start | bytes 1032200 | tf_op jit(solution)/shard_map/ppermute | solution.py:40
  107.1 17.1 %collective-permute-start.12 = (bf16[3,224,256]{2,1,0:T(8,128)(2,1)S(1)}, bf16[3,224,256]{2,1,0:T(8,128)(2,1)S(1)}, u32[]{:S(2)}, u32[]{:S(2)}) collective-permute-start(bf16[3,224,256]{2,1,0:T(8,128)(2,1)S(1)} %get-tuple-element.22), channel_id=1, source_target_pairs={{0,16},{4,20},{8,24},{12,28},{16,0},{20,4},{24,8},{28,12},{32,48},... | collective-permute-start | bytes 1032200 | tf_op jit(solution)/shard_map/ppermute | solution.py:40
  124.4 6.7 %collective-permute-start.14 = (bf16[224,256]{1,0:T(8,128)(2,1)S(1)}, bf16[224,256]{1,0:T(8,128)(2,1)S(1)}, u32[]{:S(2)}, u32[]{:S(2)}) collective-permute-start(bf16[224,256]{1,0:T(8,128)(2,1)S(1)} %get-tuple-element.23), channel_id=1, source_target_pairs={{32,0},{36,4},{40,8},{44,12},{48,16},{52,20},{56,24},{60,28},{64,3... | collective-permute-start | bytes 344072 | tf_op jit(solution)/shard_map/ppermute | solution.py:40
  126.3 8.2 %collective-permute-start.15 = (bf16[224,256]{1,0:T(8,128)(2,1)S(1)}, bf16[224,256]{1,0:T(8,128)(2,1)S(1)}, u32[]{:S(2)}, u32[]{:S(2)}) collective-permute-start(bf16[224,256]{1,0:T(8,128)(2,1)S(1)} %get-tuple-element.24), channel_id=1, source_target_pairs={{64,0},{68,4},{72,8},{76,12},{80,16},{84,20},{88,24},{92,28},{96,3... | collective-permute-start | bytes 344072 | tf_op jit(solution)/shard_map/ppermute | solution.py:40
Sparse Core Ops, SparseCore 0:
  9.7 32.8 all-gather.1
  66.1 31.5 reduce-scatter.1

commit v2 on v1

v2 whole, which is shorter than its diff:
```python
import math

import jax
import jax.numpy as jnp
from jax import lax
from jax.experimental import pallas as pl
from jax.experimental.pallas import tpu as pltpu
from jax.sharding import PartitionSpec as P

HD = 128
GROUP = 5
NX = 4
NY = 4
NZ = 4
TILE = 16
LOW = -1e30
HIGH = 1e30
F32 = jnp.float32
BF16 = jnp.bfloat16
NT = (((1,), (1,)), ((), ()))
TN = (((0,), (0,)), ((), ()))
NN = (((1,), (0,)), ((), ()))


def place(y, z, core):
    return ((y % NY) * NZ + (z % NZ)) * 2 + core


def shift(dy, dz, flip):
    pairs = []
    for y in range(NY):
        for z in range(NZ):
            for core in range(2):
                if 0 <= y + dy < NY:
                    pairs.append((place(y, z, core), place(y + dy, z + dz, core ^ flip)))
    return pairs


def move(value, dy=0, dz=0, flip=0):
    return lax.ppermute(value, "dp", shift(dy, dz, flip))


def move_x(value, dx):
    return lax.ppermute(value, "mp", [(x, (x + dx) % NX) for x in range(NX)])


def dot(a, b, dims):
    return lax.dot_general(a, b, dims, preferred_element_type=F32)


def where_am_i():
    index = lax.axis_index("dp")
    return index // (2 * NZ), (index // 2) % NZ, index % 2


def stack_heads(source, target, rows):
    for head in range(GROUP):
        target[head * rows : (head + 1) * rows, :] = source[:, head * HD : (head + 1) * HD]
    target[GROUP * rows :, :] = jnp.zeros((target.shape[0] - GROUP * rows, HD), BF16)


def spread_heads(stacked, target, rows):
    for head in range(GROUP):
        target[:, head * HD : (head + 1) * HD] = stacked[head * rows : (head + 1) * rows, :]


def joined(parts):
    return parts[0] if len(parts) == 1 else jnp.concatenate(parts, axis=0)


def seen(tile, seg, allowed, rows):
    count = jnp.sum(jnp.where(tile.astype(F32) == seg, 1.0, 0.0))
    return (rows - jnp.where(allowed, count, 0.0)).astype(jnp.int32)


def masks(refs, seg, core, info, rows, width, own):
    at = lax.broadcasted_iota(jnp.int32, (rows, width), 0)
    result = []
    for index, (ref, slot) in enumerate(refs):
        if own and index == 0:
            where = at.astype(F32)
            result.append((where <= info[0:1, :]) & (where >= info[1:2, :]))
        else:
            allowed = core == 1 if own and index == 1 else True
            result.append(at >= seen(ref[slot][rows:, :], seg, allowed, rows))
    return result


def attend(refs, visible, norm_of, q5, rows, factor, state, seen_rows):
    keys = joined([ref[slot][:rows, :HD] for ref, slot in refs])
    values = joined([ref[slot][:rows, HD:] for ref, slot in refs])
    raw = dot(keys, q5, NT)
    scores = [jnp.where(see, raw[i * rows : (i + 1) * rows], LOW) for i, see in enumerate(visible)]
    peak = jnp.max(scores[0], axis=0, keepdims=True)
    for part in scores[1:]:
        peak = jnp.maximum(peak, jnp.max(part, axis=0, keepdims=True))
    peak = peak * factor
    if seen_rows is not None:
        peak = jnp.where(seen_rows, peak, LOW)
    top, total, acc = state
    new = peak if top is None else jnp.maximum(top, peak)
    norm = new if seen_rows is None else jnp.where(seen_rows, new, HIGH)
    weights = [jnp.exp2(part * factor - norm) for part in scores]
    added = sum(jnp.sum(w, axis=0, keepdims=True) for w in weights)
    out = dot(values, joined([w.astype(BF16) for w in weights]), TN)
    if top is None:
        return new, added, out
    alpha = jnp.exp2(top - new)
    return new, total * alpha + added, acc * alpha + out


def column_refs(column, other):
    return [(column, 0), (other, 0), (column, 1), (other, 1), (column, 2), (other, 2)]


def side_refs(side, other, dz):
    return [(side, dz * 2), (other, dz * 2), (side, dz * 2 + 1), (other, dz * 2 + 1)]


def forward_column(rows, factor, seg0, info, q, column, other, top, total, acc, q5):
    stack_heads(q, q5, rows)
    _, _, core = where_am_i()
    width = info.shape[1]
    seg = seg0[0].astype(F32)
    near = info[2:3, :] > 0.5
    refs = column_refs(column, other)
    visible = masks(refs, seg, core, info, rows, width, True)
    state = attend(refs[:1], visible[:1], None, q5[...], rows, factor, (None, None, None), None)
    state = attend(refs[1:], visible[1:], None, q5[...], rows, factor, state, near)
    top[...], total[...], acc[...] = state


def forward_side(
    rows, factor, seg0, weight, info, q5, g5, side, other, top, total, acc,
    lse, delta, here, up, down, far_top, far_end, held, attn, sem,
):
    copy = pltpu.make_async_copy(weight, held, sem)
    copy.start()
    x = lax.axis_index("mp")
    _, _, core = where_am_i()
    width = info.shape[1]
    seg = seg0[0].astype(F32)
    near = info[2:3, :] > 0.5
    state = (top[...], total[...], acc[...])
    for dz in range(NZ - 1):
        refs = side_refs(side, other, dz)
        visible = masks(refs, seg, core, info, rows, width, False)
        state = attend(refs, visible, None, q5[...], rows, factor, state, near)
    out_t = (state[2] / state[1]).astype(BF16)
    spread_heads(out_t.T, attn, rows)
    lse[...] = state[0] + jnp.log2(state[1])
    delta[...] = jnp.sum(out_t.astype(F32) * g5[...].T.astype(F32), axis=0, keepdims=True)
    copy.wait()
    part = here.shape[1]

    def features(dx):
        column = pl.multiple_of(lax.rem(x + dx, NX) * part, 128)
        return dot(attn[...], held[:, pl.ds(column, part)], NN).astype(BF16)

    far = features(2)
    far_top[...] = far[: rows // 2]
    far_end[...] = far[rows // 2 :]
    up[...] = features(1)
    down[...] = features(3)
    here[...] = features(0)


def grads_of(refs, visible, norm, delta, q5, g5, rows, factor, scale):
    keys = joined([ref[slot][:rows, :HD] for ref, slot in refs])
    values = joined([ref[slot][:rows, HD:] for ref, slot in refs])
    raw = dot(keys, q5, NT)
    slope = dot(values, g5, NT)
    weights = []
    for i, see in enumerate(visible):
        part = raw[i * rows : (i + 1) * rows] * factor - norm
        weights.append(jnp.exp2(jnp.where(see, part, LOW)))
    weights = joined(weights)
    slope = (weights * (slope - delta)).astype(BF16)
    d_value = dot(weights.astype(BF16), g5, NN).astype(BF16)
    d_key = (dot(slope, q5, NN) * scale).astype(BF16)
    return d_key, d_value, dot(keys, slope, TN)


def backward_side(rows, factor, scale, parts, seg0, info, q5, g5, lse, delta, side, other, *rest):
    *before, acc, stay, leave = rest
    _, _, core = where_am_i()
    width = info.shape[1]
    seg = seg0[0].astype(F32)
    norm = jnp.where(info[2:3, :] > 0.5, lse[...], HIGH)
    total = before[0][...] if before else None
    for place_out, dz in enumerate(parts):
        refs = side_refs(side, other, dz - 1)
        visible = masks(refs, seg, core, info, rows, width, False)
        d_key, d_value, d_query = grads_of(refs, visible, norm, delta[...], q5[...], g5[...], rows, factor, scale)
        for i, (out, kind) in enumerate(((stay, 0), (leave, 0), (stay, 1), (leave, 1))):
            out[place_out, kind, :, :HD] = d_key[i * rows : (i + 1) * rows]
            out[place_out, kind, :, HD:] = d_value[i * rows : (i + 1) * rows]
        total = d_query if total is None else total + d_query
    acc[...] = total


def backward_column(rows, factor, scale, seg0, info, q5, g5, lse, delta, column, other, acc, dq, stay, leave):
    _, _, core = where_am_i()
    width = info.shape[1]
    seg = seg0[0].astype(F32)
    norm = jnp.where(info[2:3, :] > 0.5, lse[...], HIGH)
    refs = column_refs(column, other)
    outs = ((stay, 0), (leave, 0), (stay, 1), (leave, 1), (stay, 2), (leave, 2))
    visible = masks(refs, seg, core, info, rows, width, True)
    total = acc[...]
    for part, limit in ((slice(0, 1), lse[...]), (slice(1, 6), norm)):
        d_key, d_value, d_query = grads_of(
            refs[part], visible[part], limit, delta[...], q5[...], g5[...], rows, factor, scale
        )
        for i, (out, kind) in enumerate(outs[part]):
            out[kind, :, :HD] = d_key[i * rows : (i + 1) * rows]
            out[kind, :, HD:] = d_value[i * rows : (i + 1) * rows]
        total = total + d_query
    spread_heads((total * scale).astype(BF16).T, dq, rows)


def grad_heads(g0, g1, g2_top, g2_end, g3, weight, g5, held, weights, sem):
    x = lax.axis_index("mp")
    _, rows, part = held.shape
    half = rows // 2
    order = (0, 1, 3, 2)
    columns = [pl.multiple_of(lax.rem(x + NX - back, NX) * part, 128) for back in range(NX)]
    loads = [
        pltpu.make_async_copy(weight.at[:, pl.ds(columns[back], part)], weights.at[back], sem.at[back])
        for back in order
    ]
    pieces = (
        (g0, held.at[0]),
        (g1, held.at[1]),
        (g3, held.at[3]),
        (g2_top, held.at[2, pl.ds(0, half)]),
        (g2_end, held.at[2, pl.ds(half, half)]),
    )
    copies = [pltpu.make_async_copy(src, dst, sem.at[NX + i]) for i, (src, dst) in enumerate(pieces)]
    for copy in (loads[0], copies[0], loads[1], copies[1], loads[2], copies[2], loads[3], copies[3], copies[4]):
        copy.start()
    total = None
    for i, back in enumerate(order):
        loads[i].wait()
        copies[i].wait()
        if back == 2:
            copies[4].wait()
        term = dot(held[back], weights[back], NT)
        total = term if total is None else total + term
    stack_heads(total.astype(BF16), g5, rows)


def add_up(*terms):
    return sum(t.astype(F32) for t in terms)


def row_info(seg_ids, width):
    rows = seg_ids.shape[0]
    position = jnp.arange(rows, dtype=F32)
    start = jnp.sum(seg_ids[None, :] < seg_ids[:, None], axis=1).astype(F32)
    near = (seg_ids == seg_ids[0]).astype(F32)
    info = jnp.stack([position, start, near] + [jnp.zeros(rows, F32)] * 5)
    info = jnp.tile(info, (1, GROUP))
    return jnp.concatenate([info, jnp.tile(info[:, -1:], (1, width - GROUP * rows))], axis=1)


def per_device(queries, keys, values, seg_ids, out_weight, grad_out):
    rows = queries.shape[0]
    scale = 1.0 / math.sqrt(HD)
    factor = scale * math.log2(math.e)
    width = -(-GROUP * rows // 128) * 128
    _, z, _ = where_am_i()
    x = lax.axis_index("mp")
    vmem = pl.BlockSpec(memory_space=pltpu.VMEM)
    smem = pl.BlockSpec(memory_space=pltpu.SMEM)

    def shape(*dims, dtype=BF16):
        return jax.ShapeDtypeStruct(dims, dtype)

    anywhere = pl.BlockSpec(memory_space=pl.ANY)

    fixed = pl.BlockSpec(memory_space=pltpu.HBM)

    def call(body, outs, micros, *operands, scalars=1, loose=0, pinned=0, scratch=(), mib=24):
        return pl.pallas_call(
            body,
            out_shape=outs,
            in_specs=[smem] * scalars
            + [anywhere] * loose
            + [fixed] * pinned
            + [vmem] * (len(operands) - scalars - loose - pinned),
            out_specs=jax.tree.map(lambda _: vmem, outs),
            scratch_shapes=scratch,
            cost_estimate=pl.CostEstimate(flops=micros * 1_153_000_000, bytes_accessed=0, transcendentals=0),
            compiler_params=pltpu.CompilerParams(vmem_limit_bytes=mib * 1024 * 1024),
        )(*operands)

    line = shape(1, width, dtype=F32)
    square = shape(HD, width, dtype=F32)
    stacked = shape(width, HD)
    half = rows // 2

    segs = jnp.pad(
        (seg_ids + 1).astype(BF16)[None, :], ((0, TILE - 1), (0, 2 * HD - rows)), constant_values=0
    )
    seg0 = seg_ids[:1] + 1
    info = row_info(seg_ids, width)
    own = jnp.concatenate([jnp.concatenate([keys, values], axis=1), segs], axis=0)
    y1, y2 = move(own, dy=1), move(own, dy=2)
    g1, g3 = move_x(grad_out, 1), move_x(grad_out, 3)
    y1, y2, g1, g3 = lax.optimization_barrier((y1, y2, g1, g3))

    column = jnp.stack([own, y1, y2])
    column_other = move(column, flip=1)
    sides = [None] * (NZ - 1)
    for dz in (2, 1, 3):
        sides[dz - 1] = move(jnp.stack([y1, jnp.where(z + dz < NZ, own, y2)]), dz=dz)
    g2_top, g2_end = move_x(g1[:half], 1), move_x(g3[half:], 3)
    top, total, acc, q5 = call(
        lambda *refs: forward_column(rows, factor, *refs),
        (line, line, square, stacked), 3, seg0, info, queries, column, column_other,
    )
    *sides, g2_top, g2_end, top = lax.optimization_barrier((*sides, g2_top, g2_end, top))

    side = jnp.concatenate(sides)
    side_other = move(side, flip=1)
    part = grad_out.shape[1]
    g5 = call(
        grad_heads, stacked, 4, grad_out, g1, g2_top, g2_end, g3, out_weight, scalars=0, loose=5, pinned=1,
        scratch=[
            pltpu.VMEM((NX, rows, part), BF16),
            pltpu.VMEM((NX, out_weight.shape[0], part), BF16),
            pltpu.SemaphoreType.DMA((NX + 5,)),
        ],
    )
    whole, halved = shape(rows, part), shape(half, part)
    lse, delta, here, up, down, *far = call(
        lambda *refs: forward_side(rows, factor, *refs),
        (line, line, whole, whole, whole, halved, halved), 8,
        seg0, out_weight, info, q5, g5, side, side_other, top, total, acc, pinned=1, mib=30,
        scratch=[
            pltpu.VMEM(out_weight.shape, BF16),
            pltpu.VMEM((rows, GROUP * HD), BF16),
            pltpu.SemaphoreType.DMA,
        ],
    )
    early = (move_x(far[0], 1), move_x(far[1], 3))

    def side_grads(parts, micros, *before):
        pieces = shape(len(parts), 2, rows, 2 * HD)
        return call(
            lambda *refs: backward_side(rows, factor, scale, parts, *refs),
            (square, pieces, pieces), micros, seg0, info, q5, g5, lse, delta, side, side_other, *before,
        )

    acc, stay, leave, *early = lax.optimization_barrier((*side_grads((2, 1), 6), *early))
    up = jnp.concatenate([add_up(up[:half], early[0]).astype(BF16), up[half:]], axis=0)
    down = jnp.concatenate([down[:half], add_up(down[half:], early[1]).astype(BF16)], axis=0)
    other = move(leave, flip=1)
    acc, stay_last, leave_last, other = lax.optimization_barrier((*side_grads((3,), 3, acc), other))
    other_last = move(leave_last, flip=1)
    mixed = add_up(stay, other).astype(BF16)
    returned = {2: move(mixed[0], dz=-2), 1: move(mixed[1], dz=-1)}
    returned[3] = move(add_up(stay_last[0], other_last[0]).astype(BF16), dz=-3)
    column_grads = shape(3, rows, 2 * HD)
    up, down = move_x(up, 1), move_x(down, 3)
    grad_query, stay, leave, returned[1], returned[2], returned[3], up, down = lax.optimization_barrier(
        (
            *call(
                lambda *refs: backward_column(rows, factor, scale, *refs),
                (shape(rows, GROUP * HD), column_grads, column_grads), 5,
                seg0, info, q5, g5, lse, delta, column, column_other, acc,
            ),
            returned[1], returned[2], returned[3], up, down,
        )
    )
    projected = add_up(here, up, down).astype(BF16)
    mixed = add_up(stay, move(leave, flip=1))
    first, second, third = mixed[0], mixed[1], mixed[2]
    for dz in range(1, NZ):
        far, near = returned[dz][0].astype(F32), returned[dz][1].astype(F32)
        second = second + far
        first = first + jnp.where(z + dz < NZ, near, 0.0)
        third = third + jnp.where(z + dz < NZ, 0.0, near)
    second, third = second.astype(BF16), third.astype(BF16)
    grads = add_up(first, move(second, dy=-1), move(third, dy=-2)).astype(BF16)
    return (projected, grad_query, grads[:, :HD], grads[:, HD:])


def solution(mesh):
    return jax.shard_map(
        per_device,
        mesh=mesh,
        in_specs=(
            P("dp", "mp"),
            P("dp", "mp"),
            P("dp", "mp"),
            P("dp"),
            P("mp", None),
            P("dp", "mp"),
        ),
        out_specs=(P("dp", "mp"), P("dp", "mp"), P("dp", "mp"), P("dp", "mp")),
        check_vma=False,
    )
```

time: 144 us -> 97.1 us (0.67); the launches traced: 142 us -> 96.8 us
  waiting for transfers between devices: 44.3 us -> 26.5 us
  matrix products: 12.9 us -> 0 us
  between operations: 14.2 us -> 1.65 us
  starting transfers between devices: 35.4 us -> 30.6 us
  Pallas kernels: 26.5 us -> 29 us
    ppermute x16 -> x15, waiting for transfers between devices: 43.6 us -> 19.5 us  [move(): return lax.ppermute(value, 'dp', shift(dy, dz, flip))]
    ppermute x16 -> x15, starting transfers between devices: 35.3 us -> 20.9 us  [move(): return lax.ppermute(value, 'dp', shift(dy, dz, flip))]
    dot_general x2 -> x0, matrix products: 12.9 us -> none  [the longest x1 6.54 us: per_device(): lax.dot_general(lax.all_gather(grad_out, 'mp', axis=1, tiled=True), out_w...]
    ppermute x0 -> x8, starting transfers between devices: none -> 9.73 us  [move_x(): return lax.ppermute(value, 'mp', [(x, (x + dx) % NX) for x in range(NX)])]
    ppermute x0 -> x8, waiting for transfers between devices: none -> 6.95 us  [move_x(): return lax.ppermute(value, 'mp', [(x, (x + dx) % NX) for x in range(NX)])]
    pallas_call x2 -> x6, Pallas kernels: 26.5 us -> 29 us  [call(): pl.pallas_call(body, out_shape=outs, in_specs=[smem] * scalars + [anywher...]
    unnamed x10, local copies, waits for them, and re-layouts: 1.79 us -> 0.06 us
  transfers between devices with their start and end apart: 18 -> 23, of which waited for: 15 -> 11; matrix products, arithmetic and copies ran while one was open for 14% -> 7% of each run, Pallas kernels for 19% -> 22%
where the time goes in v2:
time: 97.1 us; the launch traced here: 96.8 us
  starting transfers between devices  30.6 us (32%)
  Pallas kernels  29 us (30%)
  waiting for transfers between devices  26.5 us (27%)
  other arithmetic  6.68 us (7%)
  local copies, waits for them, and re-layouts  2.42 us (2%)
  between operations  1.65 us (2%)
    pallas_call x6, Pallas kernels, call(): pl.pallas_call(body, out_shape=outs, in_specs=[smem] * scalars + [anywher...  29 us
    ppermute x15, starting transfers between devices, move(): return lax.ppermute(value, 'dp', shift(dy, dz, flip))  20.9 us
    ppermute x15, waiting for transfers between devices, move(): return lax.ppermute(value, 'dp', shift(dy, dz, flip))  19.5 us
    ppermute x8, starting transfers between devices, move_x(): return lax.ppermute(value, 'mp', [(x, (x + dx) % NX) for x in range(NX)])  9.73 us
    ppermute x8, waiting for transfers between devices, move_x(): return lax.ppermute(value, 'mp', [(x, (x + dx) % NX) for x in range(NX)])  6.95 us
  transfers between devices with their start and end apart: 23, of which 11 were waited for; matrix products, arithmetic and copies ran while one was open for 7% of the time, Pallas kernels for 22%

profile of v2, /device:TPU:14, one launch (start us, length us, event | category | flops | bytes accessed | tf_op | source)
XLA Modules:
  0.0 96.8 jit_solution(12186411831219574206)
XLA Ops:
  1.2 1.5 %collective-permute-start.3 = (bf16[224,1280]{1,0:T(8,128)(2,1)}, bf16[224,1280]{1,0:T(8,128)(2,1)S(1)}, u32[]{:S(2)}, u32[]{:S(2)}) collective-permute-start(bf16[224,1280]{1,0:T(8,128)(2,1)} %g0.1), channel_id=1, source_target_pairs={{0,3},{1,0},{2,1},{3,2},{4,7},{5,4},{6,5},{7,6},{8,11},{9,8},{10,9... | collective-permute-start | bytes 1720328 | tf_op jit(solution)/shard_map/ppermute | solution.py:44
  4.3 3.5 %collective-permute-start = (bf16[240,256]{1,0:T(8,128)(2,1)S(1)}, bf16[240,256]{1,0:T(8,128)(2,1)S(1)}, u32[]{:S(2)}, u32[]{:S(2)}) collective-permute-start(bf16[240,256]{1,0:T(8,128)(2,1)S(1)} %fusion.16), channel_id=1, source_target_pairs={{0,32},{4,36},{8,40},{12,44},{16,48},{20,52},{24,56},{28,60},{32,6... | collective-permute-start | bytes 368648 | tf_op jit(solution)/shard_map/ppermute | solution.py:40
  7.8 2.0 %collective-permute-start.1 = (bf16[240,256]{1,0:T(8,128)(2,1)S(1)}, bf16[240,256]{1,0:T(8,128)(2,1)S(1)}, u32[]{:S(2)}, u32[]{:S(2)}) collective-permute-start(bf16[240,256]{1,0:T(8,128)(2,1)S(1)} %fusion.16), channel_id=1, source_target_pairs={{0,64},{4,68},{8,72},{12,76},{16,80},{20,84},{24,88},{28,92},{32,9... | collective-permute-start | bytes 368648 | tf_op jit(solution)/shard_map/ppermute | solution.py:40
  13.5 2.2 %collective-permute-done.2.g1 = bf16[224,1280]{1,0:T(8,128)(2,1)S(1)} collective-permute-done((bf16[224,1280]{1,0:T(8,128)(2,1)}, bf16[224,1280]{1,0:T(8,128)(2,1)S(1)}, u32[]{:S(2)}, u32[]{:S(2)}) %collective-permute-start.2) | collective-permute-done | bytes 573472 | tf_op jit(solution)/shard_map/ppermute | solution.py:44
  19.2 2.0 %collective-permute-start.5 = (bf16[2,240,256]{2,1,0:T(8,128)(2,1)S(1)}, bf16[2,240,256]{2,1,0:T(8,128)(2,1)S(1)}, u32[]{:S(2)}, u32[]{:S(2)}) collective-permute-start(bf16[2,240,256]{2,1,0:T(8,128)(2,1)S(1)} %get-tuple-element.107), channel_id=1, source_target_pairs={{0,8},{4,12},{8,16},{12,20},{16,24},{20,28},{24,0},{28,4},{32,40},... | collective-permute-start | bytes 737288 | tf_op jit(solution)/shard_map/ppermute | solution.py:40
  21.1 3.6 %collective-permute-start.6 = (bf16[2,240,256]{2,1,0:T(8,128)(2,1)S(1)}, bf16[2,240,256]{2,1,0:T(8,128)(2,1)S(1)}, u32[]{:S(2)}, u32[]{:S(2)}) collective-permute-start(bf16[2,240,256]{2,1,0:T(8,128)(2,1)S(1)} %get-tuple-element.106), channel_id=1, source_target_pairs={{0,16},{4,20},{8,24},{12,28},{16,0},{20,4},{24,8},{28,12},{32,48},... | collective-permute-start | bytes 737288 | tf_op jit(solution)/shard_map/ppermute | solution.py:40
  26.2 1.8 %collective-permute-start.9 = (bf16[112,1280]{1,0:T(8,128)(2,1)S(1)}, bf16[112,1280]{1,0:T(8,128)(2,1)S(1)}, u32[]{:S(2)}, u32[]{:S(2)}) collective-permute-start(bf16[112,1280]{1,0:T(8,128)(2,1)S(1)} %slice.67), channel_id=1, source_target_pairs={{0,3},{1,0},{2,1},{3,2},{4,7},{5,4},{6,5},{7,6},{8,11},{9,8},{10,9... | collective-permute-start | bytes 860168 | tf_op jit(solution)/shard_map/ppermute | solution.py:44
  28.0 3.1 %shard_map.93 = (f32[1,1152]{1,0:T(1,128)S(1)}, f32[1,1152]{1,0:T(1,128)S(1)}, f32[128,1152]{1,0:T(8,128)S(1)}, bf16[1152,128]{1,0:T(8,128)(2,1)S(1)}) custom-call(s32[1]{0:T(128)S(6)} %add.99.refs_0_, f32[8,1152]{1,0:T(8,128)S(1)} %pad_maximum_fusion.6.refs_1_.refs_2_, bf16[224,640]{1,0:T(8,128)(2,1)S(1)} %copy-done.1, ...), custom_call_target="tpu_custom_call" | custom-call | flops 3459000064 | tf_op jit(solution)/shard_map/pallas_call | solution.py:285
  31.1 5.2 %collective-permute-done.6 = bf16[2,240,256]{2,1,0:T(8,128)(2,1)S(1)} collective-permute-done((bf16[2,240,256]{2,1,0:T(8,128)(2,1)S(1)}, bf16[2,240,256]{2,1,0:T(8,128)(2,1)S(1)}, u32[]{:S(2)}, u32[]{:S(2)}) %collective-permute-start.6) | collective-permute-done | bytes 245792 | tf_op jit(solution)/shard_map/ppermute | solution.py:40
  36.7 4.3 %shard_map.94.refs_4_.refs_3_ = bf16[1152,128]{1,0:T(8,128)(2,1)S(1)} custom-call(bf16[224,1280]{1,0:T(8,128)(2,1)S(1)} %copy-done, bf16[224,1280]{1,0:T(8,128)(2,1)S(1)} %collective-permute-done.2.g1, bf16[112,1280]{1,0:T(8,128)(2,1)S(1)} %collective-permute-done.8.g2_top, bf16[112,1280]{1,0:T(8,128)(2,1)S(1)} %collective-permute-done.9.g2_end, ...), custom_call_target="tpu_custom_call" | custom-call | flops 4611999744 | tf_op jit(solution)/shard_map/pallas_call | solution.py:285
  41.0 8.0 %shard_map.95 = (f32[1,1152]{1,0:T(1,128)S(1)}, f32[1,1152]{1,0:T(1,128)S(1)}, bf16[224,1280]{1,0:T(8,128)(2,1)S(1)}, bf16[224,1280]{1,0:T(8,128)(2,1)S(1)}, bf1...) custom-call(s32[1]{0:T(128)S(6)} %add.99.refs_0_, ...), custom_call_target="tpu_custom_call" | custom-call | flops 9223999488 | tf_op jit(solution)/shard_map/pallas_call | solution.py:285
  49.4 1.7 %collective-permute-start.12 = (bf16[112,1280]{1,0:T(8,128)(2,1)S(1)}, bf16[112,1280]{1,0:T(8,128)(2,1)S(1)}, u32[]{:S(2)}, u32[]{:S(2)}) collective-permute-start(bf16[112,1280]{1,0:T(8,128)(2,1)S(1)} %get-tuple-element.72), channel_id=1, source_target_pairs={{0,3},{1,0},{2,1},{3,2},{4,7},{5,4},{6,5},{7,6},{8,11},{9,8},{10,9... | collective-permute-start | bytes 860168 | tf_op jit(solution)/shard_map/ppermute | solution.py:44
  51.2 5.6 %shard_map.96 = (f32[128,1152]{1,0:T(8,128)S(1)}, bf16[2,2,224,256]{3,2,1,0:T(8,128)(2,1)S(1)}, bf16[2,2,224,256]{3,2,1,0:T(8,128)(2,1)S(1)}) custom-call(s32[1]{0:T(128)S(6)} %add.99.refs_0_, f32[8,1152]{1,0:T(8,128)S(1)} %pad_maximum_fusion.6.refs_1_.refs_2_, bf16[1152,128]{1,0:T(8,128)(2,1)S(1)} %get-tuple-element.53.refs_3_.refs_2_, ...), custom_call_target="tpu_custom_call" | custom-call | flops 6918000128 | tf_op jit(solution)/shard_map/pallas_call | solution.py:285
  56.8 1.6 %collective-permute-done.11 = bf16[112,1280]{1,0:T(8,128)(2,1)S(1)} collective-permute-done((bf16[112,1280]{1,0:T(8,128)(2,1)S(1)}, bf16[112,1280]{1,0:T(8,128)(2,1)S(1)}, u32[]{:S(2)}, u32[]{:S(2)}) %collective-permute-start.11) | collective-permute-done | bytes 286752 | tf_op jit(solution)/shard_map/ppermute | solution.py:44
  60.5 3.1 %collective-permute-start.18 = (bf16[224,1280]{1,0:T(8,128)(2,1)S(1)}, bf16[224,1280]{1,0:T(8,128)(2,1)S(1)}, u32[]{:S(2)}, u32[]{:S(2)}) collective-permute-start(bf16[224,1280]{1,0:T(8,128)(2,1)S(1)} %pad_maximum_fusion), channel_id=1, source_target_pairs={{0,1},{1,2},{2,3},{3,0},{4,5},{5,6},{6,7},{7,4},{8,9},{9,10},{10,1... | collective-permute-start | bytes 1720328 | tf_op jit(solution)/shard_map/ppermute | solution.py:44
  63.6 2.9 %shard_map.97 = (f32[128,1152]{1,0:T(8,128)S(1)}, bf16[1,2,224,256]{3,2,1,0:T(8,128)(2,1)S(1)}, bf16[1,2,224,256]{3,2,1,0:T(8,128)(2,1)S(1)}) custom-call(s32[1]{0:T(128)S(6)} %add.99.refs_0_, f32[8,1152]{1,0:T(8,128)S(1)} %pad_maximum_fusion.6.refs_1_.refs_2_, bf16[1152,128]{1,0:T(8,128)(2,1)S(1)} %get-tuple-element.53.refs_3_.refs_2_, ...), custom_call_target="tpu_custom_call" | custom-call | flops 3459000064 | tf_op jit(solution)/shard_map/pallas_call | solution.py:285
  66.9 2.2 %collective-permute-start.14 = (bf16[2,224,256]{2,1,0:T(8,128)(2,1)S(1)}, bf16[2,224,256]{2,1,0:T(8,128)(2,1)S(1)}, u32[]{:S(2)}, u32[]{:S(2)}) collective-permute-start(bf16[2,224,256]{2,1,0:T(8,128)(2,1)S(1)} %get-tuple-element.101), channel_id=1, source_target_pairs={{0,24},{4,28},{8,0},{12,4},{16,8},{20,12},{24,16},{28,20},{32,56},... | collective-permute-start | bytes 688136 | tf_op jit(solution)/shard_map/ppermute | solution.py:40
  71.1 5.1 %shard_map.98 = (bf16[224,640]{1,0:T(8,128)(2,1)}, bf16[3,224,256]{2,1,0:T(8,128)(2,1)S(1)}, bf16[3,224,256]{2,1,0:T(8,128)(2,1)S(1)}) custom-call(s32[1]{0:T(128)S(6)} %add.99.refs_0_, f32[8,1152]{1,0:T(8,128)S(1)} %pad_maximum_fusion.6.refs_1_.refs_2_, bf16[1152,128]{1,0:T(8,128)(2,1)S(1)} %get-tuple-element.53.refs_3_.refs_2_, ...), custom_call_target="tpu_custom_call" | custom-call | flops 5765000192 | tf_op jit(solution)/shard_map/pallas_call | solution.py:285
  76.5 2.9 %collective-permute-done.14 = bf16[2,224,256]{2,1,0:T(8,128)(2,1)S(1)} collective-permute-done((bf16[2,224,256]{2,1,0:T(8,128)(2,1)S(1)}, bf16[2,224,256]{2,1,0:T(8,128)(2,1)S(1)}, u32[]{:S(2)}, u32[]{:S(2)}) %collective-permute-start.14) | collective-permute-done | bytes 229408 | tf_op jit(solution)/shard_map/ppermute | solution.py:40
  79.4 3.7 %collective-permute-done.17 = bf16[2,224,256]{2,1,0:T(8,128)(2,1)S(1)} collective-permute-done((bf16[2,224,256]{2,1,0:T(8,128)(2,1)S(1)}, bf16[2,224,256]{2,1,0:T(8,128)(2,1)S(1)}, u32[]{:S(2)}, u32[]{:S(2)}) %collective-permute-start.17) | collective-permute-done | bytes 229408 | tf_op jit(solution)/shard_map/ppermute | solution.py:40
  83.1 1.6 %collective-permute-done.20 = bf16[3,224,256]{2,1,0:T(8,128)(2,1)S(1)} collective-permute-done((bf16[3,224,256]{2,1,0:T(8,128)(2,1)S(1)}, bf16[3,224,256]{2,1,0:T(8,128)(2,1)S(1)}, u32[]{:S(2)}, u32[]{:S(2)}) %collective-permute-start.20) | collective-permute-done | bytes 344096 | tf_op jit(solution)/shard_map/ppermute | solution.py:40
  85.0 2.7 %collective-permute-start.21 = (bf16[224,256]{1,0:T(8,128)(2,1)S(1)}, bf16[224,256]{1,0:T(8,128)(2,1)S(1)}, u32[]{:S(2)}, u32[]{:S(2)}) collective-permute-start(bf16[224,256]{1,0:T(8,128)(2,1)S(1)} %get-tuple-element.98), channel_id=1, source_target_pairs={{32,0},{36,4},{40,8},{44,12},{48,16},{52,20},{56,24},{60,28},{64,3... | collective-permute-start | bytes 344072 | tf_op jit(solution)/shard_map/ppermute | solution.py:40
  90.0 2.0 %collective-permute-done.21 = bf16[224,256]{1,0:T(8,128)(2,1)S(1)} collective-permute-done((bf16[224,256]{1,0:T(8,128)(2,1)S(1)}, bf16[224,256]{1,0:T(8,128)(2,1)S(1)}, u32[]{:S(2)}, u32[]{:S(2)}) %collective-permute-start.21) | collective-permute-done | bytes 114720 | tf_op jit(solution)/shard_map/ppermute | solution.py:40
  92.1 3.9 %collective-permute-done.22 = bf16[224,256]{1,0:T(8,128)(2,1)S(1)} collective-permute-done((bf16[224,256]{1,0:T(8,128)(2,1)S(1)}, bf16[224,256]{1,0:T(8,128)(2,1)S(1)}, u32[]{:S(2)}, u32[]{:S(2)}) %collective-permute-start.22) | collective-permute-done | bytes 114720 | tf_op jit(solution)/shard_map/ppermute | solution.py:40
  (75 shorter events, 18.8 us)
Async XLA Ops:
  0.6 15.0 %collective-permute-start.2 = (bf16[224,1280]{1,0:T(8,128)(2,1)}, bf16[224,1280]{1,0:T(8,128)(2,1)S(1)}, u32[]{:S(2)}, u32[]{:S(2)}) collective-permute-start(bf16[224,1280]{1,0:T(8,128)(2,1)} %g0.1), channel_id=1, source_target_pairs={{0,1},{1,2},{2,3},{3,0},{4,5},{5,6},{6,7},{7,4},{8,9},{9,10},{10,1... | collective-permute-start | bytes 1720328 | tf_op jit(solution)/shard_map/ppermute | solution.py:44
  1.2 15.9 %collective-permute-start.3 = (bf16[224,1280]{1,0:T(8,128)(2,1)}, bf16[224,1280]{1,0:T(8,128)(2,1)S(1)}, u32[]{:S(2)}, u32[]{:S(2)}) collective-permute-start(bf16[224,1280]{1,0:T(8,128)(2,1)} %g0.1), channel_id=1, source_target_pairs={{0,3},{1,0},{2,1},{3,2},{4,7},{5,4},{6,5},{7,6},{8,11},{9,8},{10,9... | collective-permute-start | bytes 1720328 | tf_op jit(solution)/shard_map/ppermute | solution.py:44
  4.3 9.2 %collective-permute-start = (bf16[240,256]{1,0:T(8,128)(2,1)S(1)}, bf16[240,256]{1,0:T(8,128)(2,1)S(1)}, u32[]{:S(2)}, u32[]{:S(2)}) collective-permute-start(bf16[240,256]{1,0:T(8,128)(2,1)S(1)} %fusion.16), channel_id=1, source_target_pairs={{0,32},{4,36},{8,40},{12,44},{16,48},{20,52},{24,56},{28,60},{32,6... | collective-permute-start | bytes 368648 | tf_op jit(solution)/shard_map/ppermute | solution.py:40
  7.8 5.7 %collective-permute-start.1 = (bf16[240,256]{1,0:T(8,128)(2,1)S(1)}, bf16[240,256]{1,0:T(8,128)(2,1)S(1)}, u32[]{:S(2)}, u32[]{:S(2)}) collective-permute-start(bf16[240,256]{1,0:T(8,128)(2,1)S(1)} %fusion.16), channel_id=1, source_target_pairs={{0,64},{4,68},{8,72},{12,76},{16,80},{20,84},{24,88},{28,92},{32,9... | collective-permute-start | bytes 368648 | tf_op jit(solution)/shard_map/ppermute | solution.py:40
  18.0 8.1 %collective-permute-start.4 = (bf16[3,240,256]{2,1,0:T(8,128)(2,1)S(1)}, bf16[3,240,256]{2,1,0:T(8,128)(2,1)S(1)}, u32[]{:S(2)}, u32[]{:S(2)}) collective-permute-start(bf16[3,240,256]{2,1,0:T(8,128)(2,1)S(1)} %pad_maximum_fusion.2.refs_3_.refs_6_), channel_id=1, source_target_pairs={{0,4},{4,0},{8,12},{12,8},{16,20},{20,16},{24,28},{28,24},{32,36},... | collective-permute-start | bytes 1105928 | tf_op jit(solution)/shard_map/ppermute | solution.py:40
  19.2 11.9 %collective-permute-start.5 = (bf16[2,240,256]{2,1,0:T(8,128)(2,1)S(1)}, bf16[2,240,256]{2,1,0:T(8,128)(2,1)S(1)}, u32[]{:S(2)}, u32[]{:S(2)}) collective-permute-start(bf16[2,240,256]{2,1,0:T(8,128)(2,1)S(1)} %get-tuple-element.107), channel_id=1, source_target_pairs={{0,8},{4,12},{8,16},{12,20},{16,24},{20,28},{24,0},{28,4},{32,40},... | collective-permute-start | bytes 737288 | tf_op jit(solution)/shard_map/ppermute | solution.py:40
  21.1 15.2 %collective-permute-start.6 = (bf16[2,240,256]{2,1,0:T(8,128)(2,1)S(1)}, bf16[2,240,256]{2,1,0:T(8,128)(2,1)S(1)}, u32[]{:S(2)}, u32[]{:S(2)}) collective-permute-start(bf16[2,240,256]{2,1,0:T(8,128)(2,1)S(1)} %get-tuple-element.106), channel_id=1, source_target_pairs={{0,16},{4,20},{8,24},{12,28},{16,0},{20,4},{24,8},{28,12},{32,48},... | collective-permute-start | bytes 737288 | tf_op jit(solution)/shard_map/ppermute | solution.py:40
  24.7 11.6 %collective-permute-start.7 = (bf16[2,240,256]{2,1,0:T(8,128)(2,1)S(1)}, bf16[2,240,256]{2,1,0:T(8,128)(2,1)S(1)}, u32[]{:S(2)}, u32[]{:S(2)}) collective-permute-start(bf16[2,240,256]{2,1,0:T(8,128)(2,1)S(1)} %get-tuple-element.105), channel_id=1, source_target_pairs={{0,24},{4,28},{8,0},{12,4},{16,8},{20,12},{24,16},{28,20},{32,56},... | collective-permute-start | bytes 737288 | tf_op jit(solution)/shard_map/ppermute | solution.py:40
  25.8 10.6 %collective-permute-start.8 = (bf16[112,1280]{1,0:T(8,128)(2,1)S(1)}, bf16[112,1280]{1,0:T(8,128)(2,1)S(1)}, u32[]{:S(2)}, u32[]{:S(2)}) collective-permute-start(bf16[112,1280]{1,0:T(8,128)(2,1)S(1)} %slice.66), channel_id=1, source_target_pairs={{0,1},{1,2},{2,3},{3,0},{4,5},{5,6},{6,7},{7,4},{8,9},{9,10},{10,1... | collective-permute-start | bytes 860168 | tf_op jit(solution)/shard_map/ppermute | solution.py:44
  26.1 10.6 %slice-start = ((s8[6553600]{0:T(1024)(128)(4,1)}), s8[4194304]{0:T(1024)(128)(4,1)S(1)}, s32[]{:S(2)}) async-start(s8[6553600]{0:T(1024)(128)(4,1)} %bitcast.31), calls=%async_computation | async-start | bytes 8388608
  26.2 10.2 %collective-permute-start.9 = (bf16[112,1280]{1,0:T(8,128)(2,1)S(1)}, bf16[112,1280]{1,0:T(8,128)(2,1)S(1)}, u32[]{:S(2)}, u32[]{:S(2)}) collective-permute-start(bf16[112,1280]{1,0:T(8,128)(2,1)S(1)} %slice.67), channel_id=1, source_target_pairs={{0,3},{1,0},{2,1},{3,2},{4,7},{5,4},{6,5},{7,6},{8,11},{9,8},{10,9... | collective-permute-start | bytes 860168 | tf_op jit(solution)/shard_map/ppermute | solution.py:44
  36.4 4.6 %collective-permute-start.10 = (bf16[6,240,256]{2,1,0:T(8,128)(2,1)S(1)}, bf16[6,240,256]{2,1,0:T(8,128)(2,1)S(1)}, u32[]{:S(2)}, u32[]{:S(2)}) collective-permute-start(bf16[6,240,256]{2,1,0:T(8,128)(2,1)S(1)} %constant_dynamic-update-slice_fusion.refs_5_.refs_6_), channel_id=1, source_target_pairs={{0,4},{4,0},{8,12},{12,8},{16,20},{20,16},{24,28},{28,24},{32,36},... | collective-permute-start | bytes 2211848 | tf_op jit(solution)/shard_map/ppermute | solution.py:40
  49.1 9.3 %collective-permute-start.11 = (bf16[112,1280]{1,0:T(8,128)(2,1)S(1)}, bf16[112,1280]{1,0:T(8,128)(2,1)S(1)}, u32[]{:S(2)}, u32[]{:S(2)}) collective-permute-start(bf16[112,1280]{1,0:T(8,128)(2,1)S(1)} %get-tuple-element.71), channel_id=1, source_target_pairs={{0,1},{1,2},{2,3},{3,0},{4,5},{5,6},{6,7},{7,4},{8,9},{9,10},{10,1... | collective-permute-start | bytes 860168 | tf_op jit(solution)/shard_map/ppermute | solution.py:44
  49.4 10.4 %collective-permute-start.12 = (bf16[112,1280]{1,0:T(8,128)(2,1)S(1)}, bf16[112,1280]{1,0:T(8,128)(2,1)S(1)}, u32[]{:S(2)}, u32[]{:S(2)}) collective-permute-start(bf16[112,1280]{1,0:T(8,128)(2,1)S(1)} %get-tuple-element.72), channel_id=1, source_target_pairs={{0,3},{1,0},{2,1},{3,2},{4,7},{5,4},{6,5},{7,6},{8,11},{9,8},{10,9... | collective-permute-start | bytes 860168 | tf_op jit(solution)/shard_map/ppermute | solution.py:44
  60.0 16.2 %collective-permute-start.19 = (bf16[224,1280]{1,0:T(8,128)(2,1)S(1)}, bf16[224,1280]{1,0:T(8,128)(2,1)S(1)}, u32[]{:S(2)}, u32[]{:S(2)}) collective-permute-start(bf16[224,1280]{1,0:T(8,128)(2,1)S(1)} %pad_maximum_fusion.1), channel_id=1, source_target_pairs={{0,3},{1,0},{2,1},{3,2},{4,7},{5,4},{6,5},{7,6},{8,11},{9,8},{10,9... | collective-permute-start | bytes 1720328 | tf_op jit(solution)/shard_map/ppermute | solution.py:44
  60.4 6.1 %collective-permute-start.13 = (bf16[2,2,224,256]{3,2,1,0:T(8,128)(2,1)S(1)}, bf16[2,2,224,256]{3,2,1,0:T(8,128)(2,1)S(1)}, u32[]{:S(2)}, u32[]{:S(2)}) collective-permute-start(bf16[2,2,224,256]{3,2,1,0:T(8,128)(2,1)S(1)} %get-tuple-element.77), channel_id=1, source_target_pairs={{0,4},{4,0},{8,12},{12,8},{16,20},{20,16},{24,28},{28,24},{32,36},... | collective-permute-start | bytes 1376264 | tf_op jit(solution)/shard_map/ppermute | solution.py:40
  60.5 16.0 %collective-permute-start.18 = (bf16[224,1280]{1,0:T(8,128)(2,1)S(1)}, bf16[224,1280]{1,0:T(8,128)(2,1)S(1)}, u32[]{:S(2)}, u32[]{:S(2)}) collective-permute-start(bf16[224,1280]{1,0:T(8,128)(2,1)S(1)} %pad_maximum_fusion), channel_id=1, source_target_pairs={{0,1},{1,2},{2,3},{3,0},{4,5},{5,6},{6,7},{7,4},{8,9},{9,10},{10,1... | collective-permute-start | bytes 1720328 | tf_op jit(solution)/shard_map/ppermute | solution.py:44
  66.5 3.8 %collective-permute-start.16 = (bf16[1,2,224,256]{3,2,1,0:T(8,128)(2,1)S(1)}, bf16[1,2,224,256]{3,2,1,0:T(8,128)(2,1)S(1)}, u32[]{:S(2)}, u32[]{:S(2)}) collective-permute-start(bf16[1,2,224,256]{3,2,1,0:T(8,128)(2,1)S(1)} %get-tuple-element.85), channel_id=1, source_target_pairs={{0,4},{4,0},{8,12},{12,8},{16,20},{20,16},{24,28},{28,24},{32,36},... | collective-permute-start | bytes 688136 | tf_op jit(solution)/shard_map/ppermute | solution.py:40
  66.9 12.5 %collective-permute-start.14 = (bf16[2,224,256]{2,1,0:T(8,128)(2,1)S(1)}, bf16[2,224,256]{2,1,0:T(8,128)(2,1)S(1)}, u32[]{:S(2)}, u32[]{:S(2)}) collective-permute-start(bf16[2,224,256]{2,1,0:T(8,128)(2,1)S(1)} %get-tuple-element.101), channel_id=1, source_target_pairs={{0,24},{4,28},{8,0},{12,4},{16,8},{20,12},{24,16},{28,20},{32,56},... | collective-permute-start | bytes 688136 | tf_op jit(solution)/shard_map/ppermute | solution.py:40
  69.2 10.3 %collective-permute-start.15 = (bf16[2,224,256]{2,1,0:T(8,128)(2,1)S(1)}, bf16[2,224,256]{2,1,0:T(8,128)(2,1)S(1)}, u32[]{:S(2)}, u32[]{:S(2)}) collective-permute-start(bf16[2,224,256]{2,1,0:T(8,128)(2,1)S(1)} %get-tuple-element.100), channel_id=1, source_target_pairs={{0,16},{4,20},{8,24},{12,28},{16,0},{20,4},{24,8},{28,12},{32,48},... | collective-permute-start | bytes 688136 | tf_op jit(solution)/shard_map/ppermute | solution.py:40
  70.4 12.7 %collective-permute-start.17 = (bf16[2,224,256]{2,1,0:T(8,128)(2,1)S(1)}, bf16[2,224,256]{2,1,0:T(8,128)(2,1)S(1)}, u32[]{:S(2)}, u32[]{:S(2)}) collective-permute-start(bf16[2,224,256]{2,1,0:T(8,128)(2,1)S(1)} %fusion.12), channel_id=1, source_target_pairs={{0,8},{4,12},{8,16},{12,20},{16,24},{20,28},{24,0},{28,4},{32,40},... | collective-permute-start | bytes 688136 | tf_op jit(solution)/shard_map/ppermute | solution.py:40
  83.1 1.7 %collective-permute-start.20 = (bf16[3,224,256]{2,1,0:T(8,128)(2,1)S(1)}, bf16[3,224,256]{2,1,0:T(8,128)(2,1)S(1)}, u32[]{:S(2)}, u32[]{:S(2)}) collective-permute-start(bf16[3,224,256]{2,1,0:T(8,128)(2,1)S(1)} %get-tuple-element.94), channel_id=1, source_target_pairs={{0,4},{4,0},{8,12},{12,8},{16,20},{20,16},{24,28},{28,24},{32,36},... | collective-permute-start | bytes 1032200 | tf_op jit(solution)/shard_map/ppermute | solution.py:40
  85.0 7.1 %collective-permute-start.21 = (bf16[224,256]{1,0:T(8,128)(2,1)S(1)}, bf16[224,256]{1,0:T(8,128)(2,1)S(1)}, u32[]{:S(2)}, u32[]{:S(2)}) collective-permute-start(bf16[224,256]{1,0:T(8,128)(2,1)S(1)} %get-tuple-element.98), channel_id=1, source_target_pairs={{32,0},{36,4},{40,8},{44,12},{48,16},{52,20},{56,24},{60,28},{64,3... | collective-permute-start | bytes 344072 | tf_op jit(solution)/shard_map/ppermute | solution.py:40
  87.7 8.3 %collective-permute-start.22 = (bf16[224,256]{1,0:T(8,128)(2,1)S(1)}, bf16[224,256]{1,0:T(8,128)(2,1)S(1)}, u32[]{:S(2)}, u32[]{:S(2)}) collective-permute-start(bf16[224,256]{1,0:T(8,128)(2,1)S(1)} %get-tuple-element.99), channel_id=1, source_target_pairs={{64,0},{68,4},{72,8},{76,12},{80,16},{84,20},{88,24},{92,28},{96,3... | collective-permute-start | bytes 344072 | tf_op jit(solution)/shard_map/ppermute | solution.py:40
  (3 other events, 25.1 us)

commit v3 on v2

v3 whole, which is shorter than its diff:
```python
import math

import jax
import jax.numpy as jnp
from jax import lax
from jax.experimental import pallas as pl
from jax.experimental.pallas import tpu as pltpu
from jax.sharding import PartitionSpec as P

HD = 128
GROUP = 5
NX = 4
NY = 4
NZ = 4
TILE = 16
LOW = -1e30
HIGH = 1e30
F32 = jnp.float32
BF16 = jnp.bfloat16
NT = (((1,), (1,)), ((), ()))
TN = (((0,), (0,)), ((), ()))
NN = (((1,), (0,)), ((), ()))


def place(y, z, core):
    return ((y % NY) * NZ + (z % NZ)) * 2 + core


def shift(dy, dz, flip):
    pairs = []
    for y in range(NY):
        for z in range(NZ):
            for core in range(2):
                pairs.append((place(y, z, core), place(y + dy, z + dz, core ^ flip)))
    return pairs


def move(value, dy=0, dz=0, flip=0):
    return lax.ppermute(value, "dp", shift(dy, dz, flip))


def move_x(value, dx):
    return lax.ppermute(value, "mp", [(x, (x + dx) % NX) for x in range(NX)])


def dot(a, b, dims):
    return lax.dot_general(a, b, dims, preferred_element_type=F32)


def where_am_i():
    index = lax.axis_index("dp")
    return index // (2 * NZ), (index // 2) % NZ, index % 2


def stack_heads(source, target, rows):
    for head in range(GROUP):
        target[head * rows : (head + 1) * rows, :] = source[:, head * HD : (head + 1) * HD]
    target[GROUP * rows :, :] = jnp.zeros((target.shape[0] - GROUP * rows, HD), BF16)


def spread_heads(stacked, target, rows):
    for head in range(GROUP):
        target[:, head * HD : (head + 1) * HD] = stacked[head * rows : (head + 1) * rows, :]


def joined(parts):
    return parts[0] if len(parts) == 1 else jnp.concatenate(parts, axis=0)


def seen(tile, seg, rows):
    count = jnp.sum(jnp.where(tile.astype(F32) == seg, 1.0, 0.0))
    return rows - count.astype(jnp.int32)


def masks(refs, info, rows, width, own):
    at = lax.broadcasted_iota(jnp.int32, (rows, width), 0)
    result = []
    for index, (ref, slot) in enumerate(refs):
        if own and index == 0:
            segs = ref[slot, pl.ds(rows, TILE), :].astype(F32).T[:rows, :1]
            result.append((at.astype(F32) <= info[0:1, :]) & (segs == info[1:2, :]))
        else:
            result.append(at >= seen(ref[slot, pl.ds(rows, TILE), :], info[3:4, : 2 * HD], rows))
    return result


def attend(refs, visible, norm_of, q5, rows, factor, state, seen_rows):
    keys = joined([ref[slot, pl.ds(0, rows), pl.ds(0, HD)] for ref, slot in refs])
    values = joined([ref[slot, pl.ds(0, rows), pl.ds(HD, HD)] for ref, slot in refs])
    raw = dot(keys, q5, NT)
    scores = [jnp.where(see, raw[i * rows : (i + 1) * rows], LOW) for i, see in enumerate(visible)]
    peak = jnp.max(scores[0], axis=0, keepdims=True)
    for part in scores[1:]:
        peak = jnp.maximum(peak, jnp.max(part, axis=0, keepdims=True))
    peak = peak * factor
    if seen_rows is not None:
        peak = jnp.where(seen_rows, peak, LOW)
    top, total, acc = state
    new = peak if top is None else jnp.maximum(top, peak)
    norm = new if seen_rows is None else jnp.where(seen_rows, new, HIGH)
    weights = [jnp.exp2(part * factor - norm) for part in scores]
    added = sum(jnp.sum(w, axis=0, keepdims=True) for w in weights)
    out = dot(values, joined([w.astype(BF16) for w in weights]), TN)
    if top is None:
        return new, added, out
    alpha = jnp.exp2(top - new)
    return new, total * alpha + added, acc * alpha + out


def column_refs(column, other, core):
    return [(column, 0), (column, 1), (column, 2), (other, 1), (other, 2 - 2 * core)]


def side_refs(side, other, dz):
    return [(side, dz * 2), (other, dz * 2), (side, dz * 2 + 1), (other, dz * 2 + 1)]


def pack(seg, keys, values, own, line, sem):
    rows = keys.shape[0]
    copies = [
        pltpu.make_async_copy(seg, line, sem.at[0]),
        pltpu.make_async_copy(keys, own.at[pl.ds(0, rows), pl.ds(0, HD)], sem.at[1]),
        pltpu.make_async_copy(values, own.at[pl.ds(0, rows), pl.ds(HD, HD)], sem.at[2]),
    ]
    for copy in copies:
        copy.start()
    copies[0].wait()
    own[rows:, :] = jnp.zeros((TILE, 2 * HD), BF16)
    first = lax.broadcasted_iota(jnp.int32, (TILE, rows), 0) == 0
    own[rows:, :rows] = jnp.where(first, (line[...] + 1).astype(F32), 0.0).astype(BF16)
    copies[1].wait()
    copies[2].wait()


def describe_rows(tile, rows, info):
    width = info.shape[1]
    lane = lax.broadcasted_iota(jnp.int32, (2 * HD, width), 1)
    for head in range(1, GROUP + 1):
        lane = lane - jnp.where(lane >= rows, rows, 0)
    place_in = lax.broadcasted_iota(jnp.int32, (2 * HD, width), 0)

    def picked(at):
        return dot(tile, jnp.where(place_in == at, 1.0, 0.0).astype(BF16), NN)[:1, :]

    segs, first = picked(lane), picked(0)
    info[0:1, :] = lane[:1, :].astype(F32)
    info[1:2, :] = segs
    info[2:3, :] = jnp.where(segs == first, 1.0, 0.0)
    info[3:4, :] = first
    info[4:, :] = jnp.zeros((info.shape[0] - 4, width), F32)


def forward_column(rows, factor, q, column, other, top, total, acc, q5, info):
    stack_heads(q, q5, rows)
    describe_rows(column[0, pl.ds(rows, TILE), :], rows, info)
    _, _, core = where_am_i()
    width = info.shape[1]
    near = info[2:3, :] > 0.5
    refs = column_refs(column, other, core)
    visible = masks(refs, info, rows, width, True)
    state = attend(refs[:1], visible[:1], None, q5[...], rows, factor, (None, None, None), None)
    state = attend(refs[1:], visible[1:], None, q5[...], rows, factor, state, near)
    top[...], total[...], acc[...] = state


def forward_near(
    rows, factor, weight, info, q5, partial, g2_top, g2_end, side, top, total, acc,
    top_out, total_out, acc_out, g5, held, sem,
):
    x = lax.axis_index("mp")
    part = held.shape[1]
    column = pl.multiple_of(lax.rem(x + 2, NX) * part, 128)
    copy = pltpu.make_async_copy(weight.at[:, pl.ds(column, part)], held, sem)
    copy.start()
    near = info[2:3, :] > 0.5
    state = (top[...], total[...], acc[...])
    for group in (range(0, 3), range(3, 6)):
        refs = [(side, slot) for slot in group]
        visible = masks(refs, info, rows, info.shape[1], False)
        state = attend(refs, visible, None, q5[...], rows, factor, state, near)
    top_out[...], total_out[...], acc_out[...] = state
    g2 = jnp.concatenate([g2_top[...], g2_end[...]], axis=0)
    copy.wait()
    stack_heads((partial[...] + dot(g2, held[...], NT)).astype(BF16), g5, rows)


def forward_far(
    rows, factor, weight, info, q5, g5, other, top, total, acc,
    lse, delta, here, up, down, far_top, far_end, held, attn, sem,
):
    copy = pltpu.make_async_copy(weight, held, sem)
    copy.start()
    x = lax.axis_index("mp")
    near = info[2:3, :] > 0.5
    state = (top[...], total[...], acc[...])
    for group in (range(0, 3), range(3, 6)):
        refs = [(other, slot) for slot in group]
        visible = masks(refs, info, rows, info.shape[1], False)
        state = attend(refs, visible, None, q5[...], rows, factor, state, near)
    out_t = (state[2] / state[1]).astype(BF16)
    spread_heads(out_t.T, attn, rows)
    lse[...] = state[0] + jnp.log2(state[1])
    delta[...] = jnp.sum(out_t.astype(F32) * g5[...].T.astype(F32), axis=0, keepdims=True)
    copy.wait()
    part = here.shape[1]

    def features(dx):
        column = pl.multiple_of(lax.rem(x + dx, NX) * part, 128)
        return dot(attn[...], held[:, pl.ds(column, part)], NN).astype(BF16)

    far = features(2)
    far_top[...] = far[: rows // 2]
    far_end[...] = far[rows // 2 :]
    up[...] = features(1)
    down[...] = features(3)
    here[...] = features(0)


def grads_of(refs, visible, norm, delta, q5, g5, rows, factor, scale):
    keys = joined([ref[slot, pl.ds(0, rows), pl.ds(0, HD)] for ref, slot in refs])
    values = joined([ref[slot, pl.ds(0, rows), pl.ds(HD, HD)] for ref, slot in refs])
    raw = dot(keys, q5, NT)
    slope = dot(values, g5, NT)
    weights = []
    for i, see in enumerate(visible):
        part = raw[i * rows : (i + 1) * rows] * factor - norm
        weights.append(jnp.exp2(jnp.where(see, part, LOW)))
    weights = joined(weights)
    slope = (weights * (slope - delta)).astype(BF16)
    d_value = dot(weights.astype(BF16), g5, NN).astype(BF16)
    d_key = (dot(slope, q5, NN) * scale).astype(BF16)
    return d_key, d_value, dot(keys, slope, TN)


def backward_side(rows, factor, scale, parts, info, q5, g5, lse, delta, side, other, *rest):
    if len(parts) > 1:
        column, column_other, acc, stay, leave = rest
    else:
        before, acc, stay, leave = rest
    _, _, core = where_am_i()
    width = info.shape[1]
    norm = jnp.where(info[2:3, :] > 0.5, lse[...], HIGH)
    groups = []
    for index, dz in enumerate(parts):
        outs = ((stay, 2 * index), (leave, 2 * index), (stay, 2 * index + 1), (leave, 2 * index + 1))
        groups.append((side_refs(side, other, dz - 1), outs))
    total = None
    if len(parts) > 1:
        first = 2 * len(parts)
        groups.append((column_refs(column, column_other, core)[3:], ((leave, first + 1), (leave, first + 2 - 2 * core))))
        leave[first + 2 * core] = jnp.zeros(leave.shape[1:], BF16)
    else:
        total = before[...]
    for refs, outs in groups:
        visible = masks(refs, info, rows, width, False)
        d_key, d_value, d_query = grads_of(refs, visible, norm, delta[...], q5[...], g5[...], rows, factor, scale)
        for i, (out, slot) in enumerate(outs):
            out[slot, :, :HD] = d_key[i * rows : (i + 1) * rows]
            out[slot, :, HD:] = d_value[i * rows : (i + 1) * rows]
        total = d_query if total is None else total + d_query
    acc[...] = total


def backward_column(rows, factor, scale, info, q5, g5, lse, delta, column, acc, dq, stay):
    width = info.shape[1]
    norm = jnp.where(info[2:3, :] > 0.5, lse[...], HIGH)
    refs = [(column, 0), (column, 1), (column, 2)]
    visible = masks(refs, info, rows, width, True)
    total = acc[...]
    for part, limit in ((slice(0, 1), lse[...]), (slice(1, 3), norm)):
        d_key, d_value, d_query = grads_of(
            refs[part], visible[part], limit, delta[...], q5[...], g5[...], rows, factor, scale
        )
        for i, slot in enumerate(range(3)[part]):
            stay[slot, :, :HD] = d_key[i * rows : (i + 1) * rows]
            stay[slot, :, HD:] = d_value[i * rows : (i + 1) * rows]
        total = total + d_query
    spread_heads((total * scale).astype(BF16).T, dq, rows)


def grad_heads(g0, g1, g3, weight, partial, held, weights, sem):
    x = lax.axis_index("mp")
    part = held.shape[2]
    order = (0, 1, 3)
    loads, copies = [], []
    for index, (back, piece) in enumerate(zip(order, (g0, g1, g3))):
        column = pl.multiple_of(lax.rem(x + NX - back, NX) * part, 128)
        source = weight.at[:, pl.ds(column, part)]
        loads.append(pltpu.make_async_copy(source, weights.at[index], sem.at[2 * index]))
        copies.append(pltpu.make_async_copy(piece, held.at[index], sem.at[2 * index + 1]))
        loads[-1].start()
        copies[-1].start()
    total = None
    for index in range(len(order)):
        loads[index].wait()
        copies[index].wait()
        term = dot(held[index], weights[index], NT)
        total = term if total is None else total + term
    partial[...] = total


def join_features(here, up, down, out):
    out[...] = (here[...].astype(F32) + up[...].astype(F32) + down[...].astype(F32)).astype(BF16)


def add_up(*terms):
    return sum(t.astype(F32) for t in terms)


def per_device(queries, keys, values, seg_ids, out_weight, grad_out):
    rows = queries.shape[0]
    scale = 1.0 / math.sqrt(HD)
    factor = scale * math.log2(math.e)
    width = -(-GROUP * rows // 128) * 128
    y, z, _ = where_am_i()
    x = lax.axis_index("mp")
    vmem = pl.BlockSpec(memory_space=pltpu.VMEM)

    def shape(*dims, dtype=BF16):
        return jax.ShapeDtypeStruct(dims, dtype)

    anywhere = pl.BlockSpec(memory_space=pl.ANY)

    fixed = pl.BlockSpec(memory_space=pltpu.HBM)

    def call(body, outs, micros, *operands, loose=0, pinned=0, scratch=(), mib=24):
        return pl.pallas_call(
            body,
            out_shape=outs,
            in_specs=[anywhere] * loose
            + [fixed] * pinned
            + [vmem] * (len(operands) - loose - pinned),
            out_specs=jax.tree.map(lambda _: vmem, outs),
            scratch_shapes=scratch,
            cost_estimate=pl.CostEstimate(flops=micros * 1_153_000_000, bytes_accessed=0, transcendentals=0),
            compiler_params=pltpu.CompilerParams(vmem_limit_bytes=mib * 1024 * 1024),
        )(*operands)

    line = shape(1, width, dtype=F32)
    square = shape(HD, width, dtype=F32)
    stacked = shape(width, HD)
    half = rows // 2

    own = call(
        pack, shape(rows + TILE, 2 * HD), 1, seg_ids.reshape(1, rows), keys, values, pinned=3, mib=60,
        scratch=[pltpu.VMEM((1, rows), jnp.int32), pltpu.SemaphoreType.DMA((3,))],
    )
    own, grad_out = lax.optimization_barrier((own, grad_out))
    y1, y2 = move(own, dy=1), move(own, dy=2)
    g1, g3 = move_x(grad_out, 1), move_x(grad_out, 3)
    y1, y2 = lax.optimization_barrier((y1, y2))
    y1, y2 = jnp.where(y >= 1, y1, 0), jnp.where(y >= 2, y2, 0)

    column = jnp.stack([own, y1, y2])
    column_other = move(column, flip=1)
    sides = {dz: jnp.stack([y1, jnp.where(z + dz < NZ, own, y2)]) for dz in (2, 1, 3)}
    sides[3], column_other = lax.optimization_barrier((sides[3], column_other))
    sides = [move(sides[dz], dz=dz) for dz in (1, 2, 3)]
    g2_top, g2_end = move_x(g1[:half], 1), move_x(g3[half:], 3)
    top, total, acc, q5, info = call(
        lambda *refs: forward_column(rows, factor, *refs),
        (line, line, square, stacked, shape(8, width, dtype=F32)), 1, queries, column, column_other,
    )
    part = grad_out.shape[1]
    partial = call(
        grad_heads, shape(rows, GROUP * HD, dtype=F32), 3, grad_out, g1, g3, out_weight, loose=3, pinned=1,
        scratch=[
            pltpu.VMEM((NX - 1, rows, part), BF16),
            pltpu.VMEM((NX - 1, out_weight.shape[0], part), BF16),
            pltpu.SemaphoreType.DMA((2 * (NX - 1),)),
        ],
    )
    *sides, g2_top, g2_end, top, partial = lax.optimization_barrier((*sides, g2_top, g2_end, top, partial))

    side = jnp.concatenate(sides)
    side_other = move(side, flip=1)
    top, total, acc, g5, side_other = lax.optimization_barrier(
        (
            *call(
                lambda *refs: forward_near(rows, factor, *refs),
                (line, line, square, stacked), 4,
                out_weight, info, q5, partial, g2_top, g2_end, side, top, total, acc, pinned=1,
                scratch=[pltpu.VMEM((out_weight.shape[0], part), BF16), pltpu.SemaphoreType.DMA],
            ),
            side_other,
        )
    )
    whole, halved = shape(rows, part), shape(half, part)
    lse, delta, here, up, down, *far = call(
        lambda *refs: forward_far(rows, factor, *refs),
        (line, line, whole, whole, whole, halved, halved), 6,
        out_weight, info, q5, g5, side_other, top, total, acc, pinned=1, mib=30,
        scratch=[
            pltpu.VMEM(out_weight.shape, BF16),
            pltpu.VMEM((rows, GROUP * HD), BF16),
            pltpu.SemaphoreType.DMA,
        ],
    )
    early = (move_x(far[0], 1), move_x(far[1], 3))

    def side_grads(parts, kept, sent, micros, *more):
        return call(
            lambda *refs: backward_side(rows, factor, scale, parts, *refs),
            (square, shape(kept, rows, 2 * HD), shape(sent, rows, 2 * HD)), micros,
            info, q5, g5, lse, delta, side, side_other, *more,
        )

    acc, stay, leave, *early = lax.optimization_barrier(
        (*side_grads((2, 1), 4, 7, 7, column, column_other), *early)
    )
    up = jnp.concatenate([add_up(up[:half], early[0]).astype(BF16), up[half:]], axis=0)
    down = jnp.concatenate([down[:half], add_up(down[half:], early[1]).astype(BF16)], axis=0)
    other = move(leave, flip=1)
    acc, stay_last, leave_last, other = lax.optimization_barrier((*side_grads((3,), 2, 2, 3, acc), other))
    other_last = move(leave_last, flip=1)
    mixed = add_up(stay, other[:4]).astype(BF16)
    returned = {2: move(mixed[:2], dz=-2), 1: move(mixed[2:], dz=-1)}
    returned[3] = move(add_up(stay_last, other_last).astype(BF16), dz=-3)
    up, down = move_x(up, 1), move_x(down, 3)
    grad_query, stay, returned[1], returned[2], returned[3], up, down = lax.optimization_barrier(
        (
            *call(
                lambda *refs: backward_column(rows, factor, scale, *refs),
                (shape(rows, GROUP * HD), shape(3, rows, 2 * HD)), 3,
                info, q5, g5, lse, delta, column, acc,
            ),
            returned[1], returned[2], returned[3], up, down,
        )
    )
    projected = add_up(here, up, down).astype(BF16)
    mixed = add_up(stay, other[4:])
    first, second, third = mixed[0], mixed[1], mixed[2]
    for dz in range(1, NZ):
        far, near = returned[dz][0].astype(F32), returned[dz][1].astype(F32)
        second = second + far
        first = first + jnp.where(z + dz < NZ, near, 0.0)
        third = third + jnp.where(z + dz < NZ, 0.0, near)
    second, third = second.astype(BF16), third.astype(BF16)
    grads = add_up(first, move(second, dy=-1), move(third, dy=-2)).astype(BF16)
    return (projected, grad_query, grads[:, :HD], grads[:, HD:])


def solution(mesh):
    return jax.shard_map(
        per_device,
        mesh=mesh,
        in_specs=(
            P("dp", "mp"),
            P("dp", "mp"),
            P("dp", "mp"),
            P("dp"),
            P("mp", None),
            P("dp", "mp"),
        ),
        out_specs=(P("dp", "mp"), P("dp", "mp"), P("dp", "mp"), P("dp", "mp")),
        check_vma=False,
    )
```

time: 97.1 us -> 85.1 us (0.88)
  starting transfers between devices: 30.6 us -> 25.8 us
  other arithmetic: 6.68 us -> 2.83 us
  waiting for transfers between devices: 26.5 us -> 24.1 us
  local copies, waits for them, and re-layouts: 2.42 us -> 0.84 us
    ppermute x15 -> x14, starting transfers between devices: 20.9 us -> 16.2 us  [move(): return lax.ppermute(value, 'dp', shift(dy, dz, flip))]
    ppermute x15 -> x14, waiting for transfers between devices: 19.5 us -> 17.7 us  [move(): return lax.ppermute(value, 'dp', shift(dy, dz, flip))]
    slice x2 -> x1, local copies, waits for them, and re-layouts: 1.37 us -> 0.03 us  [per_device(): returned = {2: move(mixed[:2], dz=-2), 1: move(mixed[2:], dz=-1)}]
    another operation x1 -> x0, other arithmetic: 1.33 us -> none  [row_info(): info = jnp.stack([position, start, near] + [jnp.zeros(rows, F32)] * 5)]
    pallas_call x6 -> x8, Pallas kernels: 29 us -> 29.5 us  [call(): pl.pallas_call(body, out_shape=outs, in_specs=[anywhere] * loose + [fixed...]
  transfers between devices with their start and end apart: 23 -> 22, of which waited for: 11 -> 13; matrix products, arithmetic and copies ran while one was open for 7% -> 3% of each run, Pallas kernels for 22% -> 27%
where the time goes in v3:
time: 85.1 us; the launch traced here: 84.1 us
  Pallas kernels  29.5 us (35%)
  starting transfers between devices  25.8 us (30%)
  waiting for transfers between devices  24.1 us (28%)
  other arithmetic  2.83 us (3%)
  between operations  0.91 us (1%)
    pallas_call x8, Pallas kernels, call(): pl.pallas_call(body, out_shape=outs, in_specs=[anywhere] * loose + [fixed...  29.5 us
    ppermute x14, waiting for transfers between devices, move(): return lax.ppermute(value, 'dp', shift(dy, dz, flip))  17.7 us
    ppermute x14, starting transfers between devices, move(): return lax.ppermute(value, 'dp', shift(dy, dz, flip))  16.2 us
    ppermute x8, starting transfers between devices, move_x(): return lax.ppermute(value, 'mp', [(x, (x + dx) % NX) for x in range(NX)])  9.66 us
    ppermute x8, waiting for transfers between devices, move_x(): return lax.ppermute(value, 'mp', [(x, (x + dx) % NX) for x in range(NX)])  6.43 us
  transfers between devices with their start and end apart: 22, of which 13 were waited for; matrix products, arithmetic and copies ran while one was open for 3% of the time, Pallas kernels for 27%

profile of v3, /device:TPU:14, one launch (start us, length us, event | category | flops | bytes accessed | tf_op | source)
XLA Modules:
  0.0 84.1 jit_solution(15504115368779493428)
XLA Ops:
  0.6 1.6 %shard_map.93 = bf16[240,256]{1,0:T(8,128)(2,1)} custom-call(s32[1,224]{1,0:T(1,128)} %bitcast.25, bf16[224,128]{1,0:T(8,128)(2,1)} %keys.1, bf16[224,128]{1,0:T(8,128)(2,1)} %values.1), custom_call_target="tpu_custom_call" | custom-call | flops 1152999936 | tf_op jit(solution)/shard_map/pallas_call | solution.py:327
  2.3 1.6 %collective-permute-start = (bf16[240,256]{1,0:T(8,128)(2,1)}, bf16[240,256]{1,0:T(8,128)(2,1)S(1)}, u32[]{:S(2)}, u32[]{:S(2)}) collective-permute-start(bf16[240,256]{1,0:T(8,128)(2,1)} %shard_map.93), channel_id=1, source_target_pairs={{0,32},{4,36},{8,40},{12,44},{16,48},{20,52},{24,56},{28,60},{32,6... | collective-permute-start | bytes 368648 | tf_op jit(solution)/shard_map/ppermute | solution.py:39
  5.2 1.6 %collective-permute-start.8 = (bf16[224,1280]{1,0:T(8,128)(2,1)S(1)}, bf16[224,1280]{1,0:T(8,128)(2,1)S(1)}, u32[]{:S(2)}, u32[]{:S(2)}) collective-permute-start(bf16[224,1280]{1,0:T(8,128)(2,1)S(1)} %copy-done.1), channel_id=1, source_target_pairs={{0,3},{1,0},{2,1},{3,2},{4,7},{5,4},{6,5},{7,6},{8,11},{9,8},{10,9... | collective-permute-start | bytes 1720328 | tf_op jit(solution)/shard_map/ppermute | solution.py:43
  7.6 2.9 %collective-permute-done.1 = bf16[240,256]{1,0:T(8,128)(2,1)S(1)} collective-permute-done((bf16[240,256]{1,0:T(8,128)(2,1)}, bf16[240,256]{1,0:T(8,128)(2,1)S(1)}, u32[]{:S(2)}, u32[]{:S(2)}) %collective-permute-start.1) | collective-permute-done | bytes 122912 | tf_op jit(solution)/shard_map/ppermute | solution.py:39
  11.7 2.0 %collective-permute-start.3 = (bf16[2,240,256]{2,1,0:T(8,128)(2,1)S(1)}, bf16[2,240,256]{2,1,0:T(8,128)(2,1)S(1)}, u32[]{:S(2)}, u32[]{:S(2)}) collective-permute-start(bf16[2,240,256]{2,1,0:T(8,128)(2,1)S(1)} %get-tuple-element.128), channel_id=1, source_target_pairs={{0,8},{4,12},{8,16},{12,20},{16,24},{20,28},{24,0},{28,4},{32,40},... | collective-permute-start | bytes 737288 | tf_op jit(solution)/shard_map/ppermute | solution.py:39
  13.7 3.6 %collective-permute-start.4 = (bf16[2,240,256]{2,1,0:T(8,128)(2,1)S(1)}, bf16[2,240,256]{2,1,0:T(8,128)(2,1)S(1)}, u32[]{:S(2)}, u32[]{:S(2)}) collective-permute-start(bf16[2,240,256]{2,1,0:T(8,128)(2,1)S(1)} %get-tuple-element.127), channel_id=1, source_target_pairs={{0,16},{4,20},{8,24},{12,28},{16,0},{20,4},{24,8},{28,12},{32,48},... | collective-permute-start | bytes 737288 | tf_op jit(solution)/shard_map/ppermute | solution.py:39
  18.3 2.7 %shard_map.94 = (f32[1,1152]{1,0:T(1,128)S(1)}, f32[1,1152]{1,0:T(1,128)S(1)}, f32[128,1152]{1,0:T(8,128)S(1)}, bf16[1152,128]{1,0:T(8,128)(2,1)S(1)}, f32[8,1152]{1,0:T(8,128)S(1)}) custom-call(bf16[224,640]{1,0:T(8,128)(2,1)S(1)} %copy-done.2, bf16[3,240,256]{2,1,0:T(8,128)(2,1)S(1)} %pad_maximum_fusion.2.refs_1_.refs_7_.refs_5_, ...), custom_call_target="tpu_custom_call" | custom-call | flops 1152999936 | tf_op jit(solution)/shard_map/pallas_call | solution.py:327
  21.6 1.6 %collective-permute-start.9 = (bf16[112,1280]{1,0:T(8,128)(2,1)S(1)}, bf16[112,1280]{1,0:T(8,128)(2,1)S(1)}, u32[]{:S(2)}, u32[]{:S(2)}) collective-permute-start(bf16[112,1280]{1,0:T(8,128)(2,1)S(1)} %slice.85), channel_id=1, source_target_pairs={{0,3},{1,0},{2,1},{3,2},{4,7},{5,4},{6,5},{7,6},{8,11},{9,8},{10,9... | collective-permute-start | bytes 860168 | tf_op jit(solution)/shard_map/ppermute | solution.py:43
  23.3 3.1 %shard_map.95.refs_3_ = f32[224,640]{1,0:T(8,128)S(1)} custom-call(bf16[224,1280]{1,0:T(8,128)(2,1)S(1)} %copy-done.1, bf16[224,1280]{1,0:T(8,128)(2,1)S(1)} %collective-permute-done.6.g1, bf16[224,1280]{1,0:T(8,128)(2,1)S(1)} %collective-permute-done.8.g3, bf16[640,5120]{1,0:T(8,128)(2,1)S(1)} %copy-done), custom_call_target="tpu_custom_call" | custom-call | flops 3459000064 | tf_op jit(solution)/shard_map/pallas_call | solution.py:327
  26.4 2.4 %collective-permute-done.4 = bf16[2,240,256]{2,1,0:T(8,128)(2,1)S(1)} collective-permute-done((bf16[2,240,256]{2,1,0:T(8,128)(2,1)S(1)}, bf16[2,240,256]{2,1,0:T(8,128)(2,1)S(1)}, u32[]{:S(2)}, u32[]{:S(2)}) %collective-permute-start.4) | collective-permute-done | bytes 245792 | tf_op jit(solution)/shard_map/ppermute | solution.py:39
  31.4 3.8 %shard_map.96 = (f32[1,1152]{1,0:T(1,128)S(1)}, f32[1,1152]{1,0:T(1,128)S(1)}, f32[128,1152]{1,0:T(8,128)S(1)}, bf16[1152,128]{1,0:T(8,128)(2,1)S(1)}) custom-call(bf16[640,5120]{1,0:T(8,128)(2,1)S(1)} %copy-done, f32[8,1152]{1,0:T(8,128)S(1)} %get-tuple-element.66.refs_1_.refs_0_, bf16[1152,128]{1,0:T(8,128)(2,1)S(1)} %get-tuple-element.67.refs_2_.refs_1_, ...), custom_call_target="tpu_custom_call" | custom-call | flops 4611999744 | tf_op jit(solution)/shard_map/pallas_call | solution.py:327
  35.2 5.4 %shard_map.97 = (f32[1,1152]{1,0:T(1,128)S(1)}, f32[1,1152]{1,0:T(1,128)S(1)}, bf16[224,1280]{1,0:T(8,128)(2,1)S(1)}, bf16[224,1280]{1,0:T(8,128)(2,1)S(1)}, bf1...) custom-call(bf16[640,5120]{1,0:T(8,128)(2,1)S(1)} %copy-done, ...), custom_call_target="tpu_custom_call" | custom-call | flops 6918000128 | tf_op jit(solution)/shard_map/pallas_call | solution.py:327
  41.0 1.7 %collective-permute-start.12 = (bf16[112,1280]{1,0:T(8,128)(2,1)S(1)}, bf16[112,1280]{1,0:T(8,128)(2,1)S(1)}, u32[]{:S(2)}, u32[]{:S(2)}) collective-permute-start(bf16[112,1280]{1,0:T(8,128)(2,1)S(1)} %get-tuple-element.96), channel_id=1, source_target_pairs={{0,3},{1,0},{2,1},{3,2},{4,7},{5,4},{6,5},{7,6},{8,11},{9,8},{10,9... | collective-permute-start | bytes 860168 | tf_op jit(solution)/shard_map/ppermute | solution.py:43
  42.7 6.9 %shard_map.98 = (f32[128,1152]{1,0:T(8,128)S(1)}, bf16[4,224,256]{2,1,0:T(8,128)(2,1)S(1)}, bf16[7,224,256]{2,1,0:T(8,128)(2,1)S(1)}) custom-call(f32[8,1152]{1,0:T(8,128)S(1)} %get-tuple-element.66.refs_1_.refs_0_, bf16[1152,128]{1,0:T(8,128)(2,1)S(1)} %get-tuple-element.67.refs_2_.refs_1_, bf16[1152,128]{1,0:T(8,128)(2,1)S(1)} %get-tuple-element.84.refs_3_.refs_2_, ...), custom_call_target="tpu_custom_call" | custom-call | flops 8071000064 | tf_op jit(solution)/shard_map/pallas_call | solution.py:327
  52.0 3.1 %collective-permute-start.18 = (bf16[224,1280]{1,0:T(8,128)(2,1)S(1)}, bf16[224,1280]{1,0:T(8,128)(2,1)S(1)}, u32[]{:S(2)}, u32[]{:S(2)}) collective-permute-start(bf16[224,1280]{1,0:T(8,128)(2,1)S(1)} %pad_maximum_fusion), channel_id=1, source_target_pairs={{0,1},{1,2},{2,3},{3,0},{4,5},{5,6},{6,7},{7,4},{8,9},{9,10},{10,1... | collective-permute-start | bytes 1720328 | tf_op jit(solution)/shard_map/ppermute | solution.py:43
  55.1 2.9 %shard_map.99 = (f32[128,1152]{1,0:T(8,128)S(1)}, bf16[2,224,256]{2,1,0:T(8,128)(2,1)S(1)}, bf16[2,224,256]{2,1,0:T(8,128)(2,1)S(1)}) custom-call(f32[8,1152]{1,0:T(8,128)S(1)} %get-tuple-element.66.refs_1_.refs_0_, bf16[1152,128]{1,0:T(8,128)(2,1)S(1)} %get-tuple-element.67.refs_2_.refs_1_, bf16[1152,128]{1,0:T(8,128)(2,1)S(1)} %get-tuple-element.84.refs_3_.refs_2_, ...), custom_call_target="tpu_custom_call" | custom-call | flops 3459000064 | tf_op jit(solution)/shard_map/pallas_call | solution.py:327
  58.4 2.3 %collective-permute-start.14 = (bf16[2,224,256]{2,1,0:T(8,128)(2,1)S(1)}, bf16[2,224,256]{2,1,0:T(8,128)(2,1)S(1)}, u32[]{:S(2)}, u32[]{:S(2)}) collective-permute-start(bf16[2,224,256]{2,1,0:T(8,128)(2,1)S(1)} %get-tuple-element.123), channel_id=1, source_target_pairs={{0,24},{4,28},{8,0},{12,4},{16,8},{20,12},{24,16},{28,20},{32,56},... | collective-permute-start | bytes 688136 | tf_op jit(solution)/shard_map/ppermute | solution.py:39
  62.3 3.1 %shard_map.100 = (bf16[224,640]{1,0:T(8,128)(2,1)}, bf16[3,224,256]{2,1,0:T(8,128)(2,1)S(1)}) custom-call(f32[8,1152]{1,0:T(8,128)S(1)} %get-tuple-element.66.refs_1_.refs_0_, bf16[1152,128]{1,0:T(8,128)(2,1)S(1)} %get-tuple-element.67.refs_2_.refs_1_, bf16[1152,128]{1,0:T(8,128)(2,1)S(1)} %get-tuple-element.84.refs_3_.refs_2_, ...), custom_call_target="tpu_custom_call" | custom-call | flops 3459000064 | tf_op jit(solution)/shard_map/pallas_call | solution.py:327
  65.5 1.9 %collective-permute-done.19 = bf16[224,1280]{1,0:T(8,128)(2,1)S(1)} collective-permute-done((bf16[224,1280]{1,0:T(8,128)(2,1)S(1)}, bf16[224,1280]{1,0:T(8,128)(2,1)S(1)}, u32[]{:S(2)}, u32[]{:S(2)}) %collective-permute-start.19) | collective-permute-done | bytes 573472 | tf_op jit(solution)/shard_map/ppermute | solution.py:43
  68.0 3.0 %collective-permute-done.14 = bf16[2,224,256]{2,1,0:T(8,128)(2,1)S(1)} collective-permute-done((bf16[2,224,256]{2,1,0:T(8,128)(2,1)S(1)}, bf16[2,224,256]{2,1,0:T(8,128)(2,1)S(1)}, u32[]{:S(2)}, u32[]{:S(2)}) %collective-permute-start.14) | collective-permute-done | bytes 229408 | tf_op jit(solution)/shard_map/ppermute | solution.py:39
  70.9 3.7 %collective-permute-done.17 = bf16[2,224,256]{2,1,0:T(8,128)(2,1)S(1)} collective-permute-done((bf16[2,224,256]{2,1,0:T(8,128)(2,1)S(1)}, bf16[2,224,256]{2,1,0:T(8,128)(2,1)S(1)}, u32[]{:S(2)}, u32[]{:S(2)}) %collective-permute-start.17) | collective-permute-done | bytes 229408 | tf_op jit(solution)/shard_map/ppermute | solution.py:39
  74.8 2.2 %collective-permute-start.20 = (bf16[224,256]{1,0:T(8,128)(2,1)S(1)}, bf16[224,256]{1,0:T(8,128)(2,1)S(1)}, u32[]{:S(2)}, u32[]{:S(2)}) collective-permute-start(bf16[224,256]{1,0:T(8,128)(2,1)S(1)} %get-tuple-element.120), channel_id=1, source_target_pairs={{0,96},{4,100},{8,104},{12,108},{16,112},{20,116},{24,120},{28,124... | collective-permute-start | bytes 344072 | tf_op jit(solution)/shard_map/ppermute | solution.py:39
  78.3 2.2 %collective-permute-done.20 = bf16[224,256]{1,0:T(8,128)(2,1)S(1)} collective-permute-done((bf16[224,256]{1,0:T(8,128)(2,1)S(1)}, bf16[224,256]{1,0:T(8,128)(2,1)S(1)}, u32[]{:S(2)}, u32[]{:S(2)}) %collective-permute-start.20) | collective-permute-done | bytes 114720 | tf_op jit(solution)/shard_map/ppermute | solution.py:39
  80.5 2.8 %collective-permute-done.21 = bf16[224,256]{1,0:T(8,128)(2,1)S(1)} collective-permute-done((bf16[224,256]{1,0:T(8,128)(2,1)S(1)}, bf16[224,256]{1,0:T(8,128)(2,1)S(1)}, u32[]{:S(2)}, u32[]{:S(2)}) %collective-permute-start.21) | collective-permute-done | bytes 114720 | tf_op jit(solution)/shard_map/ppermute | solution.py:39
  (59 shorter events, 15.0 us)
Async XLA Ops:
  2.2 9.2 %copy-start.3 = (bf16[240,256]{1,0:T(8,128)(2,1)S(1)}, bf16[240,256]{1,0:T(8,128)(2,1)}, u32[]{:S(2)}) copy-start(bf16[240,256]{1,0:T(8,128)(2,1)} %shard_map.93) | copy-start | bytes 368644
  2.3 5.3 %collective-permute-start = (bf16[240,256]{1,0:T(8,128)(2,1)}, bf16[240,256]{1,0:T(8,128)(2,1)S(1)}, u32[]{:S(2)}, u32[]{:S(2)}) collective-permute-start(bf16[240,256]{1,0:T(8,128)(2,1)} %shard_map.93), channel_id=1, source_target_pairs={{0,32},{4,36},{8,40},{12,44},{16,48},{20,52},{24,56},{28,60},{32,6... | collective-permute-start | bytes 368648 | tf_op jit(solution)/shard_map/ppermute | solution.py:39
  3.9 6.6 %collective-permute-start.1 = (bf16[240,256]{1,0:T(8,128)(2,1)}, bf16[240,256]{1,0:T(8,128)(2,1)S(1)}, u32[]{:S(2)}, u32[]{:S(2)}) collective-permute-start(bf16[240,256]{1,0:T(8,128)(2,1)} %shard_map.93), channel_id=1, source_target_pairs={{0,64},{4,68},{8,72},{12,76},{16,80},{20,84},{24,88},{28,92},{32,9... | collective-permute-start | bytes 368648 | tf_op jit(solution)/shard_map/ppermute | solution.py:39
  4.8 16.2 %collective-permute-start.6 = (bf16[224,1280]{1,0:T(8,128)(2,1)S(1)}, bf16[224,1280]{1,0:T(8,128)(2,1)S(1)}, u32[]{:S(2)}, u32[]{:S(2)}) collective-permute-start(bf16[224,1280]{1,0:T(8,128)(2,1)S(1)} %copy-done.1), channel_id=1, source_target_pairs={{0,1},{1,2},{2,3},{3,0},{4,5},{5,6},{6,7},{7,4},{8,9},{9,10},{10,1... | collective-permute-start | bytes 1720328 | tf_op jit(solution)/shard_map/ppermute | solution.py:43
  5.2 16.4 %collective-permute-start.8 = (bf16[224,1280]{1,0:T(8,128)(2,1)S(1)}, bf16[224,1280]{1,0:T(8,128)(2,1)S(1)}, u32[]{:S(2)}, u32[]{:S(2)}) collective-permute-start(bf16[224,1280]{1,0:T(8,128)(2,1)S(1)} %copy-done.1), channel_id=1, source_target_pairs={{0,3},{1,0},{2,1},{3,2},{4,7},{5,4},{6,5},{7,6},{8,11},{9,8},{10,9... | collective-permute-start | bytes 1720328 | tf_op jit(solution)/shard_map/ppermute | solution.py:43
  11.5 5.7 %collective-permute-start.2 = (bf16[3,240,256]{2,1,0:T(8,128)(2,1)S(1)}, bf16[3,240,256]{2,1,0:T(8,128)(2,1)S(1)}, u32[]{:S(2)}, u32[]{:S(2)}) collective-permute-start(bf16[3,240,256]{2,1,0:T(8,128)(2,1)S(1)} %pad_maximum_fusion.2.refs_1_.refs_7_.refs_5_), channel_id=1, source_target_pairs={{0,4},{4,0},{8,12},{12,8},{16,20},{20,16},{24,28},{28,24},{32,36},... | collective-permute-start | bytes 1105928 | tf_op jit(solution)/shard_map/ppermute | solution.py:39
  11.6 11.6 %copy-start = (bf16[640,5120]{1,0:T(8,128)(2,1)S(1)}, bf16[640,5120]{1,0:T(8,128)(2,1)}, u32[]{:S(2)}) copy-start(bf16[640,5120]{1,0:T(8,128)(2,1)} %refs_0_.5) | copy-start | bytes 19660804
  11.7 14.7 %collective-permute-start.3 = (bf16[2,240,256]{2,1,0:T(8,128)(2,1)S(1)}, bf16[2,240,256]{2,1,0:T(8,128)(2,1)S(1)}, u32[]{:S(2)}, u32[]{:S(2)}) collective-permute-start(bf16[2,240,256]{2,1,0:T(8,128)(2,1)S(1)} %get-tuple-element.128), channel_id=1, source_target_pairs={{0,8},{4,12},{8,16},{12,20},{16,24},{20,28},{24,0},{28,4},{32,40},... | collective-permute-start | bytes 737288 | tf_op jit(solution)/shard_map/ppermute | solution.py:39
  13.7 15.2 %collective-permute-start.4 = (bf16[2,240,256]{2,1,0:T(8,128)(2,1)S(1)}, bf16[2,240,256]{2,1,0:T(8,128)(2,1)S(1)}, u32[]{:S(2)}, u32[]{:S(2)}) collective-permute-start(bf16[2,240,256]{2,1,0:T(8,128)(2,1)S(1)} %get-tuple-element.127), channel_id=1, source_target_pairs={{0,16},{4,20},{8,24},{12,28},{16,0},{20,4},{24,8},{28,12},{32,48},... | collective-permute-start | bytes 737288 | tf_op jit(solution)/shard_map/ppermute | solution.py:39
  17.3 11.6 %collective-permute-start.5 = (bf16[2,240,256]{2,1,0:T(8,128)(2,1)S(1)}, bf16[2,240,256]{2,1,0:T(8,128)(2,1)S(1)}, u32[]{:S(2)}, u32[]{:S(2)}) collective-permute-start(bf16[2,240,256]{2,1,0:T(8,128)(2,1)S(1)} %get-tuple-element.68), channel_id=1, source_target_pairs={{0,24},{4,28},{8,0},{12,4},{16,8},{20,12},{24,16},{28,20},{32,56},... | collective-permute-start | bytes 737288 | tf_op jit(solution)/shard_map/ppermute | solution.py:39
  21.1 8.4 %collective-permute-start.7 = (bf16[112,1280]{1,0:T(8,128)(2,1)S(1)}, bf16[112,1280]{1,0:T(8,128)(2,1)S(1)}, u32[]{:S(2)}, u32[]{:S(2)}) collective-permute-start(bf16[112,1280]{1,0:T(8,128)(2,1)S(1)} %slice.84), channel_id=1, source_target_pairs={{0,1},{1,2},{2,3},{3,0},{4,5},{5,6},{6,7},{7,4},{8,9},{9,10},{10,1... | collective-permute-start | bytes 860168 | tf_op jit(solution)/shard_map/ppermute | solution.py:43
  21.6 9.4 %collective-permute-start.9 = (bf16[112,1280]{1,0:T(8,128)(2,1)S(1)}, bf16[112,1280]{1,0:T(8,128)(2,1)S(1)}, u32[]{:S(2)}, u32[]{:S(2)}) collective-permute-start(bf16[112,1280]{1,0:T(8,128)(2,1)S(1)} %slice.85), channel_id=1, source_target_pairs={{0,3},{1,0},{2,1},{3,2},{4,7},{5,4},{6,5},{7,6},{8,11},{9,8},{10,9... | collective-permute-start | bytes 860168 | tf_op jit(solution)/shard_map/ppermute | solution.py:43
  31.1 4.1 %collective-permute-start.10 = (bf16[6,240,256]{2,1,0:T(8,128)(2,1)S(1)}, bf16[6,240,256]{2,1,0:T(8,128)(2,1)S(1)}, u32[]{:S(2)}, u32[]{:S(2)}) collective-permute-start(bf16[6,240,256]{2,1,0:T(8,128)(2,1)S(1)} %constant_dynamic-update-slice_fusion.refs_6_.refs_5_), channel_id=1, source_target_pairs={{0,4},{4,0},{8,12},{12,8},{16,20},{20,16},{24,28},{28,24},{32,36},... | collective-permute-start | bytes 2211848 | tf_op jit(solution)/shard_map/ppermute | solution.py:39
  40.6 9.3 %collective-permute-start.11 = (bf16[112,1280]{1,0:T(8,128)(2,1)S(1)}, bf16[112,1280]{1,0:T(8,128)(2,1)S(1)}, u32[]{:S(2)}, u32[]{:S(2)}) collective-permute-start(bf16[112,1280]{1,0:T(8,128)(2,1)S(1)} %get-tuple-element.95), channel_id=1, source_target_pairs={{0,1},{1,2},{2,3},{3,0},{4,5},{5,6},{6,7},{7,4},{8,9},{9,10},{10,1... | collective-permute-start | bytes 860168 | tf_op jit(solution)/shard_map/ppermute | solution.py:43
  41.0 10.4 %collective-permute-start.12 = (bf16[112,1280]{1,0:T(8,128)(2,1)S(1)}, bf16[112,1280]{1,0:T(8,128)(2,1)S(1)}, u32[]{:S(2)}, u32[]{:S(2)}) collective-permute-start(bf16[112,1280]{1,0:T(8,128)(2,1)S(1)} %get-tuple-element.96), channel_id=1, source_target_pairs={{0,3},{1,0},{2,1},{3,2},{4,7},{5,4},{6,5},{7,6},{8,11},{9,8},{10,9... | collective-permute-start | bytes 860168 | tf_op jit(solution)/shard_map/ppermute | solution.py:43
  51.5 15.8 %collective-permute-start.19 = (bf16[224,1280]{1,0:T(8,128)(2,1)S(1)}, bf16[224,1280]{1,0:T(8,128)(2,1)S(1)}, u32[]{:S(2)}, u32[]{:S(2)}) collective-permute-start(bf16[224,1280]{1,0:T(8,128)(2,1)S(1)} %pad_maximum_fusion.1), channel_id=1, source_target_pairs={{0,3},{1,0},{2,1},{3,2},{4,7},{5,4},{6,5},{7,6},{8,11},{9,8},{10,9... | collective-permute-start | bytes 1720328 | tf_op jit(solution)/shard_map/ppermute | solution.py:43
  51.8 6.1 %collective-permute-start.13 = (bf16[7,224,256]{2,1,0:T(8,128)(2,1)S(1)}, bf16[7,224,256]{2,1,0:T(8,128)(2,1)S(1)}, u32[]{:S(2)}, u32[]{:S(2)}) collective-permute-start(bf16[7,224,256]{2,1,0:T(8,128)(2,1)S(1)} %get-tuple-element.101), channel_id=1, source_target_pairs={{0,4},{4,0},{8,12},{12,8},{16,20},{20,16},{24,28},{28,24},{32,36},... | collective-permute-start | bytes 2408456 | tf_op jit(solution)/shard_map/ppermute | solution.py:39
  52.0 16.0 %collective-permute-start.18 = (bf16[224,1280]{1,0:T(8,128)(2,1)S(1)}, bf16[224,1280]{1,0:T(8,128)(2,1)S(1)}, u32[]{:S(2)}, u32[]{:S(2)}) collective-permute-start(bf16[224,1280]{1,0:T(8,128)(2,1)S(1)} %pad_maximum_fusion), channel_id=1, source_target_pairs={{0,1},{1,2},{2,3},{3,0},{4,5},{5,6},{6,7},{7,4},{8,9},{9,10},{10,1... | collective-permute-start | bytes 1720328 | tf_op jit(solution)/shard_map/ppermute | solution.py:43
  57.9 3.6 %collective-permute-start.16 = (bf16[2,224,256]{2,1,0:T(8,128)(2,1)S(1)}, bf16[2,224,256]{2,1,0:T(8,128)(2,1)S(1)}, u32[]{:S(2)}, u32[]{:S(2)}) collective-permute-start(bf16[2,224,256]{2,1,0:T(8,128)(2,1)S(1)} %get-tuple-element.108), channel_id=1, source_target_pairs={{0,4},{4,0},{8,12},{12,8},{16,20},{20,16},{24,28},{28,24},{32,36},... | collective-permute-start | bytes 688136 | tf_op jit(solution)/shard_map/ppermute | solution.py:39
  58.4 12.5 %collective-permute-start.14 = (bf16[2,224,256]{2,1,0:T(8,128)(2,1)S(1)}, bf16[2,224,256]{2,1,0:T(8,128)(2,1)S(1)}, u32[]{:S(2)}, u32[]{:S(2)}) collective-permute-start(bf16[2,224,256]{2,1,0:T(8,128)(2,1)S(1)} %get-tuple-element.123), channel_id=1, source_target_pairs={{0,24},{4,28},{8,0},{12,4},{16,8},{20,12},{24,16},{28,20},{32,56},... | collective-permute-start | bytes 688136 | tf_op jit(solution)/shard_map/ppermute | solution.py:39
  60.7 10.3 %collective-permute-start.15 = (bf16[2,224,256]{2,1,0:T(8,128)(2,1)S(1)}, bf16[2,224,256]{2,1,0:T(8,128)(2,1)S(1)}, u32[]{:S(2)}, u32[]{:S(2)}) collective-permute-start(bf16[2,224,256]{2,1,0:T(8,128)(2,1)S(1)} %get-tuple-element.122), channel_id=1, source_target_pairs={{0,16},{4,20},{8,24},{12,28},{16,0},{20,4},{24,8},{28,12},{32,48},... | collective-permute-start | bytes 688136 | tf_op jit(solution)/shard_map/ppermute | solution.py:39
  61.6 13.0 %collective-permute-start.17 = (bf16[2,224,256]{2,1,0:T(8,128)(2,1)S(1)}, bf16[2,224,256]{2,1,0:T(8,128)(2,1)S(1)}, u32[]{:S(2)}, u32[]{:S(2)}) collective-permute-start(bf16[2,224,256]{2,1,0:T(8,128)(2,1)S(1)} %add_convert_fusion.4), channel_id=1, source_target_pairs={{0,8},{4,12},{8,16},{12,20},{16,24},{20,28},{24,0},{28,4},{32,40},... | collective-permute-start | bytes 688136 | tf_op jit(solution)/shard_map/ppermute | solution.py:39
  74.8 5.7 %collective-permute-start.20 = (bf16[224,256]{1,0:T(8,128)(2,1)S(1)}, bf16[224,256]{1,0:T(8,128)(2,1)S(1)}, u32[]{:S(2)}, u32[]{:S(2)}) collective-permute-start(bf16[224,256]{1,0:T(8,128)(2,1)S(1)} %get-tuple-element.120), channel_id=1, source_target_pairs={{0,96},{4,100},{8,104},{12,108},{16,112},{20,116},{24,120},{28,124... | collective-permute-start | bytes 344072 | tf_op jit(solution)/shard_map/ppermute | solution.py:39
  77.0 6.3 %collective-permute-start.21 = (bf16[224,256]{1,0:T(8,128)(2,1)S(1)}, bf16[224,256]{1,0:T(8,128)(2,1)S(1)}, u32[]{:S(2)}, u32[]{:S(2)}) collective-permute-start(bf16[224,256]{1,0:T(8,128)(2,1)S(1)} %get-tuple-element.121), channel_id=1, source_target_pairs={{0,64},{4,68},{8,72},{12,76},{16,80},{20,84},{24,88},{28,92},{32,9... | collective-permute-start | bytes 344072 | tf_op jit(solution)/shard_map/ppermute | solution.py:39
  (2 other events, 11.0 us)

commit v4 on v3

--- a/solution.py
+++ b/solution.py
@@ -68,17 +68,17 @@
 
 
 def seen(tile, seg, rows):
-    count = jnp.sum(jnp.where(tile.astype(F32) == seg, 1.0, 0.0))
-    return rows - count.astype(jnp.int32)
+    match = jnp.sum(jnp.where(tile.astype(F32) == seg, 1.0, 0.0), axis=0, keepdims=True)
+    return rows - jnp.sum(match, axis=1, keepdims=True)
 
 
 def masks(refs, info, rows, width, own):
-    at = lax.broadcasted_iota(jnp.int32, (rows, width), 0)
+    at = lax.broadcasted_iota(jnp.int32, (rows, width), 0).astype(F32)
     result = []
     for index, (ref, slot) in enumerate(refs):
         if own and index == 0:
             segs = ref[slot, pl.ds(rows, TILE), :].astype(F32).T[:rows, :1]
-            result.append((at.astype(F32) <= info[0:1, :]) & (segs == info[1:2, :]))
+            result.append((at <= info[0:1, :]) & (segs == info[1:2, :]))
         else:
             result.append(at >= seen(ref[slot, pl.ds(rows, TILE), :], info[3:4, : 2 * HD], rows))
     return result
@@ -107,8 +107,12 @@
     return new, total * alpha + added, acc * alpha + out
 
 
-def column_refs(column, other, core):
-    return [(column, 0), (column, 1), (column, 2), (other, 1), (other, 2 - 2 * core)]
+def column_refs(column):
+    return [(column, 0), (column, 1), (column, 2)]
+
+
+def beside_refs(other, core):
+    return [(other, 2 * NZ - 1), (other, 2 * NZ - 2 * core)]
 
 
 def side_refs(side, other, dz):
@@ -150,28 +154,19 @@
     info[4:, :] = jnp.zeros((info.shape[0] - 4, width), F32)
 
 
-def forward_column(rows, factor, q, column, other, top, total, acc, q5, info):
+def forward_column(rows, factor, q, column, top, total, acc, q5, info):
     stack_heads(q, q5, rows)
     describe_rows(column[0, pl.ds(rows, TILE), :], rows, info)
-    _, _, core = where_am_i()
     width = info.shape[1]
     near = info[2:3, :] > 0.5
-    refs = column_refs(column, other, core)
+    refs = column_refs(column)
     visible = masks(refs, info, rows, width, True)
     state = attend(refs[:1], visible[:1], None, q5[...], rows, factor, (None, None, None), None)
     state = attend(refs[1:], visible[1:], None, q5[...], rows, factor, state, near)
     top[...], total[...], acc[...] = state
 
 
-def forward_near(
-    rows, factor, weight, info, q5, partial, g2_top, g2_end, side, top, total, acc,
-    top_out, total_out, acc_out, g5, held, sem,
-):
-    x = lax.axis_index("mp")
-    part = held.shape[1]
-    column = pl.multiple_of(lax.rem(x + 2, NX) * part, 128)
-    copy = pltpu.make_async_copy(weight.at[:, pl.ds(column, part)], held, sem)
-    copy.start()
+def forward_near(rows, factor, info, q5, side, top, total, acc, top_out, total_out, acc_out):
     near = info[2:3, :] > 0.5
     state = (top[...], total[...], acc[...])
     for group in (range(0, 3), range(3, 6)):
@@ -179,28 +174,26 @@
         visible = masks(refs, info, rows, info.shape[1], False)
         state = attend(refs, visible, None, q5[...], rows, factor, state, near)
     top_out[...], total_out[...], acc_out[...] = state
-    g2 = jnp.concatenate([g2_top[...], g2_end[...]], axis=0)
-    copy.wait()
-    stack_heads((partial[...] + dot(g2, held[...], NT)).astype(BF16), g5, rows)
 
 
 def forward_far(
-    rows, factor, weight, info, q5, g5, other, top, total, acc,
-    lse, delta, here, up, down, far_top, far_end, held, attn, sem,
+    rows, factor, weight, info, q5, other, top, total, acc,
+    lse, attn_t, here, up, down, far_top, far_end, held, attn, sem,
 ):
     copy = pltpu.make_async_copy(weight, held, sem)
     copy.start()
     x = lax.axis_index("mp")
+    _, _, core = where_am_i()
     near = info[2:3, :] > 0.5
     state = (top[...], total[...], acc[...])
-    for group in (range(0, 3), range(3, 6)):
-        refs = [(other, slot) for slot in group]
+    shards = [(other, slot) for slot in range(2 * NZ - 2)] + beside_refs(other, core)
+    for refs in (shards[:4], shards[4:]):
         visible = masks(refs, info, rows, info.shape[1], False)
         state = attend(refs, visible, None, q5[...], rows, factor, state, near)
     out_t = (state[2] / state[1]).astype(BF16)
     spread_heads(out_t.T, attn, rows)
     lse[...] = state[0] + jnp.log2(state[1])
-    delta[...] = jnp.sum(out_t.astype(F32) * g5[...].T.astype(F32), axis=0, keepdims=True)
+    attn_t[...] = out_t
     copy.wait()
     part = here.shape[1]
 
@@ -232,27 +225,10 @@
     return d_key, d_value, dot(keys, slope, TN)
 
 
-def backward_side(rows, factor, scale, parts, info, q5, g5, lse, delta, side, other, *rest):
-    if len(parts) > 1:
-        column, column_other, acc, stay, leave = rest
-    else:
-        before, acc, stay, leave = rest
-    _, _, core = where_am_i()
-    width = info.shape[1]
+def backward_parts(rows, factor, scale, groups, info, q5, g5, lse, delta, total, acc):
     norm = jnp.where(info[2:3, :] > 0.5, lse[...], HIGH)
-    groups = []
-    for index, dz in enumerate(parts):
-        outs = ((stay, 2 * index), (leave, 2 * index), (stay, 2 * index + 1), (leave, 2 * index + 1))
-        groups.append((side_refs(side, other, dz - 1), outs))
-    total = None
-    if len(parts) > 1:
-        first = 2 * len(parts)
-        groups.append((column_refs(column, column_other, core)[3:], ((leave, first + 1), (leave, first + 2 - 2 * core))))
-        leave[first + 2 * core] = jnp.zeros(leave.shape[1:], BF16)
-    else:
-        total = before[...]
     for refs, outs in groups:
-        visible = masks(refs, info, rows, width, False)
+        visible = masks(refs, info, rows, info.shape[1], False)
         d_key, d_value, d_query = grads_of(refs, visible, norm, delta[...], q5[...], g5[...], rows, factor, scale)
         for i, (out, slot) in enumerate(outs):
             out[slot, :, :HD] = d_key[i * rows : (i + 1) * rows]
@@ -261,10 +237,41 @@
     acc[...] = total
 
 
+def side_group(side, other, dz, stay, leave, at):
+    return side_refs(side, other, dz - 1), ((stay, at), (leave, at), (stay, at + 1), (leave, at + 1))
+
+
+def backward_first(
+    rows, factor, scale, weight, info, q5, partial, g2_top, g2_end, attn_t, lse, side, other,
+    acc, stay, leave, g5, delta, held, sem,
+):
+    x = lax.axis_index("mp")
+    column = pl.multiple_of(lax.rem(x + 2, NX) * held.shape[1], 128)
+    copy = pltpu.make_async_copy(weight.at[:, pl.ds(column, held.shape[1])], held, sem)
+    copy.start()
+    _, _, core = where_am_i()
+    leave[4 + 2 * core] = jnp.zeros(leave.shape[1:], BF16)
+    g2 = jnp.concatenate([g2_top[...], g2_end[...]], axis=0)
+    copy.wait()
+    stack_heads((partial[...] + dot(g2, held[...], NT)).astype(BF16), g5, rows)
+    delta[...] = jnp.sum(attn_t[...].astype(F32) * g5[...].T.astype(F32), axis=0, keepdims=True)
+    groups = [
+        side_group(side, other, 2, stay, leave, 0),
+        side_group(side, other, 1, stay, leave, 2),
+        (beside_refs(other, core), ((leave, 5), (leave, 6 - 2 * core))),
+    ]
+    backward_parts(rows, factor, scale, groups, info, q5, g5, lse, delta, None, acc)
+
+
+def backward_second(rows, factor, scale, info, q5, g5, lse, delta, side, other, before, acc, stay, leave):
+    groups = [side_group(side, other, 3, stay, leave, 0)]
+    backward_parts(rows, factor, scale, groups, info, q5, g5, lse, delta, before[...], acc)
+
+
 def backward_column(rows, factor, scale, info, q5, g5, lse, delta, column, acc, dq, stay):
     width = info.shape[1]
     norm = jnp.where(info[2:3, :] > 0.5, lse[...], HIGH)
-    refs = [(column, 0), (column, 1), (column, 2)]
+    refs = column_refs(column)
     visible = masks(refs, info, rows, width, True)
     total = acc[...]
     for part, limit in ((slice(0, 1), lse[...]), (slice(1, 3), norm)):
@@ -345,21 +352,18 @@
         pack, shape(rows + TILE, 2 * HD), 1, seg_ids.reshape(1, rows), keys, values, pinned=3, mib=60,
         scratch=[pltpu.VMEM((1, rows), jnp.int32), pltpu.SemaphoreType.DMA((3,))],
     )
-    own, grad_out = lax.optimization_barrier((own, grad_out))
     y1, y2 = move(own, dy=1), move(own, dy=2)
     g1, g3 = move_x(grad_out, 1), move_x(grad_out, 3)
     y1, y2 = lax.optimization_barrier((y1, y2))
     y1, y2 = jnp.where(y >= 1, y1, 0), jnp.where(y >= 2, y2, 0)
 
     column = jnp.stack([own, y1, y2])
-    column_other = move(column, flip=1)
     sides = {dz: jnp.stack([y1, jnp.where(z + dz < NZ, own, y2)]) for dz in (2, 1, 3)}
-    sides[3], column_other = lax.optimization_barrier((sides[3], column_other))
     sides = [move(sides[dz], dz=dz) for dz in (1, 2, 3)]
     g2_top, g2_end = move_x(g1[:half], 1), move_x(g3[half:], 3)
     top, total, acc, q5, info = call(
         lambda *refs: forward_column(rows, factor, *refs),
-        (line, line, square, stacked, shape(8, width, dtype=F32)), 1, queries, column, column_other,
+        (line, line, square, stacked, shape(8, width, dtype=F32)), 1, queries, column,
     )
     part = grad_out.shape[1]
     partial = call(
@@ -370,48 +374,59 @@
             pltpu.SemaphoreType.DMA((2 * (NX - 1),)),
         ],
     )
-    *sides, g2_top, g2_end, top, partial = lax.optimization_barrier((*sides, g2_top, g2_end, top, partial))
-
-    side = jnp.concatenate(sides)
+    *sides, top, partial = lax.optimization_barrier((*sides, top, partial))
+
+    side = jnp.concatenate([*sides, column])
     side_other = move(side, flip=1)
-    top, total, acc, g5, side_other = lax.optimization_barrier(
+    top, total, acc, side_other = lax.optimization_barrier(
         (
             *call(
                 lambda *refs: forward_near(rows, factor, *refs),
-                (line, line, square, stacked), 4,
-                out_weight, info, q5, partial, g2_top, g2_end, side, top, total, acc, pinned=1,
-                scratch=[pltpu.VMEM((out_weight.shape[0], part), BF16), pltpu.SemaphoreType.DMA],
+                (line, line, square), 4, info, q5, side, top, total, acc,
             ),
             side_other,
         )
     )
     whole, halved = shape(rows, part), shape(half, part)
-    lse, delta, here, up, down, *far = call(
+    lse, attn_t, here, up, down, *far = call(
         lambda *refs: forward_far(rows, factor, *refs),
-        (line, line, whole, whole, whole, halved, halved), 6,
-        out_weight, info, q5, g5, side_other, top, total, acc, pinned=1, mib=30,
+        (line, shape(HD, width), whole, whole, whole, halved, halved), 1,
+        out_weight, info, q5, side_other, top, total, acc, pinned=1, mib=30,
         scratch=[
             pltpu.VMEM(out_weight.shape, BF16),
             pltpu.VMEM((rows, GROUP * HD), BF16),
             pltpu.SemaphoreType.DMA,
         ],
     )
+    lse, *far, g2_top, g2_end = lax.optimization_barrier((lse, *far, g2_top, g2_end))
     early = (move_x(far[0], 1), move_x(far[1], 3))
 
-    def side_grads(parts, kept, sent, micros, *more):
-        return call(
-            lambda *refs: backward_side(rows, factor, scale, parts, *refs),
-            (square, shape(kept, rows, 2 * HD), shape(sent, rows, 2 * HD)), micros,
-            info, q5, g5, lse, delta, side, side_other, *more,
+    def pieces(count):
+        return shape(count, rows, 2 * HD)
+
+    acc, stay, leave, g5, delta, *early = lax.optimization_barrier(
+        (
+            *call(
+                lambda *refs: backward_first(rows, factor, scale, *refs),
+                (square, pieces(4), pieces(7), stacked, line), 8,
+                out_weight, info, q5, partial, g2_top, g2_end, attn_t, lse, side, side_other, pinned=1,
+                scratch=[pltpu.VMEM((out_weight.shape[0], part), BF16), pltpu.SemaphoreType.DMA],
+            ),
+            *early,
         )
-
-    acc, stay, leave, *early = lax.optimization_barrier(
-        (*side_grads((2, 1), 4, 7, 7, column, column_other), *early)
     )
     up = jnp.concatenate([add_up(up[:half], early[0]).astype(BF16), up[half:]], axis=0)
     down = jnp.concatenate([down[:half], add_up(down[half:], early[1]).astype(BF16)], axis=0)
     other = move(leave, flip=1)
-    acc, stay_last, leave_last, other = lax.optimization_barrier((*side_grads((3,), 2, 2, 3, acc), other))
+    acc, stay_last, leave_last, other = lax.optimization_barrier(
+        (
+            *call(
+                lambda *refs: backward_second(rows, factor, scale, *refs),
+                (square, pieces(2), pieces(2)), 3, info, q5, g5, lse, delta, side, side_other, acc,
+            ),
+            other,
+        )
+    )
     other_last = move(leave_last, flip=1)
     mixed = add_up(stay, other[:4]).astype(BF16)
     returned = {2: move(mixed[:2], dz=-2), 1: move(mixed[2:], dz=-1)}
@@ -421,7 +436,7 @@
         (
             *call(
                 lambda *refs: backward_column(rows, factor, scale, *refs),
-                (shape(rows, GROUP * HD), shape(3, rows, 2 * HD)), 3,
+                (shape(rows, GROUP * HD), pieces(3)), 3,
                 info, q5, g5, lse, delta, column, acc,
             ),
             returned[1], returned[2], returned[3], up, down,

time: 85.1 us -> 84 us (0.987)
  waiting for transfers between devices: 24.1 us -> 23.2 us
    ppermute x8, waiting for transfers between devices: 6.43 us -> 4.71 us  [move_x(): return lax.ppermute(value, 'mp', [(x, (x + dx) % NX) for x in range(NX)])]
    ppermute x14 -> x13, waiting for transfers between devices: 17.7 us -> 18.4 us  [move(): return lax.ppermute(value, 'dp', shift(dy, dz, flip))]
    ppermute x14 -> x13, starting transfers between devices: 16.2 us -> 16.7 us  [move(): return lax.ppermute(value, 'dp', shift(dy, dz, flip))]
  transfers between devices with their start and end apart: 22 -> 21, of which waited for: 13 -> 11; matrix products, arithmetic and copies ran while one was open for 3% -> 3% of each run, Pallas kernels for 27% -> 33%
where the time goes in v4:
time: 84 us; the launch traced here: 83.4 us
  Pallas kernels  29 us (35%)
  starting transfers between devices  26.4 us (31%)
  waiting for transfers between devices  23.2 us (28%)
  other arithmetic  3.02 us (4%)
  between operations  0.94 us (1%)
  local copies, waits for them, and re-layouts  0.85 us (1%)
    pallas_call x8, Pallas kernels, call(): pl.pallas_call(body, out_shape=outs, in_specs=[anywhere] * loose + [fixed...  29 us
    ppermute x13, waiting for transfers between devices, move(): return lax.ppermute(value, 'dp', shift(dy, dz, flip))  18.4 us
    ppermute x13, starting transfers between devices, move(): return lax.ppermute(value, 'dp', shift(dy, dz, flip))  16.7 us
    ppermute x8, starting transfers between devices, move_x(): return lax.ppermute(value, 'mp', [(x, (x + dx) % NX) for x in range(NX)])  9.74 us
    ppermute x8, waiting for transfers between devices, move_x(): return lax.ppermute(value, 'mp', [(x, (x + dx) % NX) for x in range(NX)])  4.71 us
  transfers between devices with their start and end apart: 21, of which 11 were waited for; matrix products, arithmetic and copies ran while one was open for 3% of the time, Pallas kernels for 33%

profile of v4, /device:TPU:14, one launch (start us, length us, event | category | flops | bytes accessed | tf_op | source)
XLA Modules:
  0.0 83.4 jit_solution(7781751249093807012)
XLA Ops:
  0.6 1.6 %shard_map.93 = bf16[240,256]{1,0:T(8,128)(2,1)} custom-call(s32[1,224]{1,0:T(1,128)} %bitcast.28, bf16[224,128]{1,0:T(8,128)(2,1)} %keys.1, bf16[224,128]{1,0:T(8,128)(2,1)} %values.1), custom_call_target="tpu_custom_call" | custom-call | flops 1152999936 | tf_op jit(solution)/shard_map/pallas_call | solution.py:334
  2.2 1.6 %collective-permute-start = (bf16[240,256]{1,0:T(8,128)(2,1)}, bf16[240,256]{1,0:T(8,128)(2,1)S(1)}, u32[]{:S(2)}, u32[]{:S(2)}) collective-permute-start(bf16[240,256]{1,0:T(8,128)(2,1)} %shard_map.93), channel_id=1, source_target_pairs={{0,32},{4,36},{8,40},{12,44},{16,48},{20,52},{24,56},{28,60},{32,6... | collective-permute-start | bytes 368648 | tf_op jit(solution)/shard_map/ppermute | solution.py:39
  5.2 1.6 %collective-permute-start.6 = (bf16[224,1280]{1,0:T(8,128)(2,1)S(1)}, bf16[224,1280]{1,0:T(8,128)(2,1)S(1)}, u32[]{:S(2)}, u32[]{:S(2)}) collective-permute-start(bf16[224,1280]{1,0:T(8,128)(2,1)S(1)} %copy-done.1), channel_id=1, source_target_pairs={{0,3},{1,0},{2,1},{3,2},{4,7},{5,4},{6,5},{7,6},{8,11},{9,8},{10,9... | collective-permute-start | bytes 1720328 | tf_op jit(solution)/shard_map/ppermute | solution.py:43
  7.6 2.9 %collective-permute-done.1 = bf16[240,256]{1,0:T(8,128)(2,1)S(1)} collective-permute-done((bf16[240,256]{1,0:T(8,128)(2,1)}, bf16[240,256]{1,0:T(8,128)(2,1)S(1)}, u32[]{:S(2)}, u32[]{:S(2)}) %collective-permute-start.1) | collective-permute-done | bytes 122912 | tf_op jit(solution)/shard_map/ppermute | solution.py:39
  11.7 2.0 %collective-permute-start.2 = (bf16[2,240,256]{2,1,0:T(8,128)(2,1)S(1)}, bf16[2,240,256]{2,1,0:T(8,128)(2,1)S(1)}, u32[]{:S(2)}, u32[]{:S(2)}) collective-permute-start(bf16[2,240,256]{2,1,0:T(8,128)(2,1)S(1)} %get-tuple-element.131), channel_id=1, source_target_pairs={{0,8},{4,12},{8,16},{12,20},{16,24},{20,28},{24,0},{28,4},{32,40},... | collective-permute-start | bytes 737288 | tf_op jit(solution)/shard_map/ppermute | solution.py:39
  13.7 3.6 %collective-permute-start.3 = (bf16[2,240,256]{2,1,0:T(8,128)(2,1)S(1)}, bf16[2,240,256]{2,1,0:T(8,128)(2,1)S(1)}, u32[]{:S(2)}, u32[]{:S(2)}) collective-permute-start(bf16[2,240,256]{2,1,0:T(8,128)(2,1)S(1)} %get-tuple-element.130), channel_id=1, source_target_pairs={{0,16},{4,20},{8,24},{12,28},{16,0},{20,4},{24,8},{28,12},{32,48},... | collective-permute-start | bytes 737288 | tf_op jit(solution)/shard_map/ppermute | solution.py:39
  18.3 1.9 %shard_map.94 = (f32[1,1152]{1,0:T(1,128)S(1)}, f32[1,1152]{1,0:T(1,128)S(1)}, f32[128,1152]{1,0:T(8,128)S(1)}, bf16[1152,128]{1,0:T(8,128)(2,1)S(1)}, f32[8,1152]{1,0:T(8,128)S(1)}) custom-call(bf16[224,640]{1,0:T(8,128)(2,1)S(1)} %copy-done.2, bf16[3,240,256]{2,1,0:T(8,128)(2,1)S(1)} %pad_maximum_fusion.2.refs_1_.refs_5_), custom_call_target="tpu_custom_call" | custom-call | flops 1152999936 | tf_op jit(solution)/shard_map/pallas_call | solution.py:334
  20.6 3.1 %shard_map.95.refs_3_ = f32[224,640]{1,0:T(8,128)S(1)} custom-call(bf16[224,1280]{1,0:T(8,128)(2,1)S(1)} %copy-done.1, bf16[224,1280]{1,0:T(8,128)(2,1)S(1)} %collective-permute-done.5.g1, bf16[224,1280]{1,0:T(8,128)(2,1)S(1)} %collective-permute-done.6.g3, bf16[640,5120]{1,0:T(8,128)(2,1)S(1)} %copy-done), custom_call_target="tpu_custom_call" | custom-call | flops 3459000064 | tf_op jit(solution)/shard_map/pallas_call | solution.py:334
  23.7 3.0 %collective-permute-done.3 = bf16[2,240,256]{2,1,0:T(8,128)(2,1)S(1)} collective-permute-done((bf16[2,240,256]{2,1,0:T(8,128)(2,1)S(1)}, bf16[2,240,256]{2,1,0:T(8,128)(2,1)S(1)}, u32[]{:S(2)}, u32[]{:S(2)}) %collective-permute-start.3) | collective-permute-done | bytes 245792 | tf_op jit(solution)/shard_map/ppermute | solution.py:39
  27.6 1.8 %collective-permute-start.9 = (bf16[112,1280]{1,0:T(8,128)(2,1)S(1)}, bf16[112,1280]{1,0:T(8,128)(2,1)S(1)}, u32[]{:S(2)}, u32[]{:S(2)}) collective-permute-start(bf16[112,1280]{1,0:T(8,128)(2,1)S(1)} %slice.85), channel_id=1, source_target_pairs={{0,3},{1,0},{2,1},{3,2},{4,7},{5,4},{6,5},{7,6},{8,11},{9,8},{10,9... | collective-permute-start | bytes 860168 | tf_op jit(solution)/shard_map/ppermute | solution.py:43
  29.4 2.8 %shard_map.96 = (f32[1,1152]{1,0:T(1,128)S(1)}, f32[1,1152]{1,0:T(1,128)S(1)}, f32[128,1152]{1,0:T(8,128)S(1)}) custom-call(f32[8,1152]{1,0:T(8,128)S(1)} %get-tuple-element.65.refs_0_.refs_1_, bf16[1152,128]{1,0:T(8,128)(2,1)S(1)} %get-tuple-element.66.refs_1_.refs_2_, bf16[9,240,256]{2,1,0:T(8,128)(2,1)S(1)} %constant_dynamic-update-slice_fusion.refs_2_.refs_8_.refs_5_, ...), custom_call_target="tpu_custom_call" | custom-call | flops 4611999744 | tf_op jit(solution)/shard_map/pallas_call | solution.py:334
  32.2 6.2 %shard_map.97 = (f32[1,1152]{1,0:T(1,128)S(1)}, bf16[128,1152]{1,0:T(8,128)(2,1)S(1)}, bf16[224,1280]{1,0:T(8,128)(2,1)S(1)}, bf16[224,1280]{1,0:T(8,128)(2,1)S(...) custom-call(bf16[640,5120]{1,0:T(8,128)(2,1)S(1)} %copy-done, ...), custom_call_target="tpu_custom_call" | custom-call | flops 1152999936 | tf_op jit(solution)/shard_map/pallas_call | solution.py:334
  38.4 1.8 %collective-permute-start.10 = (bf16[112,1280]{1,0:T(8,128)(2,1)S(1)}, bf16[112,1280]{1,0:T(8,128)(2,1)S(1)}, u32[]{:S(2)}, u32[]{:S(2)}) collective-permute-start(bf16[112,1280]{1,0:T(8,128)(2,1)S(1)} %get-tuple-element.95), channel_id=1, source_target_pairs={{0,1},{1,2},{2,3},{3,0},{4,5},{5,6},{6,7},{7,4},{8,9},{9,10},{10,1... | collective-permute-start | bytes 860168 | tf_op jit(solution)/shard_map/ppermute | solution.py:43
  40.5 7.5 %shard_map.98 = (f32[128,1152]{1,0:T(8,128)S(1)}, bf16[4,224,256]{2,1,0:T(8,128)(2,1)S(1)}, bf16[7,224,256]{2,1,0:T(8,128)(2,1)S(1)}, bf16[1152,128]{1,0:T(8,128)(2,1)S(1)}, f32[1,1152]{1,0:T(1,128)S(1)}) custom-call(bf16[640,5120]{1,0:T(8,128)(2,1)S(1)} %copy-done, f32[8,1152]{1,0:T(8,128)S(1)} %get-tuple-element.65.refs_0_.refs_1_, ...), custom_call_target="tpu_custom_call" | custom-call | flops 9223999488 | tf_op jit(solution)/shard_map/pallas_call | solution.py:334
  48.1 1.7 %collective-permute-done.11 = bf16[112,1280]{1,0:T(8,128)(2,1)S(1)} collective-permute-done((bf16[112,1280]{1,0:T(8,128)(2,1)S(1)}, bf16[112,1280]{1,0:T(8,128)(2,1)S(1)}, u32[]{:S(2)}, u32[]{:S(2)}) %collective-permute-start.11) | collective-permute-done | bytes 286752 | tf_op jit(solution)/shard_map/ppermute | solution.py:43
  50.2 3.2 %collective-permute-start.17 = (bf16[224,1280]{1,0:T(8,128)(2,1)S(1)}, bf16[224,1280]{1,0:T(8,128)(2,1)S(1)}, u32[]{:S(2)}, u32[]{:S(2)}) collective-permute-start(bf16[224,1280]{1,0:T(8,128)(2,1)S(1)} %pad_maximum_fusion), channel_id=1, source_target_pairs={{0,1},{1,2},{2,3},{3,0},{4,5},{5,6},{6,7},{7,4},{8,9},{9,10},{10,1... | collective-permute-start | bytes 1720328 | tf_op jit(solution)/shard_map/ppermute | solution.py:43
  53.4 2.8 %shard_map.99 = (f32[128,1152]{1,0:T(8,128)S(1)}, bf16[2,224,256]{2,1,0:T(8,128)(2,1)S(1)}, bf16[2,224,256]{2,1,0:T(8,128)(2,1)S(1)}) custom-call(f32[8,1152]{1,0:T(8,128)S(1)} %get-tuple-element.65.refs_0_.refs_1_, bf16[1152,128]{1,0:T(8,128)(2,1)S(1)} %get-tuple-element.66.refs_1_.refs_2_, bf16[1152,128]{1,0:T(8,128)(2,1)S(1)} %get-tuple-element.97.refs_2_, ...), custom_call_target="tpu_custom_call" | custom-call | flops 3459000064 | tf_op jit(solution)/shard_map/pallas_call | solution.py:334
  56.7 2.2 %collective-permute-start.13 = (bf16[2,224,256]{2,1,0:T(8,128)(2,1)S(1)}, bf16[2,224,256]{2,1,0:T(8,128)(2,1)S(1)}, u32[]{:S(2)}, u32[]{:S(2)}) collective-permute-start(bf16[2,224,256]{2,1,0:T(8,128)(2,1)S(1)} %get-tuple-element.125), channel_id=1, source_target_pairs={{0,24},{4,28},{8,0},{12,4},{16,8},{20,12},{24,16},{28,20},{32,56},... | collective-permute-start | bytes 688136 | tf_op jit(solution)/shard_map/ppermute | solution.py:39
  60.6 3.1 %shard_map.100 = (bf16[224,640]{1,0:T(8,128)(2,1)}, bf16[3,224,256]{2,1,0:T(8,128)(2,1)S(1)}) custom-call(f32[8,1152]{1,0:T(8,128)S(1)} %get-tuple-element.65.refs_0_.refs_1_, bf16[1152,128]{1,0:T(8,128)(2,1)S(1)} %get-tuple-element.66.refs_1_.refs_2_, bf16[1152,128]{1,0:T(8,128)(2,1)S(1)} %get-tuple-element.97.refs_2_, ...), custom_call_target="tpu_custom_call" | custom-call | flops 3459000064 | tf_op jit(solution)/shard_map/pallas_call | solution.py:334
  66.4 2.9 %collective-permute-done.13 = bf16[2,224,256]{2,1,0:T(8,128)(2,1)S(1)} collective-permute-done((bf16[2,224,256]{2,1,0:T(8,128)(2,1)S(1)}, bf16[2,224,256]{2,1,0:T(8,128)(2,1)S(1)}, u32[]{:S(2)}, u32[]{:S(2)}) %collective-permute-start.13) | collective-permute-done | bytes 229408 | tf_op jit(solution)/shard_map/ppermute | solution.py:39
  69.2 3.7 %collective-permute-done.16 = bf16[2,224,256]{2,1,0:T(8,128)(2,1)S(1)} collective-permute-done((bf16[2,224,256]{2,1,0:T(8,128)(2,1)S(1)}, bf16[2,224,256]{2,1,0:T(8,128)(2,1)S(1)}, u32[]{:S(2)}, u32[]{:S(2)}) %collective-permute-start.16) | collective-permute-done | bytes 229408 | tf_op jit(solution)/shard_map/ppermute | solution.py:39
  73.1 3.3 %collective-permute-start.19 = (bf16[224,256]{1,0:T(8,128)(2,1)S(1)}, bf16[224,256]{1,0:T(8,128)(2,1)S(1)}, u32[]{:S(2)}, u32[]{:S(2)}) collective-permute-start(bf16[224,256]{1,0:T(8,128)(2,1)S(1)} %get-tuple-element.122), channel_id=1, source_target_pairs={{0,96},{4,100},{8,104},{12,108},{16,112},{20,116},{24,120},{28,124... | collective-permute-start | bytes 344072 | tf_op jit(solution)/shard_map/ppermute | solution.py:39
  77.4 2.5 %collective-permute-done.19 = bf16[224,256]{1,0:T(8,128)(2,1)S(1)} collective-permute-done((bf16[224,256]{1,0:T(8,128)(2,1)S(1)}, bf16[224,256]{1,0:T(8,128)(2,1)S(1)}, u32[]{:S(2)}, u32[]{:S(2)}) %collective-permute-start.19) | collective-permute-done | bytes 114720 | tf_op jit(solution)/shard_map/ppermute | solution.py:39
  79.9 2.8 %collective-permute-done.20 = bf16[224,256]{1,0:T(8,128)(2,1)S(1)} collective-permute-done((bf16[224,256]{1,0:T(8,128)(2,1)S(1)}, bf16[224,256]{1,0:T(8,128)(2,1)S(1)}, u32[]{:S(2)}, u32[]{:S(2)}) %collective-permute-start.20) | collective-permute-done | bytes 114720 | tf_op jit(solution)/shard_map/ppermute | solution.py:39
  (60 shorter events, 13.0 us)
Async XLA Ops:
  2.2 5.3 %collective-permute-start = (bf16[240,256]{1,0:T(8,128)(2,1)}, bf16[240,256]{1,0:T(8,128)(2,1)S(1)}, u32[]{:S(2)}, u32[]{:S(2)}) collective-permute-start(bf16[240,256]{1,0:T(8,128)(2,1)} %shard_map.93), channel_id=1, source_target_pairs={{0,32},{4,36},{8,40},{12,44},{16,48},{20,52},{24,56},{28,60},{32,6... | collective-permute-start | bytes 368648 | tf_op jit(solution)/shard_map/ppermute | solution.py:39
  3.9 6.6 %collective-permute-start.1 = (bf16[240,256]{1,0:T(8,128)(2,1)}, bf16[240,256]{1,0:T(8,128)(2,1)S(1)}, u32[]{:S(2)}, u32[]{:S(2)}) collective-permute-start(bf16[240,256]{1,0:T(8,128)(2,1)} %shard_map.93), channel_id=1, source_target_pairs={{0,64},{4,68},{8,72},{12,76},{16,80},{20,84},{24,88},{28,92},{32,9... | collective-permute-start | bytes 368648 | tf_op jit(solution)/shard_map/ppermute | solution.py:39
  4.8 15.4 %collective-permute-start.5 = (bf16[224,1280]{1,0:T(8,128)(2,1)S(1)}, bf16[224,1280]{1,0:T(8,128)(2,1)S(1)}, u32[]{:S(2)}, u32[]{:S(2)}) collective-permute-start(bf16[224,1280]{1,0:T(8,128)(2,1)S(1)} %copy-done.1), channel_id=1, source_target_pairs={{0,1},{1,2},{2,3},{3,0},{4,5},{5,6},{6,7},{7,4},{8,9},{9,10},{10,1... | collective-permute-start | bytes 1720328 | tf_op jit(solution)/shard_map/ppermute | solution.py:43
  5.2 15.3 %collective-permute-start.6 = (bf16[224,1280]{1,0:T(8,128)(2,1)S(1)}, bf16[224,1280]{1,0:T(8,128)(2,1)S(1)}, u32[]{:S(2)}, u32[]{:S(2)}) collective-permute-start(bf16[224,1280]{1,0:T(8,128)(2,1)S(1)} %copy-done.1), channel_id=1, source_target_pairs={{0,3},{1,0},{2,1},{3,2},{4,7},{5,4},{6,5},{7,6},{8,11},{9,8},{10,9... | collective-permute-start | bytes 1720328 | tf_op jit(solution)/shard_map/ppermute | solution.py:43
  6.9 11.4 %copy-start.3 = (bf16[240,256]{1,0:T(8,128)(2,1)S(1)}, bf16[240,256]{1,0:T(8,128)(2,1)}, u32[]{:S(2)}) copy-start(bf16[240,256]{1,0:T(8,128)(2,1)} %shard_map.93) | copy-start | bytes 368644
  7.6 10.7 %copy-start.2 = (bf16[224,640]{1,0:T(8,128)(2,1)S(1)}, bf16[224,640]{1,0:T(8,128)(2,1)}, u32[]{:S(2)}) copy-start(bf16[224,640]{1,0:T(8,128)(2,1)} %refs_0_.3) | copy-start | bytes 860164
  10.5 10.1 %copy-start = (bf16[640,5120]{1,0:T(8,128)(2,1)S(1)}, bf16[640,5120]{1,0:T(8,128)(2,1)}, u32[]{:S(2)}) copy-start(bf16[640,5120]{1,0:T(8,128)(2,1)} %refs_0_.5) | copy-start | bytes 19660804
  11.7 12.0 %collective-permute-start.2 = (bf16[2,240,256]{2,1,0:T(8,128)(2,1)S(1)}, bf16[2,240,256]{2,1,0:T(8,128)(2,1)S(1)}, u32[]{:S(2)}, u32[]{:S(2)}) collective-permute-start(bf16[2,240,256]{2,1,0:T(8,128)(2,1)S(1)} %get-tuple-element.131), channel_id=1, source_target_pairs={{0,8},{4,12},{8,16},{12,20},{16,24},{20,28},{24,0},{28,4},{32,40},... | collective-permute-start | bytes 737288 | tf_op jit(solution)/shard_map/ppermute | solution.py:39
  13.7 13.1 %collective-permute-start.3 = (bf16[2,240,256]{2,1,0:T(8,128)(2,1)S(1)}, bf16[2,240,256]{2,1,0:T(8,128)(2,1)S(1)}, u32[]{:S(2)}, u32[]{:S(2)}) collective-permute-start(bf16[2,240,256]{2,1,0:T(8,128)(2,1)S(1)} %get-tuple-element.130), channel_id=1, source_target_pairs={{0,16},{4,20},{8,24},{12,28},{16,0},{20,4},{24,8},{28,12},{32,48},... | collective-permute-start | bytes 737288 | tf_op jit(solution)/shard_map/ppermute | solution.py:39
  17.2 9.5 %collective-permute-start.4 = (bf16[2,240,256]{2,1,0:T(8,128)(2,1)S(1)}, bf16[2,240,256]{2,1,0:T(8,128)(2,1)S(1)}, u32[]{:S(2)}, u32[]{:S(2)}) collective-permute-start(bf16[2,240,256]{2,1,0:T(8,128)(2,1)S(1)} %get-tuple-element.129), channel_id=1, source_target_pairs={{0,24},{4,28},{8,0},{12,4},{16,8},{20,12},{24,16},{28,20},{32,56},... | collective-permute-start | bytes 737288 | tf_op jit(solution)/shard_map/ppermute | solution.py:39
  26.9 5.3 %collective-permute-start.7 = (bf16[9,240,256]{2,1,0:T(8,128)(2,1)S(1)}, bf16[9,240,256]{2,1,0:T(8,128)(2,1)S(1)}, u32[]{:S(2)}, u32[]{:S(2)}) collective-permute-start(bf16[9,240,256]{2,1,0:T(8,128)(2,1)S(1)} %constant_dynamic-update-slice_fusion.refs_2_.refs_8_.refs_5_), channel_id=1, source_target_pairs={{0,4},{4,0},{8,12},{12,8},{16,20},{20,16},{24,28},{28,24},{32,36},... | collective-permute-start | bytes 3317768 | tf_op jit(solution)/shard_map/ppermute | solution.py:39
  27.0 11.4 %collective-permute-start.8 = (bf16[112,1280]{1,0:T(8,128)(2,1)S(1)}, bf16[112,1280]{1,0:T(8,128)(2,1)S(1)}, u32[]{:S(2)}, u32[]{:S(2)}) collective-permute-start(bf16[112,1280]{1,0:T(8,128)(2,1)S(1)} %slice.84), channel_id=1, source_target_pairs={{0,1},{1,2},{2,3},{3,0},{4,5},{5,6},{6,7},{7,4},{8,9},{9,10},{10,1... | collective-permute-start | bytes 860168 | tf_op jit(solution)/shard_map/ppermute | solution.py:43
  27.6 10.9 %collective-permute-start.9 = (bf16[112,1280]{1,0:T(8,128)(2,1)S(1)}, bf16[112,1280]{1,0:T(8,128)(2,1)S(1)}, u32[]{:S(2)}, u32[]{:S(2)}) collective-permute-start(bf16[112,1280]{1,0:T(8,128)(2,1)S(1)} %slice.85), channel_id=1, source_target_pairs={{0,3},{1,0},{2,1},{3,2},{4,7},{5,4},{6,5},{7,6},{8,11},{9,8},{10,9... | collective-permute-start | bytes 860168 | tf_op jit(solution)/shard_map/ppermute | solution.py:43
  38.4 9.7 %collective-permute-start.10 = (bf16[112,1280]{1,0:T(8,128)(2,1)S(1)}, bf16[112,1280]{1,0:T(8,128)(2,1)S(1)}, u32[]{:S(2)}, u32[]{:S(2)}) collective-permute-start(bf16[112,1280]{1,0:T(8,128)(2,1)S(1)} %get-tuple-element.95), channel_id=1, source_target_pairs={{0,1},{1,2},{2,3},{3,0},{4,5},{5,6},{6,7},{7,4},{8,9},{9,10},{10,1... | collective-permute-start | bytes 860168 | tf_op jit(solution)/shard_map/ppermute | solution.py:43
  40.2 9.6 %collective-permute-start.11 = (bf16[112,1280]{1,0:T(8,128)(2,1)S(1)}, bf16[112,1280]{1,0:T(8,128)(2,1)S(1)}, u32[]{:S(2)}, u32[]{:S(2)}) collective-permute-start(bf16[112,1280]{1,0:T(8,128)(2,1)S(1)} %get-tuple-element.96), channel_id=1, source_target_pairs={{0,3},{1,0},{2,1},{3,2},{4,7},{5,4},{6,5},{7,6},{8,11},{9,8},{10,9... | collective-permute-start | bytes 860168 | tf_op jit(solution)/shard_map/ppermute | solution.py:43
  49.9 14.9 %collective-permute-start.18 = (bf16[224,1280]{1,0:T(8,128)(2,1)S(1)}, bf16[224,1280]{1,0:T(8,128)(2,1)S(1)}, u32[]{:S(2)}, u32[]{:S(2)}) collective-permute-start(bf16[224,1280]{1,0:T(8,128)(2,1)S(1)} %pad_maximum_fusion.1), channel_id=1, source_target_pairs={{0,3},{1,0},{2,1},{3,2},{4,7},{5,4},{6,5},{7,6},{8,11},{9,8},{10,9... | collective-permute-start | bytes 1720328 | tf_op jit(solution)/shard_map/ppermute | solution.py:43
  50.0 6.2 %collective-permute-start.12 = (bf16[7,224,256]{2,1,0:T(8,128)(2,1)S(1)}, bf16[7,224,256]{2,1,0:T(8,128)(2,1)S(1)}, u32[]{:S(2)}, u32[]{:S(2)}) collective-permute-start(bf16[7,224,256]{2,1,0:T(8,128)(2,1)S(1)} %get-tuple-element.103), channel_id=1, source_target_pairs={{0,4},{4,0},{8,12},{12,8},{16,20},{20,16},{24,28},{28,24},{32,36},... | collective-permute-start | bytes 2408456 | tf_op jit(solution)/shard_map/ppermute | solution.py:39
  50.2 16.1 %collective-permute-start.17 = (bf16[224,1280]{1,0:T(8,128)(2,1)S(1)}, bf16[224,1280]{1,0:T(8,128)(2,1)S(1)}, u32[]{:S(2)}, u32[]{:S(2)}) collective-permute-start(bf16[224,1280]{1,0:T(8,128)(2,1)S(1)} %pad_maximum_fusion), channel_id=1, source_target_pairs={{0,1},{1,2},{2,3},{3,0},{4,5},{5,6},{6,7},{7,4},{8,9},{9,10},{10,1... | collective-permute-start | bytes 1720328 | tf_op jit(solution)/shard_map/ppermute | solution.py:43
  56.3 3.8 %collective-permute-start.15 = (bf16[2,224,256]{2,1,0:T(8,128)(2,1)S(1)}, bf16[2,224,256]{2,1,0:T(8,128)(2,1)S(1)}, u32[]{:S(2)}, u32[]{:S(2)}) collective-permute-start(bf16[2,224,256]{2,1,0:T(8,128)(2,1)S(1)} %get-tuple-element.110), channel_id=1, source_target_pairs={{0,4},{4,0},{8,12},{12,8},{16,20},{20,16},{24,28},{28,24},{32,36},... | collective-permute-start | bytes 688136 | tf_op jit(solution)/shard_map/ppermute | solution.py:39
  56.7 12.5 %collective-permute-start.13 = (bf16[2,224,256]{2,1,0:T(8,128)(2,1)S(1)}, bf16[2,224,256]{2,1,0:T(8,128)(2,1)S(1)}, u32[]{:S(2)}, u32[]{:S(2)}) collective-permute-start(bf16[2,224,256]{2,1,0:T(8,128)(2,1)S(1)} %get-tuple-element.125), channel_id=1, source_target_pairs={{0,24},{4,28},{8,0},{12,4},{16,8},{20,12},{24,16},{28,20},{32,56},... | collective-permute-start | bytes 688136 | tf_op jit(solution)/shard_map/ppermute | solution.py:39
  59.0 10.3 %collective-permute-start.14 = (bf16[2,224,256]{2,1,0:T(8,128)(2,1)S(1)}, bf16[2,224,256]{2,1,0:T(8,128)(2,1)S(1)}, u32[]{:S(2)}, u32[]{:S(2)}) collective-permute-start(bf16[2,224,256]{2,1,0:T(8,128)(2,1)S(1)} %get-tuple-element.124), channel_id=1, source_target_pairs={{0,16},{4,20},{8,24},{12,28},{16,0},{20,4},{24,8},{28,12},{32,48},... | collective-permute-start | bytes 688136 | tf_op jit(solution)/shard_map/ppermute | solution.py:39
  60.2 12.7 %collective-permute-start.16 = (bf16[2,224,256]{2,1,0:T(8,128)(2,1)S(1)}, bf16[2,224,256]{2,1,0:T(8,128)(2,1)S(1)}, u32[]{:S(2)}, u32[]{:S(2)}) collective-permute-start(bf16[2,224,256]{2,1,0:T(8,128)(2,1)S(1)} %add_convert_fusion.4), channel_id=1, source_target_pairs={{0,8},{4,12},{8,16},{12,20},{16,24},{20,28},{24,0},{28,4},{32,40},... | collective-permute-start | bytes 688136 | tf_op jit(solution)/shard_map/ppermute | solution.py:39
  73.1 6.8 %collective-permute-start.19 = (bf16[224,256]{1,0:T(8,128)(2,1)S(1)}, bf16[224,256]{1,0:T(8,128)(2,1)S(1)}, u32[]{:S(2)}, u32[]{:S(2)}) collective-permute-start(bf16[224,256]{1,0:T(8,128)(2,1)S(1)} %get-tuple-element.122), channel_id=1, source_target_pairs={{0,96},{4,100},{8,104},{12,108},{16,112},{20,116},{24,120},{28,124... | collective-permute-start | bytes 344072 | tf_op jit(solution)/shard_map/ppermute | solution.py:39
  76.4 6.3 %collective-permute-start.20 = (bf16[224,256]{1,0:T(8,128)(2,1)S(1)}, bf16[224,256]{1,0:T(8,128)(2,1)S(1)}, u32[]{:S(2)}, u32[]{:S(2)}) collective-permute-start(bf16[224,256]{1,0:T(8,128)(2,1)S(1)} %get-tuple-element.123), channel_id=1, source_target_pairs={{0,64},{4,68},{8,72},{12,76},{16,80},{20,84},{24,88},{28,92},{32,9... | collective-permute-start | bytes 344072 | tf_op jit(solution)/shard_map/ppermute | solution.py:39
  (1 other events, 4.2 us)

commit v5 on v4

--- a/solution.py
+++ b/solution.py
@@ -178,7 +178,7 @@
 
 def forward_far(
     rows, factor, weight, info, q5, other, top, total, acc,
-    lse, attn_t, here, up, down, far_top, far_end, held, attn, sem,
+    lse, attn_t, attn, up, down, far_top, far_end, held, sem,
 ):
     copy = pltpu.make_async_copy(weight, held, sem)
     copy.start()
@@ -187,7 +187,7 @@
     near = info[2:3, :] > 0.5
     state = (top[...], total[...], acc[...])
     shards = [(other, slot) for slot in range(2 * NZ - 2)] + beside_refs(other, core)
-    for refs in (shards[:4], shards[4:]):
+    for refs in (shards,):
         visible = masks(refs, info, rows, info.shape[1], False)
         state = attend(refs, visible, None, q5[...], rows, factor, state, near)
     out_t = (state[2] / state[1]).astype(BF16)
@@ -195,7 +195,7 @@
     lse[...] = state[0] + jnp.log2(state[1])
     attn_t[...] = out_t
     copy.wait()
-    part = here.shape[1]
+    part = up.shape[1]
 
     def features(dx):
         column = pl.multiple_of(lax.rem(x + dx, NX) * part, 128)
@@ -206,7 +206,6 @@
     far_end[...] = far[rows // 2 :]
     up[...] = features(1)
     down[...] = features(3)
-    here[...] = features(0)
 
 
 def grads_of(refs, visible, norm, delta, q5, g5, rows, factor, scale):
@@ -255,11 +254,9 @@
     copy.wait()
     stack_heads((partial[...] + dot(g2, held[...], NT)).astype(BF16), g5, rows)
     delta[...] = jnp.sum(attn_t[...].astype(F32) * g5[...].T.astype(F32), axis=0, keepdims=True)
-    groups = [
-        side_group(side, other, 2, stay, leave, 0),
-        side_group(side, other, 1, stay, leave, 2),
-        (beside_refs(other, core), ((leave, 5), (leave, 6 - 2 * core))),
-    ]
+    refs, outs = side_group(side, other, 1, stay, leave, 2)
+    refs, outs = refs + beside_refs(other, core), outs + ((leave, 5), (leave, 6 - 2 * core))
+    groups = [side_group(side, other, 2, stay, leave, 0), (refs, outs)]
     backward_parts(rows, factor, scale, groups, info, q5, g5, lse, delta, None, acc)
 
 
@@ -268,7 +265,13 @@
     backward_parts(rows, factor, scale, groups, info, q5, g5, lse, delta, before[...], acc)
 
 
-def backward_column(rows, factor, scale, info, q5, g5, lse, delta, column, acc, dq, stay):
+def backward_column(
+    rows, factor, scale, weight, info, q5, g5, lse, delta, column, acc, attn, dq, stay, here, held, sem
+):
+    x = lax.axis_index("mp")
+    at = pl.multiple_of(x * held.shape[1], 128)
+    copy = pltpu.make_async_copy(weight.at[:, pl.ds(at, held.shape[1])], held, sem)
+    copy.start()
     width = info.shape[1]
     norm = jnp.where(info[2:3, :] > 0.5, lse[...], HIGH)
     refs = column_refs(column)
@@ -283,6 +286,8 @@
             stay[slot, :, HD:] = d_value[i * rows : (i + 1) * rows]
         total = total + d_query
     spread_heads((total * scale).astype(BF16).T, dq, rows)
+    copy.wait()
+    here[...] = dot(attn[...], held[...], NN).astype(BF16)
 
 
 def grad_heads(g0, g1, g3, weight, partial, held, weights, sem):
@@ -388,15 +393,11 @@
         )
     )
     whole, halved = shape(rows, part), shape(half, part)
-    lse, attn_t, here, up, down, *far = call(
+    lse, attn_t, attn, up, down, *far = call(
         lambda *refs: forward_far(rows, factor, *refs),
-        (line, shape(HD, width), whole, whole, whole, halved, halved), 1,
+        (line, shape(HD, width), shape(rows, GROUP * HD), whole, whole, halved, halved), 1,
         out_weight, info, q5, side_other, top, total, acc, pinned=1, mib=30,
-        scratch=[
-            pltpu.VMEM(out_weight.shape, BF16),
-            pltpu.VMEM((rows, GROUP * HD), BF16),
-            pltpu.SemaphoreType.DMA,
-        ],
+        scratch=[pltpu.VMEM(out_weight.shape, BF16), pltpu.SemaphoreType.DMA],
     )
     lse, *far, g2_top, g2_end = lax.optimization_barrier((lse, *far, g2_top, g2_end))
     early = (move_x(far[0], 1), move_x(far[1], 3))
@@ -418,26 +419,23 @@
     up = jnp.concatenate([add_up(up[:half], early[0]).astype(BF16), up[half:]], axis=0)
     down = jnp.concatenate([down[:half], add_up(down[half:], early[1]).astype(BF16)], axis=0)
     other = move(leave, flip=1)
-    acc, stay_last, leave_last, other = lax.optimization_barrier(
-        (
-            *call(
-                lambda *refs: backward_second(rows, factor, scale, *refs),
-                (square, pieces(2), pieces(2)), 3, info, q5, g5, lse, delta, side, side_other, acc,
-            ),
-            other,
-        )
+    acc, other = lax.optimization_barrier((acc, other))
+    acc, stay_last, leave_last = call(
+        lambda *refs: backward_second(rows, factor, scale, *refs),
+        (square, pieces(2), pieces(2)), 7, info, q5, g5, lse, delta, side, side_other, acc,
     )
     other_last = move(leave_last, flip=1)
     mixed = add_up(stay, other[:4]).astype(BF16)
     returned = {2: move(mixed[:2], dz=-2), 1: move(mixed[2:], dz=-1)}
     returned[3] = move(add_up(stay_last, other_last).astype(BF16), dz=-3)
     up, down = move_x(up, 1), move_x(down, 3)
-    grad_query, stay, returned[1], returned[2], returned[3], up, down = lax.optimization_barrier(
+    grad_query, stay, here, returned[1], returned[2], returned[3], up, down = lax.optimization_barrier(
         (
             *call(
                 lambda *refs: backward_column(rows, factor, scale, *refs),
-                (shape(rows, GROUP * HD), pieces(3)), 3,
-                info, q5, g5, lse, delta, column, acc,
+                (shape(rows, GROUP * HD), pieces(3), whole), 1,
+                out_weight, info, q5, g5, lse, delta, column, acc, attn, pinned=1,
+                scratch=[pltpu.VMEM((out_weight.shape[0], part), BF16), pltpu.SemaphoreType.DMA],
             ),
             returned[1], returned[2], returned[3], up, down,
         )

time: 84 us -> 83.6 us (level)
  transfers between devices with their start and end apart: 21 -> 21, of which waited for: 11 -> 11; matrix products, arithmetic and copies ran while one was open for 3% -> 3% of each run, Pallas kernels for 33% -> 34%
where the time goes in v5:
time: 83.6 us; the launch traced here: 83 us
  Pallas kernels  29.5 us (35%)
  starting transfers between devices  26.2 us (31%)
  waiting for transfers between devices  22.4 us (27%)
  other arithmetic  3 us (4%)
  between operations  0.94 us (1%)
  local copies, waits for them, and re-layouts  0.85 us (1%)
    pallas_call x8, Pallas kernels, call(): pl.pallas_call(body, out_shape=outs, in_specs=[anywhere] * loose + [fixed...  29.5 us
    ppermute x13, waiting for transfers between devices, move(): return lax.ppermute(value, 'dp', shift(dy, dz, flip))  18.2 us
    ppermute x13, starting transfers between devices, move(): return lax.ppermute(value, 'dp', shift(dy, dz, flip))  16.5 us
    ppermute x8, starting transfers between devices, move_x(): return lax.ppermute(value, 'mp', [(x, (x + dx) % NX) for x in range(NX)])  9.76 us
    ppermute x8, waiting for transfers between devices, move_x(): return lax.ppermute(value, 'mp', [(x, (x + dx) % NX) for x in range(NX)])  4.22 us
  transfers between devices with their start and end apart: 21, of which 11 were waited for; matrix products, arithmetic and copies ran while one was open for 3% of the time, Pallas kernels for 34%

profile of v5, /device:TPU:14, one launch (start us, length us, event | category | flops | bytes accessed | tf_op | source)
XLA Modules:
  0.0 83.0 jit_solution(16152419887437111519)
XLA Ops:
  0.6 1.6 %shard_map.93 = bf16[240,256]{1,0:T(8,128)(2,1)} custom-call(s32[1,224]{1,0:T(1,128)} %bitcast.28, bf16[224,128]{1,0:T(8,128)(2,1)} %keys.1, bf16[224,128]{1,0:T(8,128)(2,1)} %values.1), custom_call_target="tpu_custom_call" | custom-call | flops 1152999936 | tf_op jit(solution)/shard_map/pallas_call | solution.py:339
  2.2 1.6 %collective-permute-start = (bf16[240,256]{1,0:T(8,128)(2,1)}, bf16[240,256]{1,0:T(8,128)(2,1)S(1)}, u32[]{:S(2)}, u32[]{:S(2)}) collective-permute-start(bf16[240,256]{1,0:T(8,128)(2,1)} %shard_map.93), channel_id=1, source_target_pairs={{0,32},{4,36},{8,40},{12,44},{16,48},{20,52},{24,56},{28,60},{32,6... | collective-permute-start | bytes 368648 | tf_op jit(solution)/shard_map/ppermute | solution.py:39
  5.2 1.6 %collective-permute-start.6 = (bf16[224,1280]{1,0:T(8,128)(2,1)S(1)}, bf16[224,1280]{1,0:T(8,128)(2,1)S(1)}, u32[]{:S(2)}, u32[]{:S(2)}) collective-permute-start(bf16[224,1280]{1,0:T(8,128)(2,1)S(1)} %copy-done.1), channel_id=1, source_target_pairs={{0,3},{1,0},{2,1},{3,2},{4,7},{5,4},{6,5},{7,6},{8,11},{9,8},{10,9... | collective-permute-start | bytes 1720328 | tf_op jit(solution)/shard_map/ppermute | solution.py:43
  7.6 2.9 %collective-permute-done.1 = bf16[240,256]{1,0:T(8,128)(2,1)S(1)} collective-permute-done((bf16[240,256]{1,0:T(8,128)(2,1)}, bf16[240,256]{1,0:T(8,128)(2,1)S(1)}, u32[]{:S(2)}, u32[]{:S(2)}) %collective-permute-start.1) | collective-permute-done | bytes 122912 | tf_op jit(solution)/shard_map/ppermute | solution.py:39
  11.7 2.0 %collective-permute-start.2 = (bf16[2,240,256]{2,1,0:T(8,128)(2,1)S(1)}, bf16[2,240,256]{2,1,0:T(8,128)(2,1)S(1)}, u32[]{:S(2)}, u32[]{:S(2)}) collective-permute-start(bf16[2,240,256]{2,1,0:T(8,128)(2,1)S(1)} %get-tuple-element.131), channel_id=1, source_target_pairs={{0,8},{4,12},{8,16},{12,20},{16,24},{20,28},{24,0},{28,4},{32,40},... | collective-permute-start | bytes 737288 | tf_op jit(solution)/shard_map/ppermute | solution.py:39
  13.7 3.6 %collective-permute-start.3 = (bf16[2,240,256]{2,1,0:T(8,128)(2,1)S(1)}, bf16[2,240,256]{2,1,0:T(8,128)(2,1)S(1)}, u32[]{:S(2)}, u32[]{:S(2)}) collective-permute-start(bf16[2,240,256]{2,1,0:T(8,128)(2,1)S(1)} %get-tuple-element.130), channel_id=1, source_target_pairs={{0,16},{4,20},{8,24},{12,28},{16,0},{20,4},{24,8},{28,12},{32,48},... | collective-permute-start | bytes 737288 | tf_op jit(solution)/shard_map/ppermute | solution.py:39
  18.3 1.9 %shard_map.94 = (f32[1,1152]{1,0:T(1,128)S(1)}, f32[1,1152]{1,0:T(1,128)S(1)}, f32[128,1152]{1,0:T(8,128)S(1)}, bf16[1152,128]{1,0:T(8,128)(2,1)S(1)}, f32[8,1152]{1,0:T(8,128)S(1)}) custom-call(bf16[224,640]{1,0:T(8,128)(2,1)S(1)} %copy-done.2, bf16[3,240,256]{2,1,0:T(8,128)(2,1)S(1)} %pad_maximum_fusion.2.refs_1_.refs_6_), custom_call_target="tpu_custom_call" | custom-call | flops 1152999936 | tf_op jit(solution)/shard_map/pallas_call | solution.py:339
  20.6 3.1 %shard_map.95.refs_3_ = f32[224,640]{1,0:T(8,128)S(1)} custom-call(bf16[224,1280]{1,0:T(8,128)(2,1)S(1)} %copy-done.1, bf16[224,1280]{1,0:T(8,128)(2,1)S(1)} %collective-permute-done.5.g1, bf16[224,1280]{1,0:T(8,128)(2,1)S(1)} %collective-permute-done.6.g3, bf16[640,5120]{1,0:T(8,128)(2,1)S(1)} %copy-done), custom_call_target="tpu_custom_call" | custom-call | flops 3459000064 | tf_op jit(solution)/shard_map/pallas_call | solution.py:339
  23.7 3.0 %collective-permute-done.3 = bf16[2,240,256]{2,1,0:T(8,128)(2,1)S(1)} collective-permute-done((bf16[2,240,256]{2,1,0:T(8,128)(2,1)S(1)}, bf16[2,240,256]{2,1,0:T(8,128)(2,1)S(1)}, u32[]{:S(2)}, u32[]{:S(2)}) %collective-permute-start.3) | collective-permute-done | bytes 245792 | tf_op jit(solution)/shard_map/ppermute | solution.py:39
  27.6 1.8 %collective-permute-start.9 = (bf16[112,1280]{1,0:T(8,128)(2,1)S(1)}, bf16[112,1280]{1,0:T(8,128)(2,1)S(1)}, u32[]{:S(2)}, u32[]{:S(2)}) collective-permute-start(bf16[112,1280]{1,0:T(8,128)(2,1)S(1)} %slice.85), channel_id=1, source_target_pairs={{0,3},{1,0},{2,1},{3,2},{4,7},{5,4},{6,5},{7,6},{8,11},{9,8},{10,9... | collective-permute-start | bytes 860168 | tf_op jit(solution)/shard_map/ppermute | solution.py:43
  29.4 2.8 %shard_map.96 = (f32[1,1152]{1,0:T(1,128)S(1)}, f32[1,1152]{1,0:T(1,128)S(1)}, f32[128,1152]{1,0:T(8,128)S(1)}) custom-call(f32[8,1152]{1,0:T(8,128)S(1)} %get-tuple-element.65.refs_0_.refs_1_, bf16[1152,128]{1,0:T(8,128)(2,1)S(1)} %get-tuple-element.66.refs_1_.refs_2_, bf16[9,240,256]{2,1,0:T(8,128)(2,1)S(1)} %constant_dynamic-update-slice_fusion.refs_2_.refs_8_.refs_5_, ...), custom_call_target="tpu_custom_call" | custom-call | flops 4611999744 | tf_op jit(solution)/shard_map/pallas_call | solution.py:339
  32.2 5.7 %shard_map.97 = (f32[1,1152]{1,0:T(1,128)S(1)}, bf16[128,1152]{1,0:T(8,128)(2,1)S(1)}, bf16[224,640]{1,0:T(8,128)(2,1)S(1)}, bf16[224,1280]{1,0:T(8,128)(2,1)S(1...) custom-call(bf16[640,5120]{1,0:T(8,128)(2,1)S(1)} %copy-done, ...), custom_call_target="tpu_custom_call" | custom-call | flops 1152999936 | tf_op jit(solution)/shard_map/pallas_call | solution.py:339
  38.0 1.7 %collective-permute-start.10 = (bf16[112,1280]{1,0:T(8,128)(2,1)S(1)}, bf16[112,1280]{1,0:T(8,128)(2,1)S(1)}, u32[]{:S(2)}, u32[]{:S(2)}) collective-permute-start(bf16[112,1280]{1,0:T(8,128)(2,1)S(1)} %get-tuple-element.94), channel_id=1, source_target_pairs={{0,1},{1,2},{2,3},{3,0},{4,5},{5,6},{6,7},{7,4},{8,9},{9,10},{10,1... | collective-permute-start | bytes 860168 | tf_op jit(solution)/shard_map/ppermute | solution.py:43
  40.0 7.6 %shard_map.98 = (f32[128,1152]{1,0:T(8,128)S(1)}, bf16[4,224,256]{2,1,0:T(8,128)(2,1)S(1)}, bf16[7,224,256]{2,1,0:T(8,128)(2,1)S(1)}, bf16[1152,128]{1,0:T(8,128)(2,1)S(1)}, f32[1,1152]{1,0:T(1,128)S(1)}) custom-call(bf16[640,5120]{1,0:T(8,128)(2,1)S(1)} %copy-done, f32[8,1152]{1,0:T(8,128)S(1)} %get-tuple-element.65.refs_0_.refs_1_, ...), custom_call_target="tpu_custom_call" | custom-call | flops 9223999488 | tf_op jit(solution)/shard_map/pallas_call | solution.py:339
  49.7 3.3 %collective-permute-start.17 = (bf16[224,1280]{1,0:T(8,128)(2,1)S(1)}, bf16[224,1280]{1,0:T(8,128)(2,1)S(1)}, u32[]{:S(2)}, u32[]{:S(2)}) collective-permute-start(bf16[224,1280]{1,0:T(8,128)(2,1)S(1)} %pad_maximum_fusion), channel_id=1, source_target_pairs={{0,1},{1,2},{2,3},{3,0},{4,5},{5,6},{6,7},{7,4},{8,9},{9,10},{10,1... | collective-permute-start | bytes 1720328 | tf_op jit(solution)/shard_map/ppermute | solution.py:43
  53.0 2.8 %shard_map.99 = (f32[128,1152]{1,0:T(8,128)S(1)}, bf16[2,224,256]{2,1,0:T(8,128)(2,1)S(1)}, bf16[2,224,256]{2,1,0:T(8,128)(2,1)S(1)}) custom-call(f32[8,1152]{1,0:T(8,128)S(1)} %get-tuple-element.65.refs_0_.refs_1_, bf16[1152,128]{1,0:T(8,128)(2,1)S(1)} %get-tuple-element.66.refs_1_.refs_2_, bf16[1152,128]{1,0:T(8,128)(2,1)S(1)} %get-tuple-element.96.refs_2_.refs_3_, ...), custom_call_target="tpu_custom_call" | custom-call | flops 8071000064 | tf_op jit(solution)/shard_map/pallas_call | solution.py:339
  56.1 2.2 %collective-permute-start.13 = (bf16[2,224,256]{2,1,0:T(8,128)(2,1)S(1)}, bf16[2,224,256]{2,1,0:T(8,128)(2,1)S(1)}, u32[]{:S(2)}, u32[]{:S(2)}) collective-permute-start(bf16[2,224,256]{2,1,0:T(8,128)(2,1)S(1)} %get-tuple-element.125), channel_id=1, source_target_pairs={{0,24},{4,28},{8,0},{12,4},{16,8},{20,12},{24,16},{28,20},{32,56},... | collective-permute-start | bytes 688136 | tf_op jit(solution)/shard_map/ppermute | solution.py:39
  59.9 3.9 %shard_map.100 = (bf16[224,640]{1,0:T(8,128)(2,1)}, bf16[3,224,256]{2,1,0:T(8,128)(2,1)S(1)}, bf16[224,1280]{1,0:T(8,128)(2,1)S(1)}) custom-call(bf16[640,5120]{1,0:T(8,128)(2,1)S(1)} %copy-done, f32[8,1152]{1,0:T(8,128)S(1)} %get-tuple-element.65.refs_0_.refs_1_, bf16[1152,128]{1,0:T(8,128)(2,1)S(1)} %get-tuple-element.66.refs_1_.refs_2_, ...), custom_call_target="tpu_custom_call" | custom-call | flops 1152999936 | tf_op jit(solution)/shard_map/pallas_call | solution.py:339
  63.9 2.2 %collective-permute-done.18 = bf16[224,1280]{1,0:T(8,128)(2,1)S(1)} collective-permute-done((bf16[224,1280]{1,0:T(8,128)(2,1)S(1)}, bf16[224,1280]{1,0:T(8,128)(2,1)S(1)}, u32[]{:S(2)}, u32[]{:S(2)}) %collective-permute-start.18) | collective-permute-done | bytes 573472 | tf_op jit(solution)/shard_map/ppermute | solution.py:43
  66.1 2.6 %collective-permute-done.13 = bf16[2,224,256]{2,1,0:T(8,128)(2,1)S(1)} collective-permute-done((bf16[2,224,256]{2,1,0:T(8,128)(2,1)S(1)}, bf16[2,224,256]{2,1,0:T(8,128)(2,1)S(1)}, u32[]{:S(2)}, u32[]{:S(2)}) %collective-permute-start.13) | collective-permute-done | bytes 229408 | tf_op jit(solution)/shard_map/ppermute | solution.py:39
  68.8 3.7 %collective-permute-done.16 = bf16[2,224,256]{2,1,0:T(8,128)(2,1)S(1)} collective-permute-done((bf16[2,224,256]{2,1,0:T(8,128)(2,1)S(1)}, bf16[2,224,256]{2,1,0:T(8,128)(2,1)S(1)}, u32[]{:S(2)}, u32[]{:S(2)}) %collective-permute-start.16) | collective-permute-done | bytes 229408 | tf_op jit(solution)/shard_map/ppermute | solution.py:39
  72.7 3.3 %collective-permute-start.19 = (bf16[224,256]{1,0:T(8,128)(2,1)S(1)}, bf16[224,256]{1,0:T(8,128)(2,1)S(1)}, u32[]{:S(2)}, u32[]{:S(2)}) collective-permute-start(bf16[224,256]{1,0:T(8,128)(2,1)S(1)} %get-tuple-element.122), channel_id=1, source_target_pairs={{0,96},{4,100},{8,104},{12,108},{16,112},{20,116},{24,120},{28,124... | collective-permute-start | bytes 344072 | tf_op jit(solution)/shard_map/ppermute | solution.py:39
  77.0 2.5 %collective-permute-done.19 = bf16[224,256]{1,0:T(8,128)(2,1)S(1)} collective-permute-done((bf16[224,256]{1,0:T(8,128)(2,1)S(1)}, bf16[224,256]{1,0:T(8,128)(2,1)S(1)}, u32[]{:S(2)}, u32[]{:S(2)}) %collective-permute-start.19) | collective-permute-done | bytes 114720 | tf_op jit(solution)/shard_map/ppermute | solution.py:39
  79.5 2.8 %collective-permute-done.20 = bf16[224,256]{1,0:T(8,128)(2,1)S(1)} collective-permute-done((bf16[224,256]{1,0:T(8,128)(2,1)S(1)}, bf16[224,256]{1,0:T(8,128)(2,1)S(1)}, u32[]{:S(2)}, u32[]{:S(2)}) %collective-permute-start.20) | collective-permute-done | bytes 114720 | tf_op jit(solution)/shard_map/ppermute | solution.py:39
  (60 shorter events, 11.7 us)
Async XLA Ops:
  2.2 5.3 %collective-permute-start = (bf16[240,256]{1,0:T(8,128)(2,1)}, bf16[240,256]{1,0:T(8,128)(2,1)S(1)}, u32[]{:S(2)}, u32[]{:S(2)}) collective-permute-start(bf16[240,256]{1,0:T(8,128)(2,1)} %shard_map.93), channel_id=1, source_target_pairs={{0,32},{4,36},{8,40},{12,44},{16,48},{20,52},{24,56},{28,60},{32,6... | collective-permute-start | bytes 368648 | tf_op jit(solution)/shard_map/ppermute | solution.py:39
  3.9 6.6 %collective-permute-start.1 = (bf16[240,256]{1,0:T(8,128)(2,1)}, bf16[240,256]{1,0:T(8,128)(2,1)S(1)}, u32[]{:S(2)}, u32[]{:S(2)}) collective-permute-start(bf16[240,256]{1,0:T(8,128)(2,1)} %shard_map.93), channel_id=1, source_target_pairs={{0,64},{4,68},{8,72},{12,76},{16,80},{20,84},{24,88},{28,92},{32,9... | collective-permute-start | bytes 368648 | tf_op jit(solution)/shard_map/ppermute | solution.py:39
  4.8 15.4 %collective-permute-start.5 = (bf16[224,1280]{1,0:T(8,128)(2,1)S(1)}, bf16[224,1280]{1,0:T(8,128)(2,1)S(1)}, u32[]{:S(2)}, u32[]{:S(2)}) collective-permute-start(bf16[224,1280]{1,0:T(8,128)(2,1)S(1)} %copy-done.1), channel_id=1, source_target_pairs={{0,1},{1,2},{2,3},{3,0},{4,5},{5,6},{6,7},{7,4},{8,9},{9,10},{10,1... | collective-permute-start | bytes 1720328 | tf_op jit(solution)/shard_map/ppermute | solution.py:43
  5.2 15.3 %collective-permute-start.6 = (bf16[224,1280]{1,0:T(8,128)(2,1)S(1)}, bf16[224,1280]{1,0:T(8,128)(2,1)S(1)}, u32[]{:S(2)}, u32[]{:S(2)}) collective-permute-start(bf16[224,1280]{1,0:T(8,128)(2,1)S(1)} %copy-done.1), channel_id=1, source_target_pairs={{0,3},{1,0},{2,1},{3,2},{4,7},{5,4},{6,5},{7,6},{8,11},{9,8},{10,9... | collective-permute-start | bytes 1720328 | tf_op jit(solution)/shard_map/ppermute | solution.py:43
  6.9 11.4 %copy-start.3 = (bf16[240,256]{1,0:T(8,128)(2,1)S(1)}, bf16[240,256]{1,0:T(8,128)(2,1)}, u32[]{:S(2)}) copy-start(bf16[240,256]{1,0:T(8,128)(2,1)} %shard_map.93) | copy-start | bytes 368644
  7.6 10.7 %copy-start.2 = (bf16[224,640]{1,0:T(8,128)(2,1)S(1)}, bf16[224,640]{1,0:T(8,128)(2,1)}, u32[]{:S(2)}) copy-start(bf16[224,640]{1,0:T(8,128)(2,1)} %refs_0_.4) | copy-start | bytes 860164
  10.5 10.1 %copy-start = (bf16[640,5120]{1,0:T(8,128)(2,1)S(1)}, bf16[640,5120]{1,0:T(8,128)(2,1)}, u32[]{:S(2)}) copy-start(bf16[640,5120]{1,0:T(8,128)(2,1)} %refs_0_.7) | copy-start | bytes 19660804
  11.7 12.0 %collective-permute-start.2 = (bf16[2,240,256]{2,1,0:T(8,128)(2,1)S(1)}, bf16[2,240,256]{2,1,0:T(8,128)(2,1)S(1)}, u32[]{:S(2)}, u32[]{:S(2)}) collective-permute-start(bf16[2,240,256]{2,1,0:T(8,128)(2,1)S(1)} %get-tuple-element.131), channel_id=1, source_target_pairs={{0,8},{4,12},{8,16},{12,20},{16,24},{20,28},{24,0},{28,4},{32,40},... | collective-permute-start | bytes 737288 | tf_op jit(solution)/shard_map/ppermute | solution.py:39
  13.7 13.1 %collective-permute-start.3 = (bf16[2,240,256]{2,1,0:T(8,128)(2,1)S(1)}, bf16[2,240,256]{2,1,0:T(8,128)(2,1)S(1)}, u32[]{:S(2)}, u32[]{:S(2)}) collective-permute-start(bf16[2,240,256]{2,1,0:T(8,128)(2,1)S(1)} %get-tuple-element.130), channel_id=1, source_target_pairs={{0,16},{4,20},{8,24},{12,28},{16,0},{20,4},{24,8},{28,12},{32,48},... | collective-permute-start | bytes 737288 | tf_op jit(solution)/shard_map/ppermute | solution.py:39
  17.2 9.5 %collective-permute-start.4 = (bf16[2,240,256]{2,1,0:T(8,128)(2,1)S(1)}, bf16[2,240,256]{2,1,0:T(8,128)(2,1)S(1)}, u32[]{:S(2)}, u32[]{:S(2)}) collective-permute-start(bf16[2,240,256]{2,1,0:T(8,128)(2,1)S(1)} %get-tuple-element.129), channel_id=1, source_target_pairs={{0,24},{4,28},{8,0},{12,4},{16,8},{20,12},{24,16},{28,20},{32,56},... | collective-permute-start | bytes 737288 | tf_op jit(solution)/shard_map/ppermute | solution.py:39
  26.9 5.3 %collective-permute-start.7 = (bf16[9,240,256]{2,1,0:T(8,128)(2,1)S(1)}, bf16[9,240,256]{2,1,0:T(8,128)(2,1)S(1)}, u32[]{:S(2)}, u32[]{:S(2)}) collective-permute-start(bf16[9,240,256]{2,1,0:T(8,128)(2,1)S(1)} %constant_dynamic-update-slice_fusion.refs_2_.refs_8_.refs_5_), channel_id=1, source_target_pairs={{0,4},{4,0},{8,12},{12,8},{16,20},{20,16},{24,28},{28,24},{32,36},... | collective-permute-start | bytes 3317768 | tf_op jit(solution)/shard_map/ppermute | solution.py:39
  27.0 10.9 %collective-permute-start.8 = (bf16[112,1280]{1,0:T(8,128)(2,1)S(1)}, bf16[112,1280]{1,0:T(8,128)(2,1)S(1)}, u32[]{:S(2)}, u32[]{:S(2)}) collective-permute-start(bf16[112,1280]{1,0:T(8,128)(2,1)S(1)} %slice.84), channel_id=1, source_target_pairs={{0,1},{1,2},{2,3},{3,0},{4,5},{5,6},{6,7},{7,4},{8,9},{9,10},{10,1... | collective-permute-start | bytes 860168 | tf_op jit(solution)/shard_map/ppermute | solution.py:43
  27.6 10.4 %collective-permute-start.9 = (bf16[112,1280]{1,0:T(8,128)(2,1)S(1)}, bf16[112,1280]{1,0:T(8,128)(2,1)S(1)}, u32[]{:S(2)}, u32[]{:S(2)}) collective-permute-start(bf16[112,1280]{1,0:T(8,128)(2,1)S(1)} %slice.85), channel_id=1, source_target_pairs={{0,3},{1,0},{2,1},{3,2},{4,7},{5,4},{6,5},{7,6},{8,11},{9,8},{10,9... | collective-permute-start | bytes 860168 | tf_op jit(solution)/shard_map/ppermute | solution.py:43
  38.0 9.7 %collective-permute-start.10 = (bf16[112,1280]{1,0:T(8,128)(2,1)S(1)}, bf16[112,1280]{1,0:T(8,128)(2,1)S(1)}, u32[]{:S(2)}, u32[]{:S(2)}) collective-permute-start(bf16[112,1280]{1,0:T(8,128)(2,1)S(1)} %get-tuple-element.94), channel_id=1, source_target_pairs={{0,1},{1,2},{2,3},{3,0},{4,5},{5,6},{6,7},{7,4},{8,9},{9,10},{10,1... | collective-permute-start | bytes 860168 | tf_op jit(solution)/shard_map/ppermute | solution.py:43
  39.7 9.6 %collective-permute-start.11 = (bf16[112,1280]{1,0:T(8,128)(2,1)S(1)}, bf16[112,1280]{1,0:T(8,128)(2,1)S(1)}, u32[]{:S(2)}, u32[]{:S(2)}) collective-permute-start(bf16[112,1280]{1,0:T(8,128)(2,1)S(1)} %get-tuple-element.95), channel_id=1, source_target_pairs={{0,3},{1,0},{2,1},{3,2},{4,7},{5,4},{6,5},{7,6},{8,11},{9,8},{10,9... | collective-permute-start | bytes 860168 | tf_op jit(solution)/shard_map/ppermute | solution.py:43
  49.3 3.6 %collective-permute-start.12 = (bf16[7,224,256]{2,1,0:T(8,128)(2,1)S(1)}, bf16[7,224,256]{2,1,0:T(8,128)(2,1)S(1)}, u32[]{:S(2)}, u32[]{:S(2)}) collective-permute-start(bf16[7,224,256]{2,1,0:T(8,128)(2,1)S(1)} %get-tuple-element.99), channel_id=1, source_target_pairs={{0,4},{4,0},{8,12},{12,8},{16,20},{20,16},{24,28},{28,24},{32,36},... | collective-permute-start | bytes 2408456 | tf_op jit(solution)/shard_map/ppermute | solution.py:39
  49.5 16.7 %collective-permute-start.18 = (bf16[224,1280]{1,0:T(8,128)(2,1)S(1)}, bf16[224,1280]{1,0:T(8,128)(2,1)S(1)}, u32[]{:S(2)}, u32[]{:S(2)}) collective-permute-start(bf16[224,1280]{1,0:T(8,128)(2,1)S(1)} %pad_maximum_fusion.1), channel_id=1, source_target_pairs={{0,3},{1,0},{2,1},{3,2},{4,7},{5,4},{6,5},{7,6},{8,11},{9,8},{10,9... | collective-permute-start | bytes 1720328 | tf_op jit(solution)/shard_map/ppermute | solution.py:43
  49.7 16.4 %collective-permute-start.17 = (bf16[224,1280]{1,0:T(8,128)(2,1)S(1)}, bf16[224,1280]{1,0:T(8,128)(2,1)S(1)}, u32[]{:S(2)}, u32[]{:S(2)}) collective-permute-start(bf16[224,1280]{1,0:T(8,128)(2,1)S(1)} %pad_maximum_fusion), channel_id=1, source_target_pairs={{0,1},{1,2},{2,3},{3,0},{4,5},{5,6},{6,7},{7,4},{8,9},{9,10},{10,1... | collective-permute-start | bytes 1720328 | tf_op jit(solution)/shard_map/ppermute | solution.py:43
  55.8 3.6 %collective-permute-start.15 = (bf16[2,224,256]{2,1,0:T(8,128)(2,1)S(1)}, bf16[2,224,256]{2,1,0:T(8,128)(2,1)S(1)}, u32[]{:S(2)}, u32[]{:S(2)}) collective-permute-start(bf16[2,224,256]{2,1,0:T(8,128)(2,1)S(1)} %get-tuple-element.109), channel_id=1, source_target_pairs={{0,4},{4,0},{8,12},{12,8},{16,20},{20,16},{24,28},{28,24},{32,36},... | collective-permute-start | bytes 688136 | tf_op jit(solution)/shard_map/ppermute | solution.py:39
  56.1 12.7 %collective-permute-start.13 = (bf16[2,224,256]{2,1,0:T(8,128)(2,1)S(1)}, bf16[2,224,256]{2,1,0:T(8,128)(2,1)S(1)}, u32[]{:S(2)}, u32[]{:S(2)}) collective-permute-start(bf16[2,224,256]{2,1,0:T(8,128)(2,1)S(1)} %get-tuple-element.125), channel_id=1, source_target_pairs={{0,24},{4,28},{8,0},{12,4},{16,8},{20,12},{24,16},{28,20},{32,56},... | collective-permute-start | bytes 688136 | tf_op jit(solution)/shard_map/ppermute | solution.py:39
  58.3 10.5 %collective-permute-start.14 = (bf16[2,224,256]{2,1,0:T(8,128)(2,1)S(1)}, bf16[2,224,256]{2,1,0:T(8,128)(2,1)S(1)}, u32[]{:S(2)}, u32[]{:S(2)}) collective-permute-start(bf16[2,224,256]{2,1,0:T(8,128)(2,1)S(1)} %get-tuple-element.124), channel_id=1, source_target_pairs={{0,16},{4,20},{8,24},{12,28},{16,0},{20,4},{24,8},{28,12},{32,48},... | collective-permute-start | bytes 688136 | tf_op jit(solution)/shard_map/ppermute | solution.py:39
  59.5 12.9 %collective-permute-start.16 = (bf16[2,224,256]{2,1,0:T(8,128)(2,1)S(1)}, bf16[2,224,256]{2,1,0:T(8,128)(2,1)S(1)}, u32[]{:S(2)}, u32[]{:S(2)}) collective-permute-start(bf16[2,224,256]{2,1,0:T(8,128)(2,1)S(1)} %add_convert_fusion.4), channel_id=1, source_target_pairs={{0,8},{4,12},{8,16},{12,20},{16,24},{20,28},{24,0},{28,4},{32,40},... | collective-permute-start | bytes 688136 | tf_op jit(solution)/shard_map/ppermute | solution.py:39
  72.7 6.8 %collective-permute-start.19 = (bf16[224,256]{1,0:T(8,128)(2,1)S(1)}, bf16[224,256]{1,0:T(8,128)(2,1)S(1)}, u32[]{:S(2)}, u32[]{:S(2)}) collective-permute-start(bf16[224,256]{1,0:T(8,128)(2,1)S(1)} %get-tuple-element.122), channel_id=1, source_target_pairs={{0,96},{4,100},{8,104},{12,108},{16,112},{20,116},{24,120},{28,124... | collective-permute-start | bytes 344072 | tf_op jit(solution)/shard_map/ppermute | solution.py:39
  75.9 6.3 %collective-permute-start.20 = (bf16[224,256]{1,0:T(8,128)(2,1)S(1)}, bf16[224,256]{1,0:T(8,128)(2,1)S(1)}, u32[]{:S(2)}, u32[]{:S(2)}) collective-permute-start(bf16[224,256]{1,0:T(8,128)(2,1)S(1)} %get-tuple-element.123), channel_id=1, source_target_pairs={{0,64},{4,68},{8,72},{12,76},{16,80},{20,84},{24,88},{28,92},{32,9... | collective-permute-start | bytes 344072 | tf_op jit(solution)/shard_map/ppermute | solution.py:39
  (1 other events, 4.2 us)

commit v6 on v5

--- a/solution.py
+++ b/solution.py
@@ -419,10 +419,14 @@
     up = jnp.concatenate([add_up(up[:half], early[0]).astype(BF16), up[half:]], axis=0)
     down = jnp.concatenate([down[:half], add_up(down[half:], early[1]).astype(BF16)], axis=0)
     other = move(leave, flip=1)
-    acc, other = lax.optimization_barrier((acc, other))
-    acc, stay_last, leave_last = call(
-        lambda *refs: backward_second(rows, factor, scale, *refs),
-        (square, pieces(2), pieces(2)), 7, info, q5, g5, lse, delta, side, side_other, acc,
+    acc, stay_last, leave_last, other = lax.optimization_barrier(
+        (
+            *call(
+                lambda *refs: backward_second(rows, factor, scale, *refs),
+                (square, pieces(2), pieces(2)), 3, info, q5, g5, lse, delta, side, side_other, acc,
+            ),
+            other,
+        )
     )
     other_last = move(leave_last, flip=1)
     mixed = add_up(stay, other[:4]).astype(BF16)
@@ -433,7 +437,7 @@
         (
             *call(
                 lambda *refs: backward_column(rows, factor, scale, *refs),
-                (shape(rows, GROUP * HD), pieces(3), whole), 1,
+                (shape(rows, GROUP * HD), pieces(3), whole), 3,
                 out_weight, info, q5, g5, lse, delta, column, acc, attn, pinned=1,
                 scratch=[pltpu.VMEM((out_weight.shape[0], part), BF16), pltpu.SemaphoreType.DMA],
             ),

time: 83.6 us -> 83.4 us (level)
  transfers between devices with their start and end apart: 21 -> 21, of which waited for: 11 -> 12; matrix products, arithmetic and copies ran while one was open for 3% -> 3% of each run, Pallas kernels for 34% -> 34%
where the time goes in v6:
time: 83.4 us; the launch traced here: 82.9 us
  Pallas kernels  29.5 us (35%)
  starting transfers between devices  26.4 us (32%)
  waiting for transfers between devices  22.2 us (27%)
  other arithmetic  2.98 us (4%)
  between operations  0.94 us (1%)
  local copies, waits for them, and re-layouts  0.85 us (1%)
    pallas_call x8, Pallas kernels, call(): pl.pallas_call(body, out_shape=outs, in_specs=[anywhere] * loose + [fixed...  29.5 us
    ppermute x13, waiting for transfers between devices, move(): return lax.ppermute(value, 'dp', shift(dy, dz, flip))  18.5 us
    ppermute x13, starting transfers between devices, move(): return lax.ppermute(value, 'dp', shift(dy, dz, flip))  16.7 us
    ppermute x8, starting transfers between devices, move_x(): return lax.ppermute(value, 'mp', [(x, (x + dx) % NX) for x in range(NX)])  9.67 us
    ppermute x8, waiting for transfers between devices, move_x(): return lax.ppermute(value, 'mp', [(x, (x + dx) % NX) for x in range(NX)])  3.78 us
  transfers between devices with their start and end apart: 21, of which 12 were waited for; matrix products, arithmetic and copies ran while one was open for 3% of the time, Pallas kernels for 34%

profile of v6, /device:TPU:14, one launch (start us, length us, event | category | flops | bytes accessed | tf_op | source)
XLA Modules:
  0.0 82.9 jit_solution(12615126820017910992)
XLA Ops:
  0.6 1.6 %shard_map.93 = bf16[240,256]{1,0:T(8,128)(2,1)} custom-call(s32[1,224]{1,0:T(1,128)} %bitcast.28, bf16[224,128]{1,0:T(8,128)(2,1)} %keys.1, bf16[224,128]{1,0:T(8,128)(2,1)} %values.1), custom_call_target="tpu_custom_call" | custom-call | flops 1152999936 | tf_op jit(solution)/shard_map/pallas_call | solution.py:339
  2.2 1.6 %collective-permute-start = (bf16[240,256]{1,0:T(8,128)(2,1)}, bf16[240,256]{1,0:T(8,128)(2,1)S(1)}, u32[]{:S(2)}, u32[]{:S(2)}) collective-permute-start(bf16[240,256]{1,0:T(8,128)(2,1)} %shard_map.93), channel_id=1, source_target_pairs={{0,32},{4,36},{8,40},{12,44},{16,48},{20,52},{24,56},{28,60},{32,6... | collective-permute-start | bytes 368648 | tf_op jit(solution)/shard_map/ppermute | solution.py:39
  5.2 1.6 %collective-permute-start.6 = (bf16[224,1280]{1,0:T(8,128)(2,1)S(1)}, bf16[224,1280]{1,0:T(8,128)(2,1)S(1)}, u32[]{:S(2)}, u32[]{:S(2)}) collective-permute-start(bf16[224,1280]{1,0:T(8,128)(2,1)S(1)} %copy-done.1), channel_id=1, source_target_pairs={{0,3},{1,0},{2,1},{3,2},{4,7},{5,4},{6,5},{7,6},{8,11},{9,8},{10,9... | collective-permute-start | bytes 1720328 | tf_op jit(solution)/shard_map/ppermute | solution.py:43
  7.6 2.9 %collective-permute-done.1 = bf16[240,256]{1,0:T(8,128)(2,1)S(1)} collective-permute-done((bf16[240,256]{1,0:T(8,128)(2,1)}, bf16[240,256]{1,0:T(8,128)(2,1)S(1)}, u32[]{:S(2)}, u32[]{:S(2)}) %collective-permute-start.1) | collective-permute-done | bytes 122912 | tf_op jit(solution)/shard_map/ppermute | solution.py:39
  11.7 2.0 %collective-permute-start.2 = (bf16[2,240,256]{2,1,0:T(8,128)(2,1)S(1)}, bf16[2,240,256]{2,1,0:T(8,128)(2,1)S(1)}, u32[]{:S(2)}, u32[]{:S(2)}) collective-permute-start(bf16[2,240,256]{2,1,0:T(8,128)(2,1)S(1)} %get-tuple-element.135), channel_id=1, source_target_pairs={{0,8},{4,12},{8,16},{12,20},{16,24},{20,28},{24,0},{28,4},{32,40},... | collective-permute-start | bytes 737288 | tf_op jit(solution)/shard_map/ppermute | solution.py:39
  13.7 3.6 %collective-permute-start.3 = (bf16[2,240,256]{2,1,0:T(8,128)(2,1)S(1)}, bf16[2,240,256]{2,1,0:T(8,128)(2,1)S(1)}, u32[]{:S(2)}, u32[]{:S(2)}) collective-permute-start(bf16[2,240,256]{2,1,0:T(8,128)(2,1)S(1)} %get-tuple-element.134), channel_id=1, source_target_pairs={{0,16},{4,20},{8,24},{12,28},{16,0},{20,4},{24,8},{28,12},{32,48},... | collective-permute-start | bytes 737288 | tf_op jit(solution)/shard_map/ppermute | solution.py:39
  18.3 1.9 %shard_map.94 = (f32[1,1152]{1,0:T(1,128)S(1)}, f32[1,1152]{1,0:T(1,128)S(1)}, f32[128,1152]{1,0:T(8,128)S(1)}, bf16[1152,128]{1,0:T(8,128)(2,1)S(1)}, f32[8,1152]{1,0:T(8,128)S(1)}) custom-call(bf16[224,640]{1,0:T(8,128)(2,1)S(1)} %copy-done.2, bf16[3,240,256]{2,1,0:T(8,128)(2,1)S(1)} %pad_maximum_fusion.2.refs_1_.refs_6_), custom_call_target="tpu_custom_call" | custom-call | flops 1152999936 | tf_op jit(solution)/shard_map/pallas_call | solution.py:339
  20.6 3.1 %shard_map.95.refs_3_ = f32[224,640]{1,0:T(8,128)S(1)} custom-call(bf16[224,1280]{1,0:T(8,128)(2,1)S(1)} %copy-done.1, bf16[224,1280]{1,0:T(8,128)(2,1)S(1)} %collective-permute-done.5.g1, bf16[224,1280]{1,0:T(8,128)(2,1)S(1)} %collective-permute-done.6.g3, bf16[640,5120]{1,0:T(8,128)(2,1)S(1)} %copy-done), custom_call_target="tpu_custom_call" | custom-call | flops 3459000064 | tf_op jit(solution)/shard_map/pallas_call | solution.py:339
  23.7 3.0 %collective-permute-done.3 = bf16[2,240,256]{2,1,0:T(8,128)(2,1)S(1)} collective-permute-done((bf16[2,240,256]{2,1,0:T(8,128)(2,1)S(1)}, bf16[2,240,256]{2,1,0:T(8,128)(2,1)S(1)}, u32[]{:S(2)}, u32[]{:S(2)}) %collective-permute-start.3) | collective-permute-done | bytes 245792 | tf_op jit(solution)/shard_map/ppermute | solution.py:39
  27.6 1.8 %collective-permute-start.9 = (bf16[112,1280]{1,0:T(8,128)(2,1)S(1)}, bf16[112,1280]{1,0:T(8,128)(2,1)S(1)}, u32[]{:S(2)}, u32[]{:S(2)}) collective-permute-start(bf16[112,1280]{1,0:T(8,128)(2,1)S(1)} %slice.85), channel_id=1, source_target_pairs={{0,3},{1,0},{2,1},{3,2},{4,7},{5,4},{6,5},{7,6},{8,11},{9,8},{10,9... | collective-permute-start | bytes 860168 | tf_op jit(solution)/shard_map/ppermute | solution.py:43
  29.4 2.8 %shard_map.96 = (f32[1,1152]{1,0:T(1,128)S(1)}, f32[1,1152]{1,0:T(1,128)S(1)}, f32[128,1152]{1,0:T(8,128)S(1)}) custom-call(f32[8,1152]{1,0:T(8,128)S(1)} %get-tuple-element.67.refs_0_.refs_1_, bf16[1152,128]{1,0:T(8,128)(2,1)S(1)} %get-tuple-element.68.refs_1_.refs_2_, bf16[9,240,256]{2,1,0:T(8,128)(2,1)S(1)} %constant_dynamic-update-slice_fusion.refs_2_.refs_8_.refs_5_, ...), custom_call_target="tpu_custom_call" | custom-call | flops 4611999744 | tf_op jit(solution)/shard_map/pallas_call | solution.py:339
  32.2 5.7 %shard_map.97 = (f32[1,1152]{1,0:T(1,128)S(1)}, bf16[128,1152]{1,0:T(8,128)(2,1)S(1)}, bf16[224,640]{1,0:T(8,128)(2,1)S(1)}, bf16[224,1280]{1,0:T(8,128)(2,1)S(1...) custom-call(bf16[640,5120]{1,0:T(8,128)(2,1)S(1)} %copy-done, ...), custom_call_target="tpu_custom_call" | custom-call | flops 1152999936 | tf_op jit(solution)/shard_map/pallas_call | solution.py:339
  38.0 1.7 %collective-permute-start.10 = (bf16[112,1280]{1,0:T(8,128)(2,1)S(1)}, bf16[112,1280]{1,0:T(8,128)(2,1)S(1)}, u32[]{:S(2)}, u32[]{:S(2)}) collective-permute-start(bf16[112,1280]{1,0:T(8,128)(2,1)S(1)} %get-tuple-element.96), channel_id=1, source_target_pairs={{0,1},{1,2},{2,3},{3,0},{4,5},{5,6},{6,7},{7,4},{8,9},{9,10},{10,1... | collective-permute-start | bytes 860168 | tf_op jit(solution)/shard_map/ppermute | solution.py:43
  40.0 7.6 %shard_map.98 = (f32[128,1152]{1,0:T(8,128)S(1)}, bf16[4,224,256]{2,1,0:T(8,128)(2,1)S(1)}, bf16[7,224,256]{2,1,0:T(8,128)(2,1)S(1)}, bf16[1152,128]{1,0:T(8,128)(2,1)S(1)}, f32[1,1152]{1,0:T(1,128)S(1)}) custom-call(bf16[640,5120]{1,0:T(8,128)(2,1)S(1)} %copy-done, f32[8,1152]{1,0:T(8,128)S(1)} %get-tuple-element.67.refs_0_.refs_1_, ...), custom_call_target="tpu_custom_call" | custom-call | flops 9223999488 | tf_op jit(solution)/shard_map/pallas_call | solution.py:339
  47.7 1.5 %collective-permute-done.11 = bf16[112,1280]{1,0:T(8,128)(2,1)S(1)} collective-permute-done((bf16[112,1280]{1,0:T(8,128)(2,1)S(1)}, bf16[112,1280]{1,0:T(8,128)(2,1)S(1)}, u32[]{:S(2)}, u32[]{:S(2)}) %collective-permute-start.11) | collective-permute-done | bytes 286752 | tf_op jit(solution)/shard_map/ppermute | solution.py:43
  49.7 3.2 %collective-permute-start.17 = (bf16[224,1280]{1,0:T(8,128)(2,1)S(1)}, bf16[224,1280]{1,0:T(8,128)(2,1)S(1)}, u32[]{:S(2)}, u32[]{:S(2)}) collective-permute-start(bf16[224,1280]{1,0:T(8,128)(2,1)S(1)} %pad_maximum_fusion), channel_id=1, source_target_pairs={{0,1},{1,2},{2,3},{3,0},{4,5},{5,6},{6,7},{7,4},{8,9},{9,10},{10,1... | collective-permute-start | bytes 1720328 | tf_op jit(solution)/shard_map/ppermute | solution.py:43
  52.9 2.8 %shard_map.99 = (f32[128,1152]{1,0:T(8,128)S(1)}, bf16[2,224,256]{2,1,0:T(8,128)(2,1)S(1)}, bf16[2,224,256]{2,1,0:T(8,128)(2,1)S(1)}) custom-call(f32[8,1152]{1,0:T(8,128)S(1)} %get-tuple-element.67.refs_0_.refs_1_, bf16[1152,128]{1,0:T(8,128)(2,1)S(1)} %get-tuple-element.68.refs_1_.refs_2_, bf16[1152,128]{1,0:T(8,128)(2,1)S(1)} %get-tuple-element.98.refs_2_.refs_3_, ...), custom_call_target="tpu_custom_call" | custom-call | flops 3459000064 | tf_op jit(solution)/shard_map/pallas_call | solution.py:339
  56.2 2.2 %collective-permute-start.13 = (bf16[2,224,256]{2,1,0:T(8,128)(2,1)S(1)}, bf16[2,224,256]{2,1,0:T(8,128)(2,1)S(1)}, u32[]{:S(2)}, u32[]{:S(2)}) collective-permute-start(bf16[2,224,256]{2,1,0:T(8,128)(2,1)S(1)} %get-tuple-element.129), channel_id=1, source_target_pairs={{0,24},{4,28},{8,0},{12,4},{16,8},{20,12},{24,16},{28,20},{32,56},... | collective-permute-start | bytes 688136 | tf_op jit(solution)/shard_map/ppermute | solution.py:39
  60.0 3.9 %shard_map.100 = (bf16[224,640]{1,0:T(8,128)(2,1)}, bf16[3,224,256]{2,1,0:T(8,128)(2,1)S(1)}, bf16[224,1280]{1,0:T(8,128)(2,1)S(1)}) custom-call(bf16[640,5120]{1,0:T(8,128)(2,1)S(1)} %copy-done, f32[8,1152]{1,0:T(8,128)S(1)} %get-tuple-element.67.refs_0_.refs_1_, bf16[1152,128]{1,0:T(8,128)(2,1)S(1)} %get-tuple-element.68.refs_1_.refs_2_, ...), custom_call_target="tpu_custom_call" | custom-call | flops 3459000064 | tf_op jit(solution)/shard_map/pallas_call | solution.py:339
  65.8 2.9 %collective-permute-done.13 = bf16[2,224,256]{2,1,0:T(8,128)(2,1)S(1)} collective-permute-done((bf16[2,224,256]{2,1,0:T(8,128)(2,1)S(1)}, bf16[2,224,256]{2,1,0:T(8,128)(2,1)S(1)}, u32[]{:S(2)}, u32[]{:S(2)}) %collective-permute-start.13) | collective-permute-done | bytes 229408 | tf_op jit(solution)/shard_map/ppermute | solution.py:39
  68.7 3.7 %collective-permute-done.16 = bf16[2,224,256]{2,1,0:T(8,128)(2,1)S(1)} collective-permute-done((bf16[2,224,256]{2,1,0:T(8,128)(2,1)S(1)}, bf16[2,224,256]{2,1,0:T(8,128)(2,1)S(1)}, u32[]{:S(2)}, u32[]{:S(2)}) %collective-permute-start.16) | collective-permute-done | bytes 229408 | tf_op jit(solution)/shard_map/ppermute | solution.py:39
  72.6 3.3 %collective-permute-start.19 = (bf16[224,256]{1,0:T(8,128)(2,1)S(1)}, bf16[224,256]{1,0:T(8,128)(2,1)S(1)}, u32[]{:S(2)}, u32[]{:S(2)}) collective-permute-start(bf16[224,256]{1,0:T(8,128)(2,1)S(1)} %get-tuple-element.126), channel_id=1, source_target_pairs={{0,96},{4,100},{8,104},{12,108},{16,112},{20,116},{24,120},{28,124... | collective-permute-start | bytes 344072 | tf_op jit(solution)/shard_map/ppermute | solution.py:39
  76.8 2.5 %collective-permute-done.19 = bf16[224,256]{1,0:T(8,128)(2,1)S(1)} collective-permute-done((bf16[224,256]{1,0:T(8,128)(2,1)S(1)}, bf16[224,256]{1,0:T(8,128)(2,1)S(1)}, u32[]{:S(2)}, u32[]{:S(2)}) %collective-permute-start.19) | collective-permute-done | bytes 114720 | tf_op jit(solution)/shard_map/ppermute | solution.py:39
  79.3 2.8 %collective-permute-done.20 = bf16[224,256]{1,0:T(8,128)(2,1)S(1)} collective-permute-done((bf16[224,256]{1,0:T(8,128)(2,1)S(1)}, bf16[224,256]{1,0:T(8,128)(2,1)S(1)}, u32[]{:S(2)}, u32[]{:S(2)}) %collective-permute-start.20) | collective-permute-done | bytes 114720 | tf_op jit(solution)/shard_map/ppermute | solution.py:39
  (60 shorter events, 12.2 us)
Async XLA Ops:
  2.2 5.3 %collective-permute-start = (bf16[240,256]{1,0:T(8,128)(2,1)}, bf16[240,256]{1,0:T(8,128)(2,1)S(1)}, u32[]{:S(2)}, u32[]{:S(2)}) collective-permute-start(bf16[240,256]{1,0:T(8,128)(2,1)} %shard_map.93), channel_id=1, source_target_pairs={{0,32},{4,36},{8,40},{12,44},{16,48},{20,52},{24,56},{28,60},{32,6... | collective-permute-start | bytes 368648 | tf_op jit(solution)/shard_map/ppermute | solution.py:39
  3.9 6.6 %collective-permute-start.1 = (bf16[240,256]{1,0:T(8,128)(2,1)}, bf16[240,256]{1,0:T(8,128)(2,1)S(1)}, u32[]{:S(2)}, u32[]{:S(2)}) collective-permute-start(bf16[240,256]{1,0:T(8,128)(2,1)} %shard_map.93), channel_id=1, source_target_pairs={{0,64},{4,68},{8,72},{12,76},{16,80},{20,84},{24,88},{28,92},{32,9... | collective-permute-start | bytes 368648 | tf_op jit(solution)/shard_map/ppermute | solution.py:39
  4.8 15.4 %collective-permute-start.5 = (bf16[224,1280]{1,0:T(8,128)(2,1)S(1)}, bf16[224,1280]{1,0:T(8,128)(2,1)S(1)}, u32[]{:S(2)}, u32[]{:S(2)}) collective-permute-start(bf16[224,1280]{1,0:T(8,128)(2,1)S(1)} %copy-done.1), channel_id=1, source_target_pairs={{0,1},{1,2},{2,3},{3,0},{4,5},{5,6},{6,7},{7,4},{8,9},{9,10},{10,1... | collective-permute-start | bytes 1720328 | tf_op jit(solution)/shard_map/ppermute | solution.py:43
  5.2 15.3 %collective-permute-start.6 = (bf16[224,1280]{1,0:T(8,128)(2,1)S(1)}, bf16[224,1280]{1,0:T(8,128)(2,1)S(1)}, u32[]{:S(2)}, u32[]{:S(2)}) collective-permute-start(bf16[224,1280]{1,0:T(8,128)(2,1)S(1)} %copy-done.1), channel_id=1, source_target_pairs={{0,3},{1,0},{2,1},{3,2},{4,7},{5,4},{6,5},{7,6},{8,11},{9,8},{10,9... | collective-permute-start | bytes 1720328 | tf_op jit(solution)/shard_map/ppermute | solution.py:43
  6.9 11.4 %copy-start.3 = (bf16[240,256]{1,0:T(8,128)(2,1)S(1)}, bf16[240,256]{1,0:T(8,128)(2,1)}, u32[]{:S(2)}) copy-start(bf16[240,256]{1,0:T(8,128)(2,1)} %shard_map.93) | copy-start | bytes 368644
  7.6 10.7 %copy-start.2 = (bf16[224,640]{1,0:T(8,128)(2,1)S(1)}, bf16[224,640]{1,0:T(8,128)(2,1)}, u32[]{:S(2)}) copy-start(bf16[224,640]{1,0:T(8,128)(2,1)} %refs_0_.4) | copy-start | bytes 860164
  10.5 10.1 %copy-start = (bf16[640,5120]{1,0:T(8,128)(2,1)S(1)}, bf16[640,5120]{1,0:T(8,128)(2,1)}, u32[]{:S(2)}) copy-start(bf16[640,5120]{1,0:T(8,128)(2,1)} %refs_0_.7) | copy-start | bytes 19660804
  11.7 12.0 %collective-permute-start.2 = (bf16[2,240,256]{2,1,0:T(8,128)(2,1)S(1)}, bf16[2,240,256]{2,1,0:T(8,128)(2,1)S(1)}, u32[]{:S(2)}, u32[]{:S(2)}) collective-permute-start(bf16[2,240,256]{2,1,0:T(8,128)(2,1)S(1)} %get-tuple-element.135), channel_id=1, source_target_pairs={{0,8},{4,12},{8,16},{12,20},{16,24},{20,28},{24,0},{28,4},{32,40},... | collective-permute-start | bytes 737288 | tf_op jit(solution)/shard_map/ppermute | solution.py:39
  13.7 13.1 %collective-permute-start.3 = (bf16[2,240,256]{2,1,0:T(8,128)(2,1)S(1)}, bf16[2,240,256]{2,1,0:T(8,128)(2,1)S(1)}, u32[]{:S(2)}, u32[]{:S(2)}) collective-permute-start(bf16[2,240,256]{2,1,0:T(8,128)(2,1)S(1)} %get-tuple-element.134), channel_id=1, source_target_pairs={{0,16},{4,20},{8,24},{12,28},{16,0},{20,4},{24,8},{28,12},{32,48},... | collective-permute-start | bytes 737288 | tf_op jit(solution)/shard_map/ppermute | solution.py:39
  17.2 9.5 %collective-permute-start.4 = (bf16[2,240,256]{2,1,0:T(8,128)(2,1)S(1)}, bf16[2,240,256]{2,1,0:T(8,128)(2,1)S(1)}, u32[]{:S(2)}, u32[]{:S(2)}) collective-permute-start(bf16[2,240,256]{2,1,0:T(8,128)(2,1)S(1)} %get-tuple-element.133), channel_id=1, source_target_pairs={{0,24},{4,28},{8,0},{12,4},{16,8},{20,12},{24,16},{28,20},{32,56},... | collective-permute-start | bytes 737288 | tf_op jit(solution)/shard_map/ppermute | solution.py:39
  26.9 5.3 %collective-permute-start.7 = (bf16[9,240,256]{2,1,0:T(8,128)(2,1)S(1)}, bf16[9,240,256]{2,1,0:T(8,128)(2,1)S(1)}, u32[]{:S(2)}, u32[]{:S(2)}) collective-permute-start(bf16[9,240,256]{2,1,0:T(8,128)(2,1)S(1)} %constant_dynamic-update-slice_fusion.refs_2_.refs_8_.refs_5_), channel_id=1, source_target_pairs={{0,4},{4,0},{8,12},{12,8},{16,20},{20,16},{24,28},{28,24},{32,36},... | collective-permute-start | bytes 3317768 | tf_op jit(solution)/shard_map/ppermute | solution.py:39
  27.0 10.9 %collective-permute-start.8 = (bf16[112,1280]{1,0:T(8,128)(2,1)S(1)}, bf16[112,1280]{1,0:T(8,128)(2,1)S(1)}, u32[]{:S(2)}, u32[]{:S(2)}) collective-permute-start(bf16[112,1280]{1,0:T(8,128)(2,1)S(1)} %slice.84), channel_id=1, source_target_pairs={{0,1},{1,2},{2,3},{3,0},{4,5},{5,6},{6,7},{7,4},{8,9},{9,10},{10,1... | collective-permute-start | bytes 860168 | tf_op jit(solution)/shard_map/ppermute | solution.py:43
  27.6 10.4 %collective-permute-start.9 = (bf16[112,1280]{1,0:T(8,128)(2,1)S(1)}, bf16[112,1280]{1,0:T(8,128)(2,1)S(1)}, u32[]{:S(2)}, u32[]{:S(2)}) collective-permute-start(bf16[112,1280]{1,0:T(8,128)(2,1)S(1)} %slice.85), channel_id=1, source_target_pairs={{0,3},{1,0},{2,1},{3,2},{4,7},{5,4},{6,5},{7,6},{8,11},{9,8},{10,9... | collective-permute-start | bytes 860168 | tf_op jit(solution)/shard_map/ppermute | solution.py:43
  38.0 9.7 %collective-permute-start.10 = (bf16[112,1280]{1,0:T(8,128)(2,1)S(1)}, bf16[112,1280]{1,0:T(8,128)(2,1)S(1)}, u32[]{:S(2)}, u32[]{:S(2)}) collective-permute-start(bf16[112,1280]{1,0:T(8,128)(2,1)S(1)} %get-tuple-element.96), channel_id=1, source_target_pairs={{0,1},{1,2},{2,3},{3,0},{4,5},{5,6},{6,7},{7,4},{8,9},{9,10},{10,1... | collective-permute-start | bytes 860168 | tf_op jit(solution)/shard_map/ppermute | solution.py:43
  39.7 9.6 %collective-permute-start.11 = (bf16[112,1280]{1,0:T(8,128)(2,1)S(1)}, bf16[112,1280]{1,0:T(8,128)(2,1)S(1)}, u32[]{:S(2)}, u32[]{:S(2)}) collective-permute-start(bf16[112,1280]{1,0:T(8,128)(2,1)S(1)} %get-tuple-element.97), channel_id=1, source_target_pairs={{0,3},{1,0},{2,1},{3,2},{4,7},{5,4},{6,5},{7,6},{8,11},{9,8},{10,9... | collective-permute-start | bytes 860168 | tf_op jit(solution)/shard_map/ppermute | solution.py:43
  49.4 14.9 %collective-permute-start.18 = (bf16[224,1280]{1,0:T(8,128)(2,1)S(1)}, bf16[224,1280]{1,0:T(8,128)(2,1)S(1)}, u32[]{:S(2)}, u32[]{:S(2)}) collective-permute-start(bf16[224,1280]{1,0:T(8,128)(2,1)S(1)} %pad_maximum_fusion.1), channel_id=1, source_target_pairs={{0,3},{1,0},{2,1},{3,2},{4,7},{5,4},{6,5},{7,6},{8,11},{9,8},{10,9... | collective-permute-start | bytes 1720328 | tf_op jit(solution)/shard_map/ppermute | solution.py:43
  49.5 6.2 %collective-permute-start.12 = (bf16[7,224,256]{2,1,0:T(8,128)(2,1)S(1)}, bf16[7,224,256]{2,1,0:T(8,128)(2,1)S(1)}, u32[]{:S(2)}, u32[]{:S(2)}) collective-permute-start(bf16[7,224,256]{2,1,0:T(8,128)(2,1)S(1)} %get-tuple-element.104), channel_id=1, source_target_pairs={{0,4},{4,0},{8,12},{12,8},{16,20},{20,16},{24,28},{28,24},{32,36},... | collective-permute-start | bytes 2408456 | tf_op jit(solution)/shard_map/ppermute | solution.py:39
  49.7 16.1 %collective-permute-start.17 = (bf16[224,1280]{1,0:T(8,128)(2,1)S(1)}, bf16[224,1280]{1,0:T(8,128)(2,1)S(1)}, u32[]{:S(2)}, u32[]{:S(2)}) collective-permute-start(bf16[224,1280]{1,0:T(8,128)(2,1)S(1)} %pad_maximum_fusion), channel_id=1, source_target_pairs={{0,1},{1,2},{2,3},{3,0},{4,5},{5,6},{6,7},{7,4},{8,9},{9,10},{10,1... | collective-permute-start | bytes 1720328 | tf_op jit(solution)/shard_map/ppermute | solution.py:43
  55.7 3.8 %collective-permute-start.15 = (bf16[2,224,256]{2,1,0:T(8,128)(2,1)S(1)}, bf16[2,224,256]{2,1,0:T(8,128)(2,1)S(1)}, u32[]{:S(2)}, u32[]{:S(2)}) collective-permute-start(bf16[2,224,256]{2,1,0:T(8,128)(2,1)S(1)} %get-tuple-element.113), channel_id=1, source_target_pairs={{0,4},{4,0},{8,12},{12,8},{16,20},{20,16},{24,28},{28,24},{32,36},... | collective-permute-start | bytes 688136 | tf_op jit(solution)/shard_map/ppermute | solution.py:39
  56.2 12.5 %collective-permute-start.13 = (bf16[2,224,256]{2,1,0:T(8,128)(2,1)S(1)}, bf16[2,224,256]{2,1,0:T(8,128)(2,1)S(1)}, u32[]{:S(2)}, u32[]{:S(2)}) collective-permute-start(bf16[2,224,256]{2,1,0:T(8,128)(2,1)S(1)} %get-tuple-element.129), channel_id=1, source_target_pairs={{0,24},{4,28},{8,0},{12,4},{16,8},{20,12},{24,16},{28,20},{32,56},... | collective-permute-start | bytes 688136 | tf_op jit(solution)/shard_map/ppermute | solution.py:39
  58.4 10.3 %collective-permute-start.14 = (bf16[2,224,256]{2,1,0:T(8,128)(2,1)S(1)}, bf16[2,224,256]{2,1,0:T(8,128)(2,1)S(1)}, u32[]{:S(2)}, u32[]{:S(2)}) collective-permute-start(bf16[2,224,256]{2,1,0:T(8,128)(2,1)S(1)} %get-tuple-element.128), channel_id=1, source_target_pairs={{0,16},{4,20},{8,24},{12,28},{16,0},{20,4},{24,8},{28,12},{32,48},... | collective-permute-start | bytes 688136 | tf_op jit(solution)/shard_map/ppermute | solution.py:39
  59.6 12.7 %collective-permute-start.16 = (bf16[2,224,256]{2,1,0:T(8,128)(2,1)S(1)}, bf16[2,224,256]{2,1,0:T(8,128)(2,1)S(1)}, u32[]{:S(2)}, u32[]{:S(2)}) collective-permute-start(bf16[2,224,256]{2,1,0:T(8,128)(2,1)S(1)} %add_convert_fusion.4), channel_id=1, source_target_pairs={{0,8},{4,12},{8,16},{12,20},{16,24},{20,28},{24,0},{28,4},{32,40},... | collective-permute-start | bytes 688136 | tf_op jit(solution)/shard_map/ppermute | solution.py:39
  72.6 6.8 %collective-permute-start.19 = (bf16[224,256]{1,0:T(8,128)(2,1)S(1)}, bf16[224,256]{1,0:T(8,128)(2,1)S(1)}, u32[]{:S(2)}, u32[]{:S(2)}) collective-permute-start(bf16[224,256]{1,0:T(8,128)(2,1)S(1)} %get-tuple-element.126), channel_id=1, source_target_pairs={{0,96},{4,100},{8,104},{12,108},{16,112},{20,116},{24,120},{28,124... | collective-permute-start | bytes 344072 | tf_op jit(solution)/shard_map/ppermute | solution.py:39
  75.8 6.3 %collective-permute-start.20 = (bf16[224,256]{1,0:T(8,128)(2,1)S(1)}, bf16[224,256]{1,0:T(8,128)(2,1)S(1)}, u32[]{:S(2)}, u32[]{:S(2)}) collective-permute-start(bf16[224,256]{1,0:T(8,128)(2,1)S(1)} %get-tuple-element.127), channel_id=1, source_target_pairs={{0,64},{4,68},{8,72},{12,76},{16,80},{20,84},{24,88},{28,92},{32,9... | collective-permute-start | bytes 344072 | tf_op jit(solution)/shard_map/ppermute | solution.py:39
  (1 other events, 4.2 us)
